TPU v7x, 256 devices: a whole 4x4x8 slice. The times are simulated.
256 devices in a mesh: blk: 64 (over x, z_hi, y, core), rep: 4 (over z_lo).
Axes of the slice: x: 4, y: 4, z: 8 (z_hi: 2, z_lo: 4; z = z_hi * 4 + z_lo), core: 2. Of those that a mesh axis runs over, the one named last changes fastest.
Arguments:
- src_points: bfloat16 [131072, 256], P(('blk', 'rep')), may hold values from -0.75 to 0.75
- src_log_mass: float32 [131072], P(('blk', 'rep')), may hold values from -3 to 3
- tgt_points: bfloat16 [65536, 256], P('blk'), may hold values from -0.75 to 0.75
- tgt_log_mass: float32 [65536], P('blk'), may hold values from -3 to 3
- initial_potential: float32 [65536], P('blk'), may hold values from -61 to 61
- pair_list: int32 [64, 7], replicated, may hold values from -1 to 63, as said below
- pair_count: int32 [64], replicated, may hold values from 1 to 7, as said below
Outputs:
- source_potential: float32 [131072], P(('blk', 'rep'))
- target_potential: float32 [65536], P('blk')
Inputs may be any that keep to these rules, and one draw needn't show every extreme that they name: Row s of pair_list lists the target blocks kept by source block s: entry 0 is s itself, the next pair_count[s] - 1 entries are distinct blocks (s + o) mod 64 with 1 <= |o| <= 3, and the remaining entries are -1. `pair_count`: some block has 7 kept target blocks and some other block has 1.
All inputs are finite; a program needn't handle non-finite values.
Results may differ from a plain program's by a relative error of at most 0.0003.
Values may be sent and summed in bfloat16 or wider, within the bound.
No kernel may reach another device: no remote copies, remote signals or barrier semaphores. Data moves between devices by JAX's collectives and lax.ppermute only.
A program may use at most 64 MiB of HBM per device.

v0:
```python
import functools

import jax
import jax.numpy as jnp
from jax import lax
from jax.experimental import pallas as pl
from jax.experimental.pallas import tpu as pltpu
from jax.sharding import PartitionSpec as P

ITERS = 2
EPS_START = 0.5
NEG_FILL = -1e30
ROW_UNROLL = 8
COLUMN_UNROLL = 4
BUFFERS = 8
REPS = 4
SEGMENT = 8
TAIL = 16


def send(value, place, blocks):
    pairs = []
    for block in range(blocks):
        for rep in range(REPS):
            to_block, to_rep = place(block, rep)
            pairs.append((block * REPS + rep, to_block % blocks * REPS + to_rep))
    return lax.ppermute(value, ("blk", "rep"), pairs)


def along(steps, blocks):
    def place(block, rep):
        target = (block + steps) % blocks
        return target, rep if (target // SEGMENT - block // SEGMENT) % 2 == 0 else REPS - 1 - rep

    return place


def by_core(even_steps, odd_steps, blocks):
    even, odd = along(even_steps, blocks), along(odd_steps, blocks)
    return lambda block, rep: even(block, rep) if block % 2 == 0 else odd(block, rep)


def sibling(block, rep):
    return block ^ 1, rep


def diagonal(block, rep):
    return block ^ 1, rep ^ 1


def half_norms(points):
    widened = points.astype(jnp.float32)
    return 0.5 * jnp.sum(widened * widened, axis=1)


def terms(vector):
    first = lax.reduce_precision(vector, 8, 7)
    rest = vector - first
    second = lax.reduce_precision(rest, 8, 7)
    third = lax.reduce_precision(rest - second, 8, 7)
    return [part.astype(jnp.bfloat16) for part in (first, second, third)]


def from_terms(rows, which):
    rows = rows[6 * which : 6 * which + 6]
    vector = rows[0:2] + rows[2:4] + rows[4:6]
    return [vector[q // 2 : q // 2 + 1, q % 2 * 128 : q % 2 * 128 + 128] for q in range(4)]


def log_merge(*parts):
    top = functools.reduce(jnp.maximum, parts)
    return top + jnp.log(sum(jnp.exp(part - top) for part in parts))


def spread_rows(vector_ref, bias_ref):
    for q in range(bias_ref.shape[0] // 128):
        row = vector_ref[q : q + 1, :]
        bias_ref[q * 128 : (q + 1) * 128, :] = jnp.broadcast_to(row, (128, 128)).T


def fold(value, combine):
    rows = value.shape[0]
    while rows > 8:
        rows //= 2
        value = combine(value[:rows], value[rows:])
    return value


def row_update(cross_ref, index, bias, twice, side, half, top_ref, total_ref):
    step = 64

    def chunk(r, _):
        at = pl.ds(pl.multiple_of(side * half + r * step, step), step)
        scores = []
        for q, term in enumerate(bias):
            part = cross_ref[index, at, q * 128 : (q + 1) * 128]
            scores.append((part + part if twice else part) + term)
        old = top_ref[at, :]
        top = jnp.maximum(old, functools.reduce(jnp.maximum, scores))
        total = functools.reduce(jnp.add, [jnp.exp(part - top) for part in scores])
        total_ref[at, :] = total_ref[at, :] * jnp.exp(old - top) + total
        top_ref[at, :] = top
        return 0

    lax.fori_loop(0, half // step, chunk, 0, unroll=ROW_UNROLL)


def row_finish(top_ref, total_ref, out):
    for q in range(out.shape[0]):
        top = top_ref[q * 128 : (q + 1) * 128, :].T
        greatest = jnp.max(top, axis=0, keepdims=True)
        total = total_ref[q * 128 : (q + 1) * 128, :].T * jnp.exp(top - greatest)
        out[q : q + 1, :] = greatest + jnp.log(jnp.sum(total, axis=0, keepdims=True))


def each_kept(flags, first, count, body):
    def unit(u, _):
        number, side = first + lax.div(u, 2), lax.rem(u, 2)

        @pl.when(flags[side * BUFFERS + number] != 0)
        def _():
            body(number, side)

        return 0

    lax.fori_loop(0, 2 * count, unit, 0)


def first_kernel(numbers, first, last, flags, *refs):
    count = len(numbers)
    sources, targets = refs[:2], refs[2 : 2 + count]
    refs = refs[2 + count :]
    if not first:
        refs = refs[4:]
    cross, masses, top_ref, total_ref = refs[:4]
    src_ref, tgt_ref, bias_ref = refs[-3:]
    if first:
        top_ref[...] = jnp.full(top_ref.shape, NEG_FILL, jnp.float32)
        total_ref[...] = jnp.zeros(total_ref.shape, jnp.float32)
    half = sources[0].shape[0]
    width = cross.shape[2]
    for side, src in enumerate(sources):
        src_ref[side] = src[...]
    for k, number in enumerate(numbers):
        tgt_ref[k] = targets[k][:width, :]
        tail = targets[k][width:, :].astype(jnp.float32)
        for q, (row, mass) in enumerate(zip(from_terms(tail, 0), from_terms(tail, 1))):
            bias_ref[k, q : q + 1, :] = row
            masses[number, q : q + 1, :] = mass

    def body(number, side):
        k = number - numbers[0]
        for c in range(0, width, 256):
            for r in range(0, half, 256):
                at = pl.ds(pl.multiple_of(side * half + r, 256), 256)
                cross[number, at, c : c + 256] = lax.dot_general(
                    src_ref[side, r : r + 256, :],
                    tgt_ref[k, c : c + 256, :],
                    (((1,), (1,)), ((), ())),
                    preferred_element_type=jnp.float32,
                )
        bias = [bias_ref[k, q : q + 1, :] for q in range(width // 128)]
        row_update(cross, number, bias, False, side, half, top_ref, total_ref)

    each_kept(flags, numbers[0], count, body)
    if last:
        row_finish(top_ref, total_ref, refs[4])


def row_kernel(flags, cross, masses, sums, out, top_ref, total_ref):
    top_ref[...] = jnp.full(top_ref.shape, NEG_FILL, jnp.float32)
    total_ref[...] = jnp.zeros(total_ref.shape, jnp.float32)
    half = top_ref.shape[0] // 2

    def body(number, side):
        slot = flags[2 * BUFFERS + number]
        bias = [
            masses[number, q : q + 1, :] - 2.0 * sums[slot, q : q + 1, :] for q in range(masses.shape[1])
        ]
        row_update(cross, number, bias, True, side, half, top_ref, total_ref)

    each_kept(flags, 0, BUFFERS, body)
    row_finish(top_ref, total_ref, out)


def column_kernel(twice, flags, cross, weights, out, bias, top_ref, total_ref):
    out[...] = jnp.full(out.shape, NEG_FILL, jnp.float32)
    top_ref[...] = jnp.full(top_ref.shape, NEG_FILL, jnp.float32)
    total_ref[...] = jnp.zeros(total_ref.shape, jnp.float32)
    spread_rows(weights, bias)
    half = bias.shape[0] // 2
    pieces = cross.shape[2] // 128
    step = 128

    def body(number, side):
        def chunk(r, state):
            at = pl.ds(pl.multiple_of(side * half + r * step, step), step)
            weight = bias[at, :]
            tops, totals = [], []
            for q in range(pieces):
                part = cross[number, at, q * 128 : (q + 1) * 128]
                scores = (part + part if twice else part) + weight
                top = jnp.maximum(state[0][q], fold(scores, jnp.maximum))
                total = jnp.sum(jnp.exp(scores.reshape(-1, 8, 128) - top[None]), axis=0)
                totals.append(state[1][q] * jnp.exp(state[0][q] - top) + total)
                tops.append(top)
            return tuple(tops), tuple(totals)

        state = (
            tuple(top_ref[number, :, q * 128 : (q + 1) * 128] for q in range(pieces)),
            tuple(total_ref[number, :, q * 128 : (q + 1) * 128] for q in range(pieces)),
        )
        tops, totals = lax.fori_loop(0, half // step, chunk, state, unroll=COLUMN_UNROLL)
        for q in range(pieces):
            top_ref[number, :, q * 128 : (q + 1) * 128] = tops[q]
            total_ref[number, :, q * 128 : (q + 1) * 128] = totals[q]

    each_kept(flags, 0, BUFFERS, body)

    def finish(number, _):
        @pl.when((flags[number] | flags[BUFFERS + number]) != 0)
        def _():
            for q in range(pieces):
                top = top_ref[number, :, q * 128 : (q + 1) * 128]
                greatest = jnp.max(top, axis=0, keepdims=True)
                total = total_ref[number, :, q * 128 : (q + 1) * 128] * jnp.exp(top - greatest)
                out[flags[2 * BUFFERS + number], q : q + 1, :] = greatest + jnp.log(
                    jnp.sum(total, axis=0, keepdims=True)
                )

        return 0

    lax.fori_loop(0, BUFFERS, finish, 0)


WHOLE = pl.BlockSpec(memory_space=pltpu.VMEM)
SCALARS = pl.BlockSpec(memory_space=pltpu.SMEM)
PARAMS = pltpu.CompilerParams(vmem_limit_bytes=20 * 2**20)


def in_vmem(value):
    return pltpu.with_memory_space_constraint(value, pltpu.VMEM)


def call_first(numbers, first, last, flags, sources, targets, state):
    half, depth = sources[0].shape
    rows, columns, count = 2 * half, targets[0].shape[0] - TAIL, len(numbers)
    out_shape = [
        pltpu.VMEM((BUFFERS, rows, columns), jnp.float32),
        pltpu.VMEM((BUFFERS, columns // 128, 128), jnp.float32),
        pltpu.VMEM((rows, 128), jnp.float32),
        pltpu.VMEM((rows, 128), jnp.float32),
    ]
    if last:
        out_shape.append(jax.ShapeDtypeStruct((rows // 128, 128), jnp.float32))
    operands = [flags, *sources, *targets]
    aliases = {}
    if not first:
        aliases = {len(operands) + i: i for i in range(4)}
        operands += [in_vmem(value) for value in state]
    return pl.pallas_call(
        functools.partial(first_kernel, numbers, first, last),
        out_shape=out_shape,
        in_specs=[SCALARS] + [WHOLE] * (len(operands) - 1),
        out_specs=[WHOLE] * len(out_shape),
        scratch_shapes=[
            pltpu.VMEM((2, half, depth), jnp.bfloat16),
            pltpu.VMEM((count, columns, depth), jnp.bfloat16),
            pltpu.VMEM((count, columns // 128, 128), jnp.float32),
        ],
        input_output_aliases=aliases,
        compiler_params=PARAMS,
        cost_estimate=pl.CostEstimate(
            flops=2 * count * rows * columns * depth,
            bytes_accessed=count * rows * columns,
            transcendentals=count * rows * columns,
        ),
        name="first_rows",
    )(*operands)


def call_rows(flags, cross, masses, sums):
    rows = cross.shape[1]
    return pl.pallas_call(
        row_kernel,
        out_shape=jax.ShapeDtypeStruct((rows // 128, 128), jnp.float32),
        in_specs=[SCALARS] + [WHOLE] * 3,
        out_specs=WHOLE,
        scratch_shapes=[pltpu.VMEM((rows, 128), jnp.float32)] * 2,
        compiler_params=PARAMS,
        name="rows",
    )(flags, in_vmem(cross), in_vmem(masses), sums)


def call_columns(twice, flags, cross, weights):
    rows, columns = cross.shape[1:]
    return pl.pallas_call(
        functools.partial(column_kernel, twice),
        out_shape=jax.ShapeDtypeStruct((BUFFERS, columns // 128, 128), jnp.float32),
        in_specs=[SCALARS] + [WHOLE] * 2,
        out_specs=WHOLE,
        scratch_shapes=[pltpu.VMEM((rows, 128), jnp.float32)]
        + [pltpu.VMEM((BUFFERS, 8, columns), jnp.float32)] * 2,
        compiler_params=PARAMS,
        name="columns",
    )(flags, in_vmem(cross), weights)


def fill_rows(value, before, after):
    return jnp.pad(value, ((before, after), (0, 0), (0, 0)), constant_values=NEG_FILL)


def local(src_points, src_log_mass, tgt_points, tgt_log_mass, initial_potential, pair_list, pair_count):
    block = lax.axis_index("blk")
    rep = lax.axis_index("rep")
    blocks = lax.axis_size("blk")
    core = block % 2
    half_index = (rep % 2) ^ ((block // SEGMENT) % 2)
    rows = src_points.shape[0]
    width = tgt_points.shape[0]
    columns = width // 2

    def my_half(value):
        return lax.dynamic_slice_in_dim(value, half_index * columns, columns, 0)

    first_scale = 1.0 / EPS_START
    points = my_half(tgt_points)
    masses = my_half(tgt_log_mass)
    bias = masses + (my_half(initial_potential) - half_norms(points)) * first_scale
    tail = [part.reshape(-1, points.shape[1]) for part in terms(bias) + terms(masses)]
    tail.append(jnp.zeros((TAIL - 6 * columns // points.shape[1], points.shape[1]), jnp.bfloat16))
    message = jnp.concatenate([points * jnp.bfloat16(first_scale)] + tail, axis=0)

    before = send(message, along(2, blocks), blocks)
    after = send(message, along(-2, blocks), blocks)
    third = send(message, by_core(-3, 3, blocks), blocks)
    beside = send(message, sibling, blocks)
    mate = send(src_points, diagonal, blocks)
    sources = [src_points, mate]
    groups = ((0, 1), (2, 3, 4), (5, 6, 7))

    even_slots = (3, 4, 1, 5, 0, 2, 6, 7)
    odd_slots = (4, 3, 2, 6, 7, 1, 5, 0)
    slots = jnp.where(core == 0, jnp.array(even_slots, jnp.int32), jnp.array(odd_slots, jnp.int32))
    names = (block - core - 3 + slots) % blocks

    def kept(source_block):
        row_names = pair_list[source_block]
        in_use = jnp.arange(row_names.shape[0], dtype=jnp.int32) < pair_count[source_block]
        return jnp.any((row_names[None, :] == names[:, None]) & in_use[None, :], axis=1).astype(jnp.int32)

    flags = jnp.concatenate([kept(block), kept(block + 1 - 2 * core), slots])

    state = call_first(groups[0], True, False, flags, sources, [message, beside], ())
    state, arrived = lax.optimization_barrier((state, (before, after, third)))
    passed_on = [send(value, sibling, blocks) for value in arrived]
    state = call_first(groups[1], False, False, flags, sources, arrived, state)
    *state, last = call_first(groups[2], False, True, flags, sources, passed_on, state)
    cross, window_masses = state[:2]
    part = last.reshape(-1)

    for sweep in range(ITERS):
        epsilon = EPS_START * 0.5**sweep
        if sweep == 0:
            got = send(jnp.concatenate([part, src_log_mass]), diagonal, blocks)
            both_masses = jnp.concatenate([src_log_mass, got[2 * rows :]])
        else:
            part = call_rows(flags, cross, window_masses, column_sums).reshape(-1)
            got = send(part, diagonal, blocks)
        row_sums = log_merge(part, jnp.concatenate([got[rows : 2 * rows], got[:rows]]))
        weighted = (both_masses - row_sums).reshape(2 * rows // 128, 128)
        part = call_columns(sweep > 0, flags, cross, weighted)
        chip = log_merge(
            part,
            send(part, sibling, blocks),
            send(part, lambda b, r: (b, r ^ 2), blocks),
            send(part, lambda b, r: (b ^ 1, r ^ 2), blocks),
        )
        forward = core == 0
        if sweep + 1 < ITERS:
            got = []
            for n in (1, 2, 3):
                kept_rows = 8 - 2 * n
                out = jnp.where(forward, chip[2 * n :], chip[:kept_rows])
                out = send(out, by_core(2 * n, -2 * n, blocks), blocks)
                got.append(
                    jnp.where(forward, fill_rows(out, 0, 2 * n), fill_rows(out, 2 * n, 0))
                )
            side = log_merge(*got)
            column_sums = log_merge(chip, side, send(side, sibling, blocks))
        else:
            near = jnp.where(forward, chip[5:7], chip[1:3])
            near = send(near, by_core(2, -2, blocks), blocks)
            far = jnp.where(forward, chip[7], chip[0])
            far = send(far, by_core(4, -4, blocks), blocks)
            empty = jnp.full_like(far, NEG_FILL)
            far = jnp.where(forward, jnp.stack([far, empty]), jnp.stack([empty, far]))
            side = log_merge(near, far)
            column_sums = log_merge(chip[3:5], side, send(side, sibling, blocks))
            mine = jnp.where(core == 0, column_sums[0], column_sums[1]).reshape(columns)
            other = send(mine, lambda b, r: (b, r ^ 1), blocks)
            whole = jnp.where(
                half_index == 0, jnp.concatenate([mine, other]), jnp.concatenate([other, mine])
            )
            source_pot = half_norms(src_points) - epsilon * row_sums[:rows]
            target_pot = half_norms(tgt_points) - epsilon * whole
    return source_pot, target_pot


def solution(mesh):
    in_specs = (
        P(("blk", "rep"), None),
        P(("blk", "rep")),
        P("blk", None),
        P("blk"),
        P("blk"),
        P(),
        P(),
    )
    out_specs = (P(("blk", "rep")), P("blk"))
    return jax.shard_map(local, mesh=mesh, in_specs=in_specs, out_specs=out_specs, check_vma=False)
```

profile of v0, /device:TPU:1, one launch (start us, length us, event | category | flops | bytes accessed | tf_op | source)
XLA Modules:
  0.0 99.3 jit_solution(5757814822389705227)
XLA Ops:
  0.7 1.1 %multiply_reduce_fusion.1 = f32[512]{0:T(512)S(1)} fusion(bf16[1024,256]{1,0:T(8,128)(2,1)} %param.11, s32[]{:T(128)S(6)} %select_n.130), kind=kLoop, calls=%fused_computation.1 | loop fusion | flops 392704 | bytes 264196 | tf_op jit(solution)/shard_map/reduce_sum | solution.py:53
  1.8 1.0 %dynamic-slice_multiply_fusion = bf16[512,256]{1,0:T(8,128)(2,1)S(1)} fusion(bf16[1024,256]{1,0:T(8,128)(2,1)} %param.11, s32[]{:T(128)S(6)} %select_n.130), kind=kLoop, calls=%fused_computation.3 | loop fusion | flops 524288 | bytes 524292 | tf_op jit(solution)/shard_map/mul | solution.py:332
  2.8 0.8 fusion.9
  3.7 0.1 concatenate.33.refs_2_
  3.8 3.3 %collective-permute-start.1 = (bf16[528,256]{1,0:T(8,128)(2,1)S(1)}, bf16[528,256]{1,0:T(8,128)(2,1)S(1)}, u32[]{:S(2)}, u32[]{:S(2)}) collective-permute-start(bf16[528,256]{1,0:T(8,128)(2,1)S(1)} %concatenate.33.refs_2_), channel_id=1, source_target_pairs={{0,4},{1,5},{2,6},{3,7},{4,0},{5,1},{6,2},{7,3},{8,12},{9,13},{10,... | collective-permute-start | bytes 811016 | tf_op jit(solution)/shard_map/ppermute | solution.py:27
  7.1 8.5 %collective-permute-start.3 = (bf16[528,256]{1,0:T(8,128)(2,1)S(1)}, bf16[528,256]{1,0:T(8,128)(2,1)S(1)}, u32[]{:S(2)}, u32[]{:S(2)}) collective-permute-start(bf16[528,256]{1,0:T(8,128)(2,1)S(1)} %concatenate.33.refs_2_), channel_id=1, source_target_pairs={{0,251},{1,250},{2,249},{3,248},{4,255},{5,254},{6,253},{7,252},{8... | collective-permute-start | bytes 811016 | tf_op jit(solution)/shard_map/ppermute | solution.py:27
  15.6 0.0 collective-permute-start.4
  15.6 3.6 %collective-permute-start = (bf16[512,256]{1,0:T(8,128)(2,1)}, bf16[512,256]{1,0:T(8,128)(2,1)S(1)}, u32[]{:S(2)}, u32[]{:S(2)}) collective-permute-start(bf16[512,256]{1,0:T(8,128)(2,1)} %refs_0_.5), channel_id=1, source_target_pairs={{0,5},{1,4},{2,7},{3,6},{4,1},{5,0},{6,3},{7,2},{8,13},{9,12},{10,... | collective-permute-start | bytes 786440 | tf_op jit(solution)/shard_map/ppermute | solution.py:27
  19.2 1.3 %fusion.13 = (s32[1]{0:T(128)}, s32[1]{0:T(128)}) fusion(s32[64]{0:T(128)} %param.15, s32[]{:T(128)S(6)} %select_n.126, s32[]{:T(128)S(6)} %select_n.121), kind=kLoop, calls=%fused_computation.68 | loop fusion | bytes 24 | tf_op jit(solution)/shard_map/dynamic_slice | solution.py:349
  20.5 0.7 and_select_fusion
  21.2 1.3 %iota_compare_fusion = (pred[7]{0:T(512)(128)(4,1)S(1)}, pred[7]{0:T(512)(128)(4,1)S(1)}) fusion(s32[]{:T(128)} %bitcast.1, s32[]{:T(128)} %bitcast), kind=kLoop, calls=%fused_computation.64 | loop fusion | flops 14 | bytes 22 | tf_op jit(solution)/shard_map/lt | solution.py:349
  22.5 1.0 dynamic-slice_reduce_fusion.1
  23.5 0.2 and_reduce_fusion.1
  23.7 0.1 pad_add_fusion.flags
  23.7 9.0 %collective-permute-done.refs_1_ = bf16[512,256]{1,0:T(8,128)(2,1)S(1)} collective-permute-done((bf16[512,256]{1,0:T(8,128)(2,1)}, bf16[512,256]{1,0:T(8,128)(2,1)S(1)}, u32[]{:S(2)}, u32[]{:S(2)}) %collective-permute-start) | collective-permute-done | bytes 262176 | tf_op jit(solution)/shard_map/ppermute | solution.py:27
  32.8 0.0 collective-permute-done.1.refs_3_
  32.8 0.9 copy-done
  33.7 1.9 %first_rows.3 = (f32[8,1024,512]{2,1,0:T(8,128)S(1)}, f32[8,4,128]{2,1,0:T(4,128)S(1)}, f32[1024,128]{1,0:T(8,128)S(1)}, f32[1024,128]{1,0:T(8,128)S(1)}) custom-call(s32[24]{0:T(128)S(1)} %pad_add_fusion.flags, bf16[512,256]{1,0:T(8,128)(2,1)S(1)} %copy-done, bf16[512,256]{1,0:T(8,128)(2,1)S(1)} %collective-permute-done.refs_1_, ...), custom_call_target="tpu_custom_call" | custom-call | flops 536870912 | bytes 1048576 | tf_op jit(solution)/shard_map/first_rows/pallas_call | solution.py:261
  35.7 0.0 collective-permute-done.2.refs_2_
  35.7 0.0 copy-start.2
  35.7 0.4 collective-permute-start.5
  36.1 0.2 collective-permute-start.6
  36.3 0.3 collective-permute-start.7
  36.6 0.7 first_rows.4
  37.3 0.0 collective-permute-done.5.refs_2_
  37.3 0.4 collective-permute-done.6.refs_3_
  37.7 0.4 collective-permute-done.7.refs_4_
  38.1 1.1 %first_rows.5 = (f32[8,1024,512]{2,1,0:T(8,128)S(1)}, f32[8,4,128]{2,1,0:T(4,128)S(1)}, f32[1024,128]{1,0:T(8,128)S(1)}, f32[1024,128]{1,0:T(8,128)S(1)}, f32[8,128]{1,0:T(8,128)S(1)}) custom-call(s32[24]{0:T(128)S(1)} %pad_add_fusion.flags, bf16[512,256]{1,0:T(8,128)(2,1)S(1)} %copy-done, ...), custom_call_target="tpu_custom_call", output_to_operand_aliasing={{0}: (6, {}), {1}: (7, {}), {2}: (8, {}), {3}: (9, {})} | custom-call | flops 805306368 | bytes 1572864 | tf_op jit(solution)/shard_map/first_rows/pallas_call | solution.py:261
  39.2 2.4 %collective-permute-start.8 = (f32[1536]{0:T(1024)S(1)}, f32[1536]{0:T(1024)S(1)}, u32[]{:S(2)}, u32[]{:S(2)}) collective-permute-start(f32[1536]{0:T(1024)S(1)} %pad_maximum_fusion), channel_id=1, source_target_pairs={{0,5},{1,4},{2,7},{3,6},{4,1},{5,0},{6,3},{7,2},{8,13},{9,12},{10,... | collective-permute-start | bytes 18440 | tf_op jit(solution)/shard_map/ppermute | solution.py:27
  41.7 1.3 %collective-permute-done.8 = f32[1536]{0:T(1024)S(1)} collective-permute-done((f32[1536]{0:T(1024)S(1)}, f32[1536]{0:T(1024)S(1)}, u32[]{:S(2)}, u32[]{:S(2)}) %collective-permute-start.8) | collective-permute-done | bytes 6176 | tf_op jit(solution)/shard_map/ppermute | solution.py:27
  43.0 1.7 %columns.2 = f32[8,4,128]{2,1,0:T(4,128)S(1)} custom-call(s32[24]{0:T(128)S(1)} %pad_add_fusion.flags, f32[8,1024,512]{2,1,0:T(8,128)S(1)} %get-tuple-element.35.cross, f32[8,128]{1,0:T(8,128)S(1)} %add_subtract_fusion.1.weights), custom_call_target="tpu_custom_call" | custom-call | tf_op jit(solution)/shard_map/columns/pallas_call | solution.py:297
  44.7 2.3 %collective-permute-start.11 = (f32[8,4,128]{2,1,0:T(4,128)S(1)}, f32[8,4,128]{2,1,0:T(4,128)S(1)}, u32[]{:S(2)}, u32[]{:S(2)}) collective-permute-start(f32[8,4,128]{2,1,0:T(4,128)S(1)} %columns.2), channel_id=1, source_target_pairs={{0,6},{1,7},{2,4},{3,5},{4,2},{5,3},{6,0},{7,1},{8,14},{9,15},{10,... | collective-permute-start | bytes 49160 | tf_op jit(solution)/shard_map/ppermute | solution.py:27
  47.0 0.2 collective-permute-start.10
  47.2 0.6 collective-permute-start.9
  47.9 1.0 %collective-permute-done.11 = f32[8,4,128]{2,1,0:T(4,128)S(1)} collective-permute-done((f32[8,4,128]{2,1,0:T(4,128)S(1)}, f32[8,4,128]{2,1,0:T(4,128)S(1)}, u32[]{:S(2)}, u32[]{:S(2)}) %collective-permute-start.11) | collective-permute-done | bytes 16416 | tf_op jit(solution)/shard_map/ppermute | solution.py:27
  48.9 1.6 %collective-permute-done.10 = f32[8,4,128]{2,1,0:T(4,128)S(1)} collective-permute-done((f32[8,4,128]{2,1,0:T(4,128)S(1)}, f32[8,4,128]{2,1,0:T(4,128)S(1)}, u32[]{:S(2)}, u32[]{:S(2)}) %collective-permute-start.10) | collective-permute-done | bytes 16416 | tf_op jit(solution)/shard_map/ppermute | solution.py:27
  50.6 3.1 %collective-permute-start.12 = (f32[6,4,128]{2,1,0:T(4,128)S(1)}, f32[6,4,128]{2,1,0:T(4,128)S(1)}, u32[]{:S(2)}, u32[]{:S(2)}) collective-permute-start(f32[6,4,128]{2,1,0:T(4,128)S(1)} %slice_select_fusion), channel_id=1, source_target_pairs={{0,8},{1,9},{2,10},{3,11},{4,255},{5,254},{6,253},{7,252},{8,16},{... | collective-permute-start | bytes 36872 | tf_op jit(solution)/shard_map/ppermute | solution.py:27
  53.7 1.1 %collective-permute-start.13 = (f32[4,4,128]{2,1,0:T(4,128)S(1)}, f32[4,4,128]{2,1,0:T(4,128)S(1)}, u32[]{:S(2)}, u32[]{:S(2)}) collective-permute-start(f32[4,4,128]{2,1,0:T(4,128)S(1)} %slice_select_fusion.1), channel_id=1, source_target_pairs={{0,16},{1,17},{2,18},{3,19},{4,247},{5,246},{6,245},{7,244},{8,24}... | collective-permute-start | bytes 24584 | tf_op jit(solution)/shard_map/ppermute | solution.py:27
  54.8 3.4 %collective-permute-start.14 = (f32[2,4,128]{2,1,0:T(4,128)S(1)}, f32[2,4,128]{2,1,0:T(4,128)S(1)}, u32[]{:S(2)}, u32[]{:S(2)}) collective-permute-start(f32[2,4,128]{2,1,0:T(4,128)S(1)} %slice_select_fusion.3), channel_id=1, source_target_pairs={{0,24},{1,25},{2,26},{3,27},{4,239},{5,238},{6,237},{7,236},{8,35}... | collective-permute-start | bytes 12296 | tf_op jit(solution)/shard_map/ppermute | solution.py:27
  58.2 0.8 collective-permute-done.14
  59.0 3.0 %collective-permute-start.15 = (f32[8,4,128]{2,1,0:T(4,128)S(1)}, f32[8,4,128]{2,1,0:T(4,128)S(1)}, u32[]{:S(2)}, u32[]{:S(2)}) collective-permute-start(f32[8,4,128]{2,1,0:T(4,128)S(1)} %log_add_fusion.2), channel_id=1, source_target_pairs={{0,4},{1,5},{2,6},{3,7},{4,0},{5,1},{6,2},{7,3},{8,12},{9,13},{10,... | collective-permute-start | bytes 49160 | tf_op jit(solution)/shard_map/ppermute | solution.py:27
  62.0 0.8 collective-permute-done.15
  62.9 0.0 copy-start.1
  62.9 1.8 %rows.1 = f32[8,128]{1,0:T(8,128)S(1)} custom-call(s32[24]{0:T(128)S(1)} %pad_add_fusion.flags, f32[8,1024,512]{2,1,0:T(8,128)S(1)} %get-tuple-element.35.cross, f32[8,4,128]{2,1,0:T(4,128)S(1)} %get-tuple-element.36.masses, f32[8,4,128]{2,1,0:T(4,128)S(1)} %bitcast.37), custom_call_target="tpu_custom_call" | custom-call | tf_op jit(solution)/shard_map/rows/pallas_call | solution.py:284
  64.7 3.9 %collective-permute-start.16 = (f32[1024]{0:T(1024)S(1)}, f32[1024]{0:T(1024)S(1)}, u32[]{:S(2)}, u32[]{:S(2)}) collective-permute-start(f32[1024]{0:T(1024)S(1)} %bitcast.38), channel_id=1, source_target_pairs={{0,5},{1,4},{2,7},{3,6},{4,1},{5,0},{6,3},{7,2},{8,13},{9,12},{10,... | collective-permute-start | bytes 12296 | tf_op jit(solution)/shard_map/ppermute | solution.py:27
  68.5 1.3 %collective-permute-done.16 = f32[1024]{0:T(1024)S(1)} collective-permute-done((f32[1024]{0:T(1024)S(1)}, f32[1024]{0:T(1024)S(1)}, u32[]{:S(2)}, u32[]{:S(2)}) %collective-permute-start.16) | collective-permute-done | bytes 4128 | tf_op jit(solution)/shard_map/ppermute | solution.py:27
  69.9 1.7 %columns.3 = f32[8,4,128]{2,1,0:T(4,128)S(1)} custom-call(s32[24]{0:T(128)S(1)} %pad_add_fusion.flags, f32[8,1024,512]{2,1,0:T(8,128)S(1)} %get-tuple-element.35.cross, f32[8,128]{1,0:T(8,128)S(1)} %add_subtract_fusion.weights), custom_call_target="tpu_custom_call" | custom-call | tf_op jit(solution)/shard_map/columns/pallas_call | solution.py:297
  71.6 2.3 %collective-permute-start.19 = (f32[8,4,128]{2,1,0:T(4,128)S(1)}, f32[8,4,128]{2,1,0:T(4,128)S(1)}, u32[]{:S(2)}, u32[]{:S(2)}) collective-permute-start(f32[8,4,128]{2,1,0:T(4,128)S(1)} %columns.3), channel_id=1, source_target_pairs={{0,6},{1,7},{2,4},{3,5},{4,2},{5,3},{6,0},{7,1},{8,14},{9,15},{10,... | collective-permute-start | bytes 49160 | tf_op jit(solution)/shard_map/ppermute | solution.py:27
  73.9 0.2 collective-permute-start.18
  74.1 0.6 collective-permute-start.17
  74.7 0.2 multiply_reduce_fusion
  74.9 0.8 collective-permute-done.19
  75.7 1.6 %collective-permute-done.18 = f32[8,4,128]{2,1,0:T(4,128)S(1)} collective-permute-done((f32[8,4,128]{2,1,0:T(4,128)S(1)}, f32[8,4,128]{2,1,0:T(4,128)S(1)}, u32[]{:S(2)}, u32[]{:S(2)}) %collective-permute-start.18) | collective-permute-done | bytes 16416 | tf_op jit(solution)/shard_map/ppermute | solution.py:27
  77.4 5.4 %collective-permute-start.21 = (f32[4,128]{1,0:T(4,128)S(1)}, f32[4,128]{1,0:T(4,128)S(1)}, u32[]{:S(2)}, u32[]{:S(2)}) collective-permute-start(f32[4,128]{1,0:T(4,128)S(1)} %fusion.11), channel_id=1, source_target_pairs={{0,16},{1,17},{2,18},{3,19},{4,247},{5,246},{6,245},{7,244},{8,24}... | collective-permute-start | bytes 6152 | tf_op jit(solution)/shard_map/ppermute | solution.py:27
  82.8 0.8 collective-permute-start.20
  83.6 0.1 multiply_reduce_fusion.2
  83.8 0.4 collective-permute-done.21
  84.2 2.0 %collective-permute-done.20 = f32[2,4,128]{2,1,0:T(4,128)S(1)} collective-permute-done((f32[2,4,128]{2,1,0:T(4,128)S(1)}, f32[2,4,128]{2,1,0:T(4,128)S(1)}, u32[]{:S(2)}, u32[]{:S(2)}) %collective-permute-start.20) | collective-permute-done | bytes 4128 | tf_op jit(solution)/shard_map/ppermute | solution.py:27
  86.2 8.8 %collective-permute-start.22 = (f32[2,4,128]{2,1,0:T(4,128)S(1)}, f32[2,4,128]{2,1,0:T(4,128)S(1)}, u32[]{:S(2)}, u32[]{:S(2)}) collective-permute-start(f32[2,4,128]{2,1,0:T(4,128)S(1)} %log_add_fusion.5), channel_id=1, source_target_pairs={{0,4},{1,5},{2,6},{3,7},{4,0},{5,1},{6,2},{7,3},{8,12},{9,13},{10,... | collective-permute-start | bytes 12296 | tf_op jit(solution)/shard_map/ppermute | solution.py:27
  95.0 0.8 collective-permute-done.22
  95.9 1.8 %collective-permute-start.23 = (f32[512]{0:T(512)S(1)}, f32[512]{0:T(512)S(1)}, u32[]{:S(2)}, u32[]{:S(2)}) collective-permute-start(f32[512]{0:T(512)S(1)} %fusion.10), channel_id=1, source_target_pairs={{0,1},{1,0},{2,3},{3,2},{4,5},{5,4},{6,7},{7,6},{8,9},{9,8},{10,11... | collective-permute-start | bytes 6152 | tf_op jit(solution)/shard_map/ppermute | solution.py:27
  97.7 0.6 multiply_subtract_fusion
  98.3 0.4 collective-permute-done.23
  98.7 0.6 fusion.1
  (38 shorter events, 0.4 us)
Async XLA Ops:
  3.8 29.0 %collective-permute-start.1 = (bf16[528,256]{1,0:T(8,128)(2,1)S(1)}, bf16[528,256]{1,0:T(8,128)(2,1)S(1)}, u32[]{:S(2)}, u32[]{:S(2)}) collective-permute-start(bf16[528,256]{1,0:T(8,128)(2,1)S(1)} %concatenate.33.refs_2_), channel_id=1, source_target_pairs={{0,4},{1,5},{2,6},{3,7},{4,0},{5,1},{6,2},{7,3},{8,12},{9,13},{10,... | collective-permute-start | bytes 811016 | tf_op jit(solution)/shard_map/ppermute | solution.py:27
  7.1 28.5 %collective-permute-start.2 = (bf16[528,256]{1,0:T(8,128)(2,1)S(1)}, bf16[528,256]{1,0:T(8,128)(2,1)S(1)}, u32[]{:S(2)}, u32[]{:S(2)}) collective-permute-start(bf16[528,256]{1,0:T(8,128)(2,1)S(1)} %concatenate.33.refs_2_), channel_id=1, source_target_pairs={{0,8},{1,9},{2,10},{3,11},{4,12},{5,13},{6,14},{7,15},{8,16},{9,17... | collective-permute-start | bytes 811016 | tf_op jit(solution)/shard_map/ppermute | solution.py:27
  7.1 28.5 %collective-permute-start.3 = (bf16[528,256]{1,0:T(8,128)(2,1)S(1)}, bf16[528,256]{1,0:T(8,128)(2,1)S(1)}, u32[]{:S(2)}, u32[]{:S(2)}) collective-permute-start(bf16[528,256]{1,0:T(8,128)(2,1)S(1)} %concatenate.33.refs_2_), channel_id=1, source_target_pairs={{0,251},{1,250},{2,249},{3,248},{4,255},{5,254},{6,253},{7,252},{8... | collective-permute-start | bytes 811016 | tf_op jit(solution)/shard_map/ppermute | solution.py:27
  15.6 20.1 %collective-permute-start.4 = (bf16[528,256]{1,0:T(8,128)(2,1)S(1)}, bf16[528,256]{1,0:T(8,128)(2,1)S(1)}, u32[]{:S(2)}, u32[]{:S(2)}) collective-permute-start(bf16[528,256]{1,0:T(8,128)(2,1)S(1)} %concatenate.33.refs_2_), channel_id=1, source_target_pairs={{0,247},{1,246},{2,245},{3,244},{4,16},{5,17},{6,18},{7,19},{8,255... | collective-permute-start | bytes 811016 | tf_op jit(solution)/shard_map/ppermute | solution.py:27
  15.6 17.1 %collective-permute-start = (bf16[512,256]{1,0:T(8,128)(2,1)}, bf16[512,256]{1,0:T(8,128)(2,1)S(1)}, u32[]{:S(2)}, u32[]{:S(2)}) collective-permute-start(bf16[512,256]{1,0:T(8,128)(2,1)} %refs_0_.5), channel_id=1, source_target_pairs={{0,5},{1,4},{2,7},{3,6},{4,1},{5,0},{6,3},{7,2},{8,13},{9,12},{10,... | collective-permute-start | bytes 786440 | tf_op jit(solution)/shard_map/ppermute | solution.py:27
  32.8 1.0 copy-start
  35.7 3.5 %copy-start.2 = (f32[512]{0:T(512)S(1)}, f32[512]{0:T(512)}, u32[]{:S(2)}) copy-start(f32[512]{0:T(512)} %param.10) | copy-start | bytes 6148
  35.7 1.6 %collective-permute-start.5 = (bf16[528,256]{1,0:T(8,128)(2,1)S(1)}, bf16[528,256]{1,0:T(8,128)(2,1)S(1)}, u32[]{:S(2)}, u32[]{:S(2)}) collective-permute-start(bf16[528,256]{1,0:T(8,128)(2,1)S(1)} %collective-permute-done.2.refs_2_), channel_id=1, source_target_pairs={{0,4},{1,5},{2,6},{3,7},{4,0},{5,1},{6,2},{7,3},{8,12},{9,13},{10,... | collective-permute-start | bytes 811016 | tf_op jit(solution)/shard_map/ppermute | solution.py:27
  36.1 1.7 %collective-permute-start.6 = (bf16[528,256]{1,0:T(8,128)(2,1)S(1)}, bf16[528,256]{1,0:T(8,128)(2,1)S(1)}, u32[]{:S(2)}, u32[]{:S(2)}) collective-permute-start(bf16[528,256]{1,0:T(8,128)(2,1)S(1)} %collective-permute-done.3.refs_3_), channel_id=1, source_target_pairs={{0,4},{1,5},{2,6},{3,7},{4,0},{5,1},{6,2},{7,3},{8,12},{9,13},{10,... | collective-permute-start | bytes 811016 | tf_op jit(solution)/shard_map/ppermute | solution.py:27
  36.3 1.8 %collective-permute-start.7 = (bf16[528,256]{1,0:T(8,128)(2,1)S(1)}, bf16[528,256]{1,0:T(8,128)(2,1)S(1)}, u32[]{:S(2)}, u32[]{:S(2)}) collective-permute-start(bf16[528,256]{1,0:T(8,128)(2,1)S(1)} %collective-permute-done.4.refs_4_), channel_id=1, source_target_pairs={{0,4},{1,5},{2,6},{3,7},{4,0},{5,1},{6,2},{7,3},{8,12},{9,13},{10,... | collective-permute-start | bytes 811016 | tf_op jit(solution)/shard_map/ppermute | solution.py:27
  39.2 3.8 %collective-permute-start.8 = (f32[1536]{0:T(1024)S(1)}, f32[1536]{0:T(1024)S(1)}, u32[]{:S(2)}, u32[]{:S(2)}) collective-permute-start(f32[1536]{0:T(1024)S(1)} %pad_maximum_fusion), channel_id=1, source_target_pairs={{0,5},{1,4},{2,7},{3,6},{4,1},{5,0},{6,3},{7,2},{8,13},{9,12},{10,... | collective-permute-start | bytes 18440 | tf_op jit(solution)/shard_map/ppermute | solution.py:27
  44.7 4.2 %collective-permute-start.11 = (f32[8,4,128]{2,1,0:T(4,128)S(1)}, f32[8,4,128]{2,1,0:T(4,128)S(1)}, u32[]{:S(2)}, u32[]{:S(2)}) collective-permute-start(f32[8,4,128]{2,1,0:T(4,128)S(1)} %columns.2), channel_id=1, source_target_pairs={{0,6},{1,7},{2,4},{3,5},{4,2},{5,3},{6,0},{7,1},{8,14},{9,15},{10,... | collective-permute-start | bytes 49160 | tf_op jit(solution)/shard_map/ppermute | solution.py:27
  47.0 3.5 %collective-permute-start.10 = (f32[8,4,128]{2,1,0:T(4,128)S(1)}, f32[8,4,128]{2,1,0:T(4,128)S(1)}, u32[]{:S(2)}, u32[]{:S(2)}) collective-permute-start(f32[8,4,128]{2,1,0:T(4,128)S(1)} %columns.2), channel_id=1, source_target_pairs={{0,2},{1,3},{2,0},{3,1},{4,6},{5,7},{6,4},{7,5},{8,10},{9,11},{10,... | collective-permute-start | bytes 49160 | tf_op jit(solution)/shard_map/ppermute | solution.py:27
  47.2 3.3 %collective-permute-start.9 = (f32[8,4,128]{2,1,0:T(4,128)S(1)}, f32[8,4,128]{2,1,0:T(4,128)S(1)}, u32[]{:S(2)}, u32[]{:S(2)}) collective-permute-start(f32[8,4,128]{2,1,0:T(4,128)S(1)} %columns.2), channel_id=1, source_target_pairs={{0,4},{1,5},{2,6},{3,7},{4,0},{5,1},{6,2},{7,3},{8,12},{9,13},{10,... | collective-permute-start | bytes 49160 | tf_op jit(solution)/shard_map/ppermute | solution.py:27
  50.6 8.4 %collective-permute-start.12 = (f32[6,4,128]{2,1,0:T(4,128)S(1)}, f32[6,4,128]{2,1,0:T(4,128)S(1)}, u32[]{:S(2)}, u32[]{:S(2)}) collective-permute-start(f32[6,4,128]{2,1,0:T(4,128)S(1)} %slice_select_fusion), channel_id=1, source_target_pairs={{0,8},{1,9},{2,10},{3,11},{4,255},{5,254},{6,253},{7,252},{8,16},{... | collective-permute-start | bytes 36872 | tf_op jit(solution)/shard_map/ppermute | solution.py:27
  53.7 5.3 %collective-permute-start.13 = (f32[4,4,128]{2,1,0:T(4,128)S(1)}, f32[4,4,128]{2,1,0:T(4,128)S(1)}, u32[]{:S(2)}, u32[]{:S(2)}) collective-permute-start(f32[4,4,128]{2,1,0:T(4,128)S(1)} %slice_select_fusion.1), channel_id=1, source_target_pairs={{0,16},{1,17},{2,18},{3,19},{4,247},{5,246},{6,245},{7,244},{8,24}... | collective-permute-start | bytes 24584 | tf_op jit(solution)/shard_map/ppermute | solution.py:27
  54.8 4.2 %collective-permute-start.14 = (f32[2,4,128]{2,1,0:T(4,128)S(1)}, f32[2,4,128]{2,1,0:T(4,128)S(1)}, u32[]{:S(2)}, u32[]{:S(2)}) collective-permute-start(f32[2,4,128]{2,1,0:T(4,128)S(1)} %slice_select_fusion.3), channel_id=1, source_target_pairs={{0,24},{1,25},{2,26},{3,27},{4,239},{5,238},{6,237},{7,236},{8,35}... | collective-permute-start | bytes 12296 | tf_op jit(solution)/shard_map/ppermute | solution.py:27
  59.0 3.8 %collective-permute-start.15 = (f32[8,4,128]{2,1,0:T(4,128)S(1)}, f32[8,4,128]{2,1,0:T(4,128)S(1)}, u32[]{:S(2)}, u32[]{:S(2)}) collective-permute-start(f32[8,4,128]{2,1,0:T(4,128)S(1)} %log_add_fusion.2), channel_id=1, source_target_pairs={{0,4},{1,5},{2,6},{3,7},{4,0},{5,1},{6,2},{7,3},{8,12},{9,13},{10,... | collective-permute-start | bytes 49160 | tf_op jit(solution)/shard_map/ppermute | solution.py:27
  62.9 11.8 %copy-start.1 = (bf16[1024,256]{1,0:T(8,128)(2,1)S(1)}, bf16[1024,256]{1,0:T(8,128)(2,1)}, u32[]{:S(2)}) copy-start(bf16[1024,256]{1,0:T(8,128)(2,1)} %param.11) | copy-start | bytes 1572868
  64.7 5.1 %collective-permute-start.16 = (f32[1024]{0:T(1024)S(1)}, f32[1024]{0:T(1024)S(1)}, u32[]{:S(2)}, u32[]{:S(2)}) collective-permute-start(f32[1024]{0:T(1024)S(1)} %bitcast.38), channel_id=1, source_target_pairs={{0,5},{1,4},{2,7},{3,6},{4,1},{5,0},{6,3},{7,2},{8,13},{9,12},{10,... | collective-permute-start | bytes 12296 | tf_op jit(solution)/shard_map/ppermute | solution.py:27
  71.6 4.2 %collective-permute-start.19 = (f32[8,4,128]{2,1,0:T(4,128)S(1)}, f32[8,4,128]{2,1,0:T(4,128)S(1)}, u32[]{:S(2)}, u32[]{:S(2)}) collective-permute-start(f32[8,4,128]{2,1,0:T(4,128)S(1)} %columns.3), channel_id=1, source_target_pairs={{0,6},{1,7},{2,4},{3,5},{4,2},{5,3},{6,0},{7,1},{8,14},{9,15},{10,... | collective-permute-start | bytes 49160 | tf_op jit(solution)/shard_map/ppermute | solution.py:27
  73.9 3.5 %collective-permute-start.18 = (f32[8,4,128]{2,1,0:T(4,128)S(1)}, f32[8,4,128]{2,1,0:T(4,128)S(1)}, u32[]{:S(2)}, u32[]{:S(2)}) collective-permute-start(f32[8,4,128]{2,1,0:T(4,128)S(1)} %columns.3), channel_id=1, source_target_pairs={{0,2},{1,3},{2,0},{3,1},{4,6},{5,7},{6,4},{7,5},{8,10},{9,11},{10,... | collective-permute-start | bytes 49160 | tf_op jit(solution)/shard_map/ppermute | solution.py:27
  74.1 3.2 %collective-permute-start.17 = (f32[8,4,128]{2,1,0:T(4,128)S(1)}, f32[8,4,128]{2,1,0:T(4,128)S(1)}, u32[]{:S(2)}, u32[]{:S(2)}) collective-permute-start(f32[8,4,128]{2,1,0:T(4,128)S(1)} %columns.3), channel_id=1, source_target_pairs={{0,4},{1,5},{2,6},{3,7},{4,0},{5,1},{6,2},{7,3},{8,12},{9,13},{10,... | collective-permute-start | bytes 49160 | tf_op jit(solution)/shard_map/ppermute | solution.py:27
  77.4 6.8 %collective-permute-start.21 = (f32[4,128]{1,0:T(4,128)S(1)}, f32[4,128]{1,0:T(4,128)S(1)}, u32[]{:S(2)}, u32[]{:S(2)}) collective-permute-start(f32[4,128]{1,0:T(4,128)S(1)} %fusion.11), channel_id=1, source_target_pairs={{0,16},{1,17},{2,18},{3,19},{4,247},{5,246},{6,245},{7,244},{8,24}... | collective-permute-start | bytes 6152 | tf_op jit(solution)/shard_map/ppermute | solution.py:27
  82.8 3.4 %collective-permute-start.20 = (f32[2,4,128]{2,1,0:T(4,128)S(1)}, f32[2,4,128]{2,1,0:T(4,128)S(1)}, u32[]{:S(2)}, u32[]{:S(2)}) collective-permute-start(f32[2,4,128]{2,1,0:T(4,128)S(1)} %slice_select_fusion.2), channel_id=1, source_target_pairs={{0,8},{1,9},{2,10},{3,11},{4,255},{5,254},{6,253},{7,252},{8,16},{... | collective-permute-start | bytes 12296 | tf_op jit(solution)/shard_map/ppermute | solution.py:27
  86.2 9.6 %collective-permute-start.22 = (f32[2,4,128]{2,1,0:T(4,128)S(1)}, f32[2,4,128]{2,1,0:T(4,128)S(1)}, u32[]{:S(2)}, u32[]{:S(2)}) collective-permute-start(f32[2,4,128]{2,1,0:T(4,128)S(1)} %log_add_fusion.5), channel_id=1, source_target_pairs={{0,4},{1,5},{2,6},{3,7},{4,0},{5,1},{6,2},{7,3},{8,12},{9,13},{10,... | collective-permute-start | bytes 12296 | tf_op jit(solution)/shard_map/ppermute | solution.py:27
  95.9 2.8 %collective-permute-start.23 = (f32[512]{0:T(512)S(1)}, f32[512]{0:T(512)S(1)}, u32[]{:S(2)}, u32[]{:S(2)}) collective-permute-start(f32[512]{0:T(512)S(1)} %fusion.10), channel_id=1, source_target_pairs={{0,1},{1,0},{2,3},{3,2},{4,5},{5,4},{6,7},{7,6},{8,9},{9,8},{10,11... | collective-permute-start | bytes 6152 | tf_op jit(solution)/shard_map/ppermute | solution.py:27
where the time goes:
time: 98.7 us; the launch traced here: 99.3 us
  starting transfers between devices  56.2 us (57%)
  waiting for transfers between devices  22.8 us (23%)
  Pallas kernels  8.96 us (9%)
  other arithmetic  6.94 us (7%)
  local copies, waits for them, and re-layouts  3.5 us (4%)
    ppermute x24, starting transfers between devices, send(): return lax.ppermute(value, ('blk', 'rep'), pairs)  56.2 us
    ppermute x24, waiting for transfers between devices, send(): return lax.ppermute(value, ('blk', 'rep'), pairs)  22.8 us
    pallas_call x3, Pallas kernels, call_first(): pl.pallas_call(functools.partial(first_kernel, numbers, first, last), out...  3.73 us
    pallas_call x2, Pallas kernels, call_columns(): pl.pallas_call(functools.partial(column_kernel, twice), out_shape=jax.Sha...  3.44 us
  transfers between devices with their start and end apart: 24, of which 15 were waited for; matrix products, arithmetic and copies ran while one was open for 6% of the time, Pallas kernels for 3%

commit v1 on v0

--- a/solution.py
+++ b/solution.py
@@ -54,17 +54,11 @@
 
 
 def terms(vector):
-    first = lax.reduce_precision(vector, 8, 7)
-    rest = vector - first
-    second = lax.reduce_precision(rest, 8, 7)
-    third = lax.reduce_precision(rest - second, 8, 7)
-    return [part.astype(jnp.bfloat16) for part in (first, second, third)]
-
-
-def from_terms(rows, which):
-    rows = rows[6 * which : 6 * which + 6]
-    vector = rows[0:2] + rows[2:4] + rows[4:6]
-    return [vector[q // 2 : q // 2 + 1, q % 2 * 128 : q % 2 * 128 + 128] for q in range(4)]
+    parts = []
+    for _ in range(3):
+        parts.append(vector.astype(jnp.bfloat16).astype(jnp.float32))
+        vector = vector - parts[-1]
+    return parts
 
 
 def log_merge(*parts):
@@ -126,10 +120,48 @@
     lax.fori_loop(0, 2 * count, unit, 0)
 
 
+def message_kernel(scale, half, points, masses, initial, src, out, src_out, block_ref, mass_ref, initial_ref, sems):
+    columns, depth = block_ref.shape
+    src_copy = pltpu.make_async_copy(src, src_out, sems.at[1])
+    copy = pltpu.make_async_copy(
+        points.at[pl.ds(pl.multiple_of(half[0] * columns, columns), columns), :], block_ref, sems.at[0]
+    )
+    small = [
+        pltpu.make_async_copy(masses, mass_ref, sems.at[2]),
+        pltpu.make_async_copy(initial, initial_ref, sems.at[3]),
+    ]
+    for start in (copy, *small, src_copy):
+        start.start()
+    copy.wait()
+    value = block_ref[...].astype(jnp.float32)
+    out[:columns, :] = (value * scale).astype(jnp.bfloat16)
+    squares = value * value
+    high = squares.astype(jnp.bfloat16)
+    low = (squares - high.astype(jnp.float32)).astype(jnp.bfloat16)
+    ones = jnp.ones((8, depth), jnp.bfloat16)
+    norms = sum(
+        lax.dot_general(ones, part, (((1,), (1,)), ((), ())), preferred_element_type=jnp.float32)
+        for part in (high, low)
+    )
+    count = columns // 128
+    norms = jnp.concatenate([norms[0:1, q * 128 : (q + 1) * 128] for q in range(count)], axis=0)
+
+    def pick(ref):
+        return jnp.where(half[0] == 0, ref[:count, :], ref[count:, :])
+
+    for copy in small:
+        copy.wait()
+    mass = pick(mass_ref)
+    bias = mass + (pick(initial_ref) - 0.5 * norms) * scale
+    rows = [jnp.concatenate(pair, axis=1) for pair in zip(terms(bias), terms(mass))]
+    rows.append(jnp.zeros((TAIL - 3 * count, 256), jnp.float32))
+    out[columns:, :] = jnp.concatenate(rows, axis=0).astype(jnp.bfloat16)
+    src_copy.wait()
+
+
 def first_kernel(numbers, first, last, flags, *refs):
-    count = len(numbers)
-    sources, targets = refs[:2], refs[2 : 2 + count]
-    refs = refs[2 + count :]
+    sources, targets = refs[:2], refs[2 : 2 + len(numbers)]
+    refs = refs[2 + len(numbers) :]
     if not first:
         refs = refs[4:]
     cross, masses, top_ref, total_ref = refs[:4]
@@ -144,9 +176,10 @@
     for k, number in enumerate(numbers):
         tgt_ref[k] = targets[k][:width, :]
         tail = targets[k][width:, :].astype(jnp.float32)
-        for q, (row, mass) in enumerate(zip(from_terms(tail, 0), from_terms(tail, 1))):
-            bias_ref[k, q : q + 1, :] = row
-            masses[number, q : q + 1, :] = mass
+        count = width // 128
+        vectors = tail[:count] + tail[count : 2 * count] + tail[2 * count : 3 * count]
+        bias_ref[k] = vectors[:, :128]
+        masses[number] = vectors[:, 128:]
 
     def body(number, side):
         k = number - numbers[0]
@@ -162,7 +195,7 @@
         bias = [bias_ref[k, q : q + 1, :] for q in range(width // 128)]
         row_update(cross, number, bias, False, side, half, top_ref, total_ref)
 
-    each_kept(flags, numbers[0], count, body)
+    each_kept(flags, numbers[0], len(numbers), body)
     if last:
         row_finish(top_ref, total_ref, refs[4])
 
@@ -240,6 +273,31 @@
 
 def in_vmem(value):
     return pltpu.with_memory_space_constraint(value, pltpu.VMEM)
+
+
+def in_hbm(value):
+    return pltpu.with_memory_space_constraint(value, pltpu.HBM)
+
+
+def call_message(scale, half_index, points, masses, initial, src):
+    columns, depth = points.shape[0] // 2, points.shape[1]
+    return pl.pallas_call(
+        functools.partial(message_kernel, scale),
+        out_shape=[
+            pltpu.VMEM((columns + TAIL, depth), jnp.bfloat16),
+            pltpu.VMEM(src.shape, jnp.bfloat16),
+        ],
+        in_specs=[SCALARS] + [pl.BlockSpec(memory_space=pltpu.HBM)] * 4,
+        out_specs=[WHOLE] * 2,
+        scratch_shapes=[
+            pltpu.VMEM((columns, depth), jnp.bfloat16),
+            pltpu.VMEM((2 * columns // 128, 128), jnp.float32),
+            pltpu.VMEM((2 * columns // 128, 128), jnp.float32),
+            pltpu.SemaphoreType.DMA((4,)),
+        ],
+        compiler_params=PARAMS,
+        name="message",
+    )(half_index.reshape(1), *map(in_hbm, (points, masses.reshape(-1, 128), initial.reshape(-1, 128), src)))
 
 
 def call_first(numbers, first, last, flags, sources, targets, state):
@@ -320,23 +378,17 @@
     width = tgt_points.shape[0]
     columns = width // 2
 
-    def my_half(value):
-        return lax.dynamic_slice_in_dim(value, half_index * columns, columns, 0)
-
-    first_scale = 1.0 / EPS_START
-    points = my_half(tgt_points)
-    masses = my_half(tgt_log_mass)
-    bias = masses + (my_half(initial_potential) - half_norms(points)) * first_scale
-    tail = [part.reshape(-1, points.shape[1]) for part in terms(bias) + terms(masses)]
-    tail.append(jnp.zeros((TAIL - 6 * columns // points.shape[1], points.shape[1]), jnp.bfloat16))
-    message = jnp.concatenate([points * jnp.bfloat16(first_scale)] + tail, axis=0)
+    mate = send(src_points, diagonal, blocks)
+    message, own = call_message(
+        1.0 / EPS_START, half_index, tgt_points, tgt_log_mass, initial_potential, src_points
+    )
 
     before = send(message, along(2, blocks), blocks)
     after = send(message, along(-2, blocks), blocks)
-    third = send(message, by_core(-3, 3, blocks), blocks)
+    tied, mate = lax.optimization_barrier((message, mate))
+    third = send(tied, by_core(-3, 3, blocks), blocks)
     beside = send(message, sibling, blocks)
-    mate = send(src_points, diagonal, blocks)
-    sources = [src_points, mate]
+    sources = [own, mate]
     groups = ((0, 1), (2, 3, 4), (5, 6, 7))
 
     even_slots = (3, 4, 1, 5, 0, 2, 6, 7)

time: 98.7 us -> 94.3 us (0.955); the launches traced: 99.3 us -> 93.2 us
  starting transfers between devices: 56.2 us -> 51 us
  Pallas kernels: 8.96 us -> 13.2 us
  other arithmetic: 6.94 us -> 4.05 us
  local copies, waits for them, and re-layouts: 3.5 us -> 2.32 us
  waiting for transfers between devices: 22.8 us -> 21.7 us
    ppermute x24, starting transfers between devices: 56.2 us -> 51 us  [send(): return lax.ppermute(value, ('blk', 'rep'), pairs)]
    pallas_call x0 -> x1, Pallas kernels: none -> 1.3 us  [call_message(): pl.pallas_call(functools.partial(message_kernel, scale), out_shape=[pltpu...]
    pallas_call x3, Pallas kernels: 3.73 us -> 4.91 us  [call_first(): pl.pallas_call(functools.partial(first_kernel, numbers, first, last), out...]
    pallas_call x2, Pallas kernels: 3.44 us -> 4.61 us  [call_columns(): pl.pallas_call(functools.partial(column_kernel, twice), out_shape=jax.Sha...]
    reduce_sum x3 -> x2, other arithmetic: 1.46 us -> 0.36 us  [half_norms(): return 0.5 * jnp.sum(widened * widened, axis=1)]
    ppermute x24, waiting for transfers between devices: 22.8 us -> 21.7 us  [send(): return lax.ppermute(value, ('blk', 'rep'), pairs)]
    mul x1 -> x0, other arithmetic: 1 us -> none  [local(): points * jnp.bfloat16(first_scale)]
  transfers between devices with their start and end apart: 24 -> 24, of which waited for: 15 -> 14; matrix products, arithmetic and copies ran while one was open for 6% -> 6% of each run, Pallas kernels for 3% -> 5%
where the time goes in v1:
time: 94.3 us; the launch traced here: 93.2 us
  starting transfers between devices  51 us (54%)
  waiting for transfers between devices  21.7 us (23%)
  Pallas kernels  13.2 us (14%)
  other arithmetic  4.05 us (4%)
  local copies, waits for them, and re-layouts  2.32 us (2%)
    ppermute x24, starting transfers between devices, send(): return lax.ppermute(value, ('blk', 'rep'), pairs)  51 us
    ppermute x24, waiting for transfers between devices, send(): return lax.ppermute(value, ('blk', 'rep'), pairs)  21.7 us
    pallas_call x3, Pallas kernels, call_first(): pl.pallas_call(functools.partial(first_kernel, numbers, first, last), out...  4.91 us
    pallas_call x2, Pallas kernels, call_columns(): pl.pallas_call(functools.partial(column_kernel, twice), out_shape=jax.Sha...  4.61 us
    pallas_call x1, Pallas kernels, call_rows(): pl.pallas_call(row_kernel, out_shape=jax.ShapeDtypeStruct((rows // 128, 1...  2.36 us
  transfers between devices with their start and end apart: 24, of which 14 were waited for; matrix products, arithmetic and copies ran while one was open for 6% of the time, Pallas kernels for 5%

profile of v1, /device:TPU:1, one launch (start us, length us, event | category | flops | bytes accessed | tf_op | source)
XLA Modules:
  0.0 93.2 jit_solution(7065909680766294471)
XLA Ops:
  0.6 3.1 %collective-permute-start = (bf16[512,256]{1,0:T(8,128)(2,1)}, bf16[512,256]{1,0:T(8,128)(2,1)S(1)}, u32[]{:S(2)}, u32[]{:S(2)}) collective-permute-start(bf16[512,256]{1,0:T(8,128)(2,1)} %src.1), channel_id=1, source_target_pairs={{0,5},{1,4},{2,7},{3,6},{4,1},{5,0},{6,3},{7,2},{8,13},{9,12},{10,... | collective-permute-start | bytes 786440 | tf_op jit(solution)/shard_map/ppermute | solution.py:27
  3.7 1.3 %message.1 = (bf16[528,256]{1,0:T(8,128)(2,1)S(1)}, bf16[512,256]{1,0:T(8,128)(2,1)S(1)}) custom-call(s32[1]{0:T(128)} %bitcast.2.half, bf16[1024,256]{1,0:T(8,128)(2,1)} %points.1, f32[8,128]{1,0:T(8,128)} %bitcast.61, f32[8,128]{1,0:T(8,128)} %bitcast.62, bf16[512,256]{1,0:T(8,128)(2,1)} %src.1), custom_call_target="tpu_custom_call" | custom-call | tf_op jit(solution)/shard_map/message/pallas_call | solution.py:284
  5.1 0.4 collective-permute-start.1
  5.4 1.1 %collective-permute-start.2 = (bf16[528,256]{1,0:T(8,128)(2,1)S(1)}, bf16[528,256]{1,0:T(8,128)(2,1)S(1)}, u32[]{:S(2)}, u32[]{:S(2)}) collective-permute-start(bf16[528,256]{1,0:T(8,128)(2,1)S(1)} %get-tuple-element.31.refs_2_), channel_id=1, source_target_pairs={{0,8},{1,9},{2,10},{3,11},{4,12},{5,13},{6,14},{7,15},{8,16},{9,17... | collective-permute-start | bytes 811016 | tf_op jit(solution)/shard_map/ppermute | solution.py:27
  6.5 8.1 %collective-permute-start.3 = (bf16[528,256]{1,0:T(8,128)(2,1)S(1)}, bf16[528,256]{1,0:T(8,128)(2,1)S(1)}, u32[]{:S(2)}, u32[]{:S(2)}) collective-permute-start(bf16[528,256]{1,0:T(8,128)(2,1)S(1)} %get-tuple-element.31.refs_2_), channel_id=1, source_target_pairs={{0,251},{1,250},{2,249},{3,248},{4,255},{5,254},{6,253},{7,252},{8... | collective-permute-start | bytes 811016 | tf_op jit(solution)/shard_map/ppermute | solution.py:27
  14.6 1.3 %fusion.9 = (s32[1]{0:T(128)}, s32[1]{0:T(128)}) fusion(s32[64]{0:T(128)} %param.15, s32[]{:T(128)S(6)} %select_n.121, s32[]{:T(128)S(6)} %select_n.116), kind=kLoop, calls=%fused_computation.53 | loop fusion | bytes 24 | tf_op jit(solution)/shard_map/dynamic_slice | solution.py:401
  15.9 0.7 and_select_fusion
  16.6 1.3 %iota_compare_fusion = (pred[7]{0:T(512)(128)(4,1)S(1)}, pred[7]{0:T(512)(128)(4,1)S(1)}) fusion(s32[]{:T(128)} %bitcast.1, s32[]{:T(128)} %bitcast), kind=kLoop, calls=%fused_computation.49 | loop fusion | flops 14 | bytes 22 | tf_op jit(solution)/shard_map/lt | solution.py:401
  17.9 1.0 %dynamic-slice_reduce_fusion.1 = (s32[7]{0:T(128)S(1)}, s32[7]{0:T(128)S(1)}) fusion(s32[64,7]{0,1:T(8,128)} %param.14, s32[]{:T(128)S(6)} %select_n.116, s32[]{:T(128)S(6)} %select_n.121), kind=kLoop, calls=%fused_computation.32 | loop fusion | bytes 120 | tf_op jit(solution)/shard_map/dynamic_slice | solution.py:400
  18.9 0.0 collective-permute-done.refs_1_
  18.9 0.1 collective-permute-start.4
  19.0 0.2 and_reduce_fusion.1
  19.2 0.1 pad_add_fusion.flags
  19.3 0.0 collective-permute-done.1.refs_3_
  19.3 1.9 %first_rows.3 = (f32[8,1024,512]{2,1,0:T(8,128)S(1)}, f32[8,4,128]{2,1,0:T(4,128)S(1)}, f32[1024,128]{1,0:T(8,128)S(1)}, f32[1024,128]{1,0:T(8,128)S(1)}) custom-call(s32[24]{0:T(128)S(1)} %pad_add_fusion.flags, bf16[512,256]{1,0:T(8,128)(2,1)S(1)} %get-tuple-element.24.refs_0_, bf16[512,256]{1,0:T(8,128)(2,1)S(1)} %collective-permute-done.refs_1_, ...), custom_call_target="tpu_custom_call" | custom-call | flops 536870912 | bytes 1048576 | tf_op jit(solution)/shard_map/first_rows/pallas_call | solution.py:319
  21.2 5.6 %collective-permute-done.2.refs_2_ = bf16[528,256]{1,0:T(8,128)(2,1)S(1)} collective-permute-done((bf16[528,256]{1,0:T(8,128)(2,1)S(1)}, bf16[528,256]{1,0:T(8,128)(2,1)S(1)}, u32[]{:S(2)}, u32[]{:S(2)}) %collective-permute-start.2) | collective-permute-done | bytes 270368 | tf_op jit(solution)/shard_map/ppermute | solution.py:27
  26.8 2.0 %collective-permute-done.3.refs_3_ = bf16[528,256]{1,0:T(8,128)(2,1)S(1)} collective-permute-done((bf16[528,256]{1,0:T(8,128)(2,1)S(1)}, bf16[528,256]{1,0:T(8,128)(2,1)S(1)}, u32[]{:S(2)}, u32[]{:S(2)}) %collective-permute-start.3) | collective-permute-done | bytes 270368 | tf_op jit(solution)/shard_map/ppermute | solution.py:27
  28.9 0.0 collective-permute-done.4.refs_4_
  28.9 5.3 %collective-permute-start.5 = (bf16[528,256]{1,0:T(8,128)(2,1)S(1)}, bf16[528,256]{1,0:T(8,128)(2,1)S(1)}, u32[]{:S(2)}, u32[]{:S(2)}) collective-permute-start(bf16[528,256]{1,0:T(8,128)(2,1)S(1)} %collective-permute-done.2.refs_2_), channel_id=1, source_target_pairs={{0,4},{1,5},{2,6},{3,7},{4,0},{5,1},{6,2},{7,3},{8,12},{9,13},{10,... | collective-permute-start | bytes 811016 | tf_op jit(solution)/shard_map/ppermute | solution.py:27
  34.1 0.0 collective-permute-start.6
  34.1 0.5 collective-permute-start.7
  34.6 1.3 %first_rows.4 = (f32[8,1024,512]{2,1,0:T(8,128)S(1)}, f32[8,4,128]{2,1,0:T(4,128)S(1)}, f32[1024,128]{1,0:T(8,128)S(1)}, f32[1024,128]{1,0:T(8,128)S(1)}) custom-call(s32[24]{0:T(128)S(1)} %pad_add_fusion.flags, bf16[512,256]{1,0:T(8,128)(2,1)S(1)} %get-tuple-element.24.refs_0_, ...), custom_call_target="tpu_custom_call", output_to_operand_aliasing={{0}: (6, {}), {1}: (7, {}), {2}: (8, {}), {3}: (9, {})} | custom-call | flops 805306368 | bytes 1572864 | tf_op jit(solution)/shard_map/first_rows/pallas_call | solution.py:319
  36.0 0.0 collective-permute-done.5.refs_2_
  36.0 0.1 collective-permute-done.7.refs_4_
  36.1 1.7 %first_rows.5 = (f32[8,1024,512]{2,1,0:T(8,128)S(1)}, f32[8,4,128]{2,1,0:T(4,128)S(1)}, f32[1024,128]{1,0:T(8,128)S(1)}, f32[1024,128]{1,0:T(8,128)S(1)}, f32[8,128]{1,0:T(8,128)S(1)}) custom-call(s32[24]{0:T(128)S(1)} %pad_add_fusion.flags, ...), custom_call_target="tpu_custom_call", output_to_operand_aliasing={{0}: (6, {}), {1}: (7, {}), {2}: (8, {}), {3}: (9, {})} | custom-call | flops 805306368 | bytes 1572864 | tf_op jit(solution)/shard_map/first_rows/pallas_call | solution.py:319
  37.8 1.0 %collective-permute-start.8 = (f32[1536]{0:T(1024)S(1)}, f32[1536]{0:T(1024)S(1)}, u32[]{:S(2)}, u32[]{:S(2)}) collective-permute-start(f32[1536]{0:T(1024)S(1)} %pad_maximum_fusion), channel_id=1, source_target_pairs={{0,5},{1,4},{2,7},{3,6},{4,1},{5,0},{6,3},{7,2},{8,13},{9,12},{10,... | collective-permute-start | bytes 18440 | tf_op jit(solution)/shard_map/ppermute | solution.py:27
  38.8 2.2 %collective-permute-done.8 = f32[1536]{0:T(1024)S(1)} collective-permute-done((f32[1536]{0:T(1024)S(1)}, f32[1536]{0:T(1024)S(1)}, u32[]{:S(2)}, u32[]{:S(2)}) %collective-permute-start.8) | collective-permute-done | bytes 6176 | tf_op jit(solution)/shard_map/ppermute | solution.py:27
  41.0 2.3 %columns.2 = f32[8,4,128]{2,1,0:T(4,128)S(1)} custom-call(s32[24]{0:T(128)S(1)} %pad_add_fusion.flags, f32[8,1024,512]{2,1,0:T(8,128)S(1)} %get-tuple-element.43.cross, f32[8,128]{1,0:T(8,128)S(1)} %add_subtract_fusion.1.weights), custom_call_target="tpu_custom_call" | custom-call | tf_op jit(solution)/shard_map/columns/pallas_call | solution.py:355
  43.3 2.0 %collective-permute-start.11 = (f32[8,4,128]{2,1,0:T(4,128)S(1)}, f32[8,4,128]{2,1,0:T(4,128)S(1)}, u32[]{:S(2)}, u32[]{:S(2)}) collective-permute-start(f32[8,4,128]{2,1,0:T(4,128)S(1)} %columns.2), channel_id=1, source_target_pairs={{0,6},{1,7},{2,4},{3,5},{4,2},{5,3},{6,0},{7,1},{8,14},{9,15},{10,... | collective-permute-start | bytes 49160 | tf_op jit(solution)/shard_map/ppermute | solution.py:27
  45.2 0.7 collective-permute-start.10
  46.0 0.4 collective-permute-start.9
  46.4 1.2 %collective-permute-done.11 = f32[8,4,128]{2,1,0:T(4,128)S(1)} collective-permute-done((f32[8,4,128]{2,1,0:T(4,128)S(1)}, f32[8,4,128]{2,1,0:T(4,128)S(1)}, u32[]{:S(2)}, u32[]{:S(2)}) %collective-permute-start.11) | collective-permute-done | bytes 16416 | tf_op jit(solution)/shard_map/ppermute | solution.py:27
  47.6 1.1 %collective-permute-done.10 = f32[8,4,128]{2,1,0:T(4,128)S(1)} collective-permute-done((f32[8,4,128]{2,1,0:T(4,128)S(1)}, f32[8,4,128]{2,1,0:T(4,128)S(1)}, u32[]{:S(2)}, u32[]{:S(2)}) %collective-permute-start.10) | collective-permute-done | bytes 16416 | tf_op jit(solution)/shard_map/ppermute | solution.py:27
  48.7 0.0 collective-permute-done.9
  48.8 3.8 %collective-permute-start.12 = (f32[6,4,128]{2,1,0:T(4,128)S(1)}, f32[6,4,128]{2,1,0:T(4,128)S(1)}, u32[]{:S(2)}, u32[]{:S(2)}) collective-permute-start(f32[6,4,128]{2,1,0:T(4,128)S(1)} %slice_select_fusion), channel_id=1, source_target_pairs={{0,8},{1,9},{2,10},{3,11},{4,255},{5,254},{6,253},{7,252},{8,16},{... | collective-permute-start | bytes 36872 | tf_op jit(solution)/shard_map/ppermute | solution.py:27
  52.6 1.2 %collective-permute-start.13 = (f32[4,4,128]{2,1,0:T(4,128)S(1)}, f32[4,4,128]{2,1,0:T(4,128)S(1)}, u32[]{:S(2)}, u32[]{:S(2)}) collective-permute-start(f32[4,4,128]{2,1,0:T(4,128)S(1)} %slice_select_fusion.1), channel_id=1, source_target_pairs={{0,16},{1,17},{2,18},{3,19},{4,247},{5,246},{6,245},{7,244},{8,24}... | collective-permute-start | bytes 24584 | tf_op jit(solution)/shard_map/ppermute | solution.py:27
  53.8 1.2 %collective-permute-start.14 = (f32[2,4,128]{2,1,0:T(4,128)S(1)}, f32[2,4,128]{2,1,0:T(4,128)S(1)}, u32[]{:S(2)}, u32[]{:S(2)}) collective-permute-start(f32[2,4,128]{2,1,0:T(4,128)S(1)} %slice_select_fusion.3), channel_id=1, source_target_pairs={{0,24},{1,25},{2,26},{3,27},{4,239},{5,238},{6,237},{7,236},{8,35}... | collective-permute-start | bytes 12296 | tf_op jit(solution)/shard_map/ppermute | solution.py:27
  54.9 2.8 %collective-permute-done.14 = f32[2,4,128]{2,1,0:T(4,128)S(1)} collective-permute-done((f32[2,4,128]{2,1,0:T(4,128)S(1)}, f32[2,4,128]{2,1,0:T(4,128)S(1)}, u32[]{:S(2)}, u32[]{:S(2)}) %collective-permute-start.14) | collective-permute-done | bytes 4128 | tf_op jit(solution)/shard_map/ppermute | solution.py:27
  57.7 0.0 collective-permute-done.13
  57.7 0.0 collective-permute-done.12
  57.8 3.1 %collective-permute-start.15 = (f32[8,4,128]{2,1,0:T(4,128)S(1)}, f32[8,4,128]{2,1,0:T(4,128)S(1)}, u32[]{:S(2)}, u32[]{:S(2)}) collective-permute-start(f32[8,4,128]{2,1,0:T(4,128)S(1)} %log_add_fusion.2), channel_id=1, source_target_pairs={{0,4},{1,5},{2,6},{3,7},{4,0},{5,1},{6,2},{7,3},{8,12},{9,13},{10,... | collective-permute-start | bytes 49160 | tf_op jit(solution)/shard_map/ppermute | solution.py:27
  60.9 0.8 collective-permute-done.15
  61.7 0.0 copy-start
  61.8 0.0 copy-start.1
  61.8 2.4 %rows.1 = f32[8,128]{1,0:T(8,128)S(1)} custom-call(s32[24]{0:T(128)S(1)} %pad_add_fusion.flags, f32[8,1024,512]{2,1,0:T(8,128)S(1)} %get-tuple-element.43.cross, f32[8,4,128]{2,1,0:T(4,128)S(1)} %get-tuple-element.44.masses, f32[8,4,128]{2,1,0:T(4,128)S(1)} %bitcast.40), custom_call_target="tpu_custom_call" | custom-call | tf_op jit(solution)/shard_map/rows/pallas_call | solution.py:342
  64.1 2.2 %collective-permute-start.16 = (f32[1024]{0:T(1024)S(1)}, f32[1024]{0:T(1024)S(1)}, u32[]{:S(2)}, u32[]{:S(2)}) collective-permute-start(f32[1024]{0:T(1024)S(1)} %bitcast.41), channel_id=1, source_target_pairs={{0,5},{1,4},{2,7},{3,6},{4,1},{5,0},{6,3},{7,2},{8,13},{9,12},{10,... | collective-permute-start | bytes 12296 | tf_op jit(solution)/shard_map/ppermute | solution.py:27
  66.4 1.3 %collective-permute-done.16 = f32[1024]{0:T(1024)S(1)} collective-permute-done((f32[1024]{0:T(1024)S(1)}, f32[1024]{0:T(1024)S(1)}, u32[]{:S(2)}, u32[]{:S(2)}) %collective-permute-start.16) | collective-permute-done | bytes 4128 | tf_op jit(solution)/shard_map/ppermute | solution.py:27
  67.7 2.3 %columns.3 = f32[8,4,128]{2,1,0:T(4,128)S(1)} custom-call(s32[24]{0:T(128)S(1)} %pad_add_fusion.flags, f32[8,1024,512]{2,1,0:T(8,128)S(1)} %get-tuple-element.43.cross, f32[8,128]{1,0:T(8,128)S(1)} %add_subtract_fusion.weights), custom_call_target="tpu_custom_call" | custom-call | tf_op jit(solution)/shard_map/columns/pallas_call | solution.py:355
  70.0 2.9 %collective-permute-start.19 = (f32[8,4,128]{2,1,0:T(4,128)S(1)}, f32[8,4,128]{2,1,0:T(4,128)S(1)}, u32[]{:S(2)}, u32[]{:S(2)}) collective-permute-start(f32[8,4,128]{2,1,0:T(4,128)S(1)} %columns.3), channel_id=1, source_target_pairs={{0,6},{1,7},{2,4},{3,5},{4,2},{5,3},{6,0},{7,1},{8,14},{9,15},{10,... | collective-permute-start | bytes 49160 | tf_op jit(solution)/shard_map/ppermute | solution.py:27
  72.9 0.0 collective-permute-start.18
  72.9 0.5 collective-permute-start.17
  73.4 0.2 multiply_reduce_fusion
  73.6 0.7 collective-permute-done.19
  74.3 2.1 %collective-permute-done.18 = f32[8,4,128]{2,1,0:T(4,128)S(1)} collective-permute-done((f32[8,4,128]{2,1,0:T(4,128)S(1)}, f32[8,4,128]{2,1,0:T(4,128)S(1)}, u32[]{:S(2)}, u32[]{:S(2)}) %collective-permute-start.18) | collective-permute-done | bytes 16416 | tf_op jit(solution)/shard_map/ppermute | solution.py:27
  76.4 2.8 %collective-permute-start.21 = (f32[4,128]{1,0:T(4,128)S(1)}, f32[4,128]{1,0:T(4,128)S(1)}, u32[]{:S(2)}, u32[]{:S(2)}) collective-permute-start(f32[4,128]{1,0:T(4,128)S(1)} %fusion.7), channel_id=1, source_target_pairs={{0,16},{1,17},{2,18},{3,19},{4,247},{5,246},{6,245},{7,244},{8,24}... | collective-permute-start | bytes 6152 | tf_op jit(solution)/shard_map/ppermute | solution.py:27
  79.3 3.8 %collective-permute-start.20 = (f32[2,4,128]{2,1,0:T(4,128)S(1)}, f32[2,4,128]{2,1,0:T(4,128)S(1)}, u32[]{:S(2)}, u32[]{:S(2)}) collective-permute-start(f32[2,4,128]{2,1,0:T(4,128)S(1)} %slice_select_fusion.2), channel_id=1, source_target_pairs={{0,8},{1,9},{2,10},{3,11},{4,255},{5,254},{6,253},{7,252},{8,16},{... | collective-permute-start | bytes 12296 | tf_op jit(solution)/shard_map/ppermute | solution.py:27
  83.1 0.1 multiply_reduce_fusion.1
  83.3 0.6 collective-permute-done.20
  83.9 5.0 %collective-permute-start.22 = (f32[2,4,128]{2,1,0:T(4,128)S(1)}, f32[2,4,128]{2,1,0:T(4,128)S(1)}, u32[]{:S(2)}, u32[]{:S(2)}) collective-permute-start(f32[2,4,128]{2,1,0:T(4,128)S(1)} %log_add_fusion.5), channel_id=1, source_target_pairs={{0,4},{1,5},{2,6},{3,7},{4,0},{5,1},{6,2},{7,3},{8,12},{9,13},{10,... | collective-permute-start | bytes 12296 | tf_op jit(solution)/shard_map/ppermute | solution.py:27
  88.9 0.8 collective-permute-done.22
  89.8 1.8 %collective-permute-start.23 = (f32[512]{0:T(512)S(1)}, f32[512]{0:T(512)S(1)}, u32[]{:S(2)}, u32[]{:S(2)}) collective-permute-start(f32[512]{0:T(512)S(1)} %fusion.6), channel_id=1, source_target_pairs={{0,1},{1,0},{2,3},{3,2},{4,5},{5,4},{6,7},{7,6},{8,9},{9,8},{10,11... | collective-permute-start | bytes 6152 | tf_op jit(solution)/shard_map/ppermute | solution.py:27
  91.6 0.6 multiply_subtract_fusion
  92.2 0.4 collective-permute-done.23
  92.6 0.6 fusion.1
  (27 shorter events, 0.3 us)
Async XLA Ops:
  0.6 18.3 %collective-permute-start = (bf16[512,256]{1,0:T(8,128)(2,1)}, bf16[512,256]{1,0:T(8,128)(2,1)S(1)}, u32[]{:S(2)}, u32[]{:S(2)}) collective-permute-start(bf16[512,256]{1,0:T(8,128)(2,1)} %src.1), channel_id=1, source_target_pairs={{0,5},{1,4},{2,7},{3,6},{4,1},{5,0},{6,3},{7,2},{8,13},{9,12},{10,... | collective-permute-start | bytes 786440 | tf_op jit(solution)/shard_map/ppermute | solution.py:27
  5.1 14.2 %collective-permute-start.1 = (bf16[528,256]{1,0:T(8,128)(2,1)S(1)}, bf16[528,256]{1,0:T(8,128)(2,1)S(1)}, u32[]{:S(2)}, u32[]{:S(2)}) collective-permute-start(bf16[528,256]{1,0:T(8,128)(2,1)S(1)} %get-tuple-element.31.refs_2_), channel_id=1, source_target_pairs={{0,4},{1,5},{2,6},{3,7},{4,0},{5,1},{6,2},{7,3},{8,12},{9,13},{10,... | collective-permute-start | bytes 811016 | tf_op jit(solution)/shard_map/ppermute | solution.py:27
  5.4 21.4 %collective-permute-start.2 = (bf16[528,256]{1,0:T(8,128)(2,1)S(1)}, bf16[528,256]{1,0:T(8,128)(2,1)S(1)}, u32[]{:S(2)}, u32[]{:S(2)}) collective-permute-start(bf16[528,256]{1,0:T(8,128)(2,1)S(1)} %get-tuple-element.31.refs_2_), channel_id=1, source_target_pairs={{0,8},{1,9},{2,10},{3,11},{4,12},{5,13},{6,14},{7,15},{8,16},{9,17... | collective-permute-start | bytes 811016 | tf_op jit(solution)/shard_map/ppermute | solution.py:27
  6.5 22.3 %collective-permute-start.3 = (bf16[528,256]{1,0:T(8,128)(2,1)S(1)}, bf16[528,256]{1,0:T(8,128)(2,1)S(1)}, u32[]{:S(2)}, u32[]{:S(2)}) collective-permute-start(bf16[528,256]{1,0:T(8,128)(2,1)S(1)} %get-tuple-element.31.refs_2_), channel_id=1, source_target_pairs={{0,251},{1,250},{2,249},{3,248},{4,255},{5,254},{6,253},{7,252},{8... | collective-permute-start | bytes 811016 | tf_op jit(solution)/shard_map/ppermute | solution.py:27
  18.9 10.0 %collective-permute-start.4 = (bf16[528,256]{1,0:T(8,128)(2,1)S(1)}, bf16[528,256]{1,0:T(8,128)(2,1)S(1)}, u32[]{:S(2)}, u32[]{:S(2)}) collective-permute-start(bf16[528,256]{1,0:T(8,128)(2,1)S(1)} %get-tuple-element.31.refs_2_), channel_id=1, source_target_pairs={{0,247},{1,246},{2,245},{3,244},{4,16},{5,17},{6,18},{7,19},{8,255... | collective-permute-start | bytes 811016 | tf_op jit(solution)/shard_map/ppermute | solution.py:27
  28.9 8.9 %copy-start.2 = (f32[512]{0:T(512)S(1)}, f32[512]{0:T(512)}, u32[]{:S(2)}) copy-start(f32[512]{0:T(512)} %param.10) | copy-start | bytes 6148
  28.9 7.1 %collective-permute-start.5 = (bf16[528,256]{1,0:T(8,128)(2,1)S(1)}, bf16[528,256]{1,0:T(8,128)(2,1)S(1)}, u32[]{:S(2)}, u32[]{:S(2)}) collective-permute-start(bf16[528,256]{1,0:T(8,128)(2,1)S(1)} %collective-permute-done.2.refs_2_), channel_id=1, source_target_pairs={{0,4},{1,5},{2,6},{3,7},{4,0},{5,1},{6,2},{7,3},{8,12},{9,13},{10,... | collective-permute-start | bytes 811016 | tf_op jit(solution)/shard_map/ppermute | solution.py:27
  34.1 1.9 %collective-permute-start.6 = (bf16[528,256]{1,0:T(8,128)(2,1)S(1)}, bf16[528,256]{1,0:T(8,128)(2,1)S(1)}, u32[]{:S(2)}, u32[]{:S(2)}) collective-permute-start(bf16[528,256]{1,0:T(8,128)(2,1)S(1)} %collective-permute-done.3.refs_3_), channel_id=1, source_target_pairs={{0,4},{1,5},{2,6},{3,7},{4,0},{5,1},{6,2},{7,3},{8,12},{9,13},{10,... | collective-permute-start | bytes 811016 | tf_op jit(solution)/shard_map/ppermute | solution.py:27
  34.1 1.9 %collective-permute-start.7 = (bf16[528,256]{1,0:T(8,128)(2,1)S(1)}, bf16[528,256]{1,0:T(8,128)(2,1)S(1)}, u32[]{:S(2)}, u32[]{:S(2)}) collective-permute-start(bf16[528,256]{1,0:T(8,128)(2,1)S(1)} %collective-permute-done.4.refs_4_), channel_id=1, source_target_pairs={{0,4},{1,5},{2,6},{3,7},{4,0},{5,1},{6,2},{7,3},{8,12},{9,13},{10,... | collective-permute-start | bytes 811016 | tf_op jit(solution)/shard_map/ppermute | solution.py:27
  37.8 3.2 %collective-permute-start.8 = (f32[1536]{0:T(1024)S(1)}, f32[1536]{0:T(1024)S(1)}, u32[]{:S(2)}, u32[]{:S(2)}) collective-permute-start(f32[1536]{0:T(1024)S(1)} %pad_maximum_fusion), channel_id=1, source_target_pairs={{0,5},{1,4},{2,7},{3,6},{4,1},{5,0},{6,3},{7,2},{8,13},{9,12},{10,... | collective-permute-start | bytes 18440 | tf_op jit(solution)/shard_map/ppermute | solution.py:27
  43.3 4.3 %collective-permute-start.11 = (f32[8,4,128]{2,1,0:T(4,128)S(1)}, f32[8,4,128]{2,1,0:T(4,128)S(1)}, u32[]{:S(2)}, u32[]{:S(2)}) collective-permute-start(f32[8,4,128]{2,1,0:T(4,128)S(1)} %columns.2), channel_id=1, source_target_pairs={{0,6},{1,7},{2,4},{3,5},{4,2},{5,3},{6,0},{7,1},{8,14},{9,15},{10,... | collective-permute-start | bytes 49160 | tf_op jit(solution)/shard_map/ppermute | solution.py:27
  45.2 3.5 %collective-permute-start.10 = (f32[8,4,128]{2,1,0:T(4,128)S(1)}, f32[8,4,128]{2,1,0:T(4,128)S(1)}, u32[]{:S(2)}, u32[]{:S(2)}) collective-permute-start(f32[8,4,128]{2,1,0:T(4,128)S(1)} %columns.2), channel_id=1, source_target_pairs={{0,2},{1,3},{2,0},{3,1},{4,6},{5,7},{6,4},{7,5},{8,10},{9,11},{10,... | collective-permute-start | bytes 49160 | tf_op jit(solution)/shard_map/ppermute | solution.py:27
  46.0 2.7 %collective-permute-start.9 = (f32[8,4,128]{2,1,0:T(4,128)S(1)}, f32[8,4,128]{2,1,0:T(4,128)S(1)}, u32[]{:S(2)}, u32[]{:S(2)}) collective-permute-start(f32[8,4,128]{2,1,0:T(4,128)S(1)} %columns.2), channel_id=1, source_target_pairs={{0,4},{1,5},{2,6},{3,7},{4,0},{5,1},{6,2},{7,3},{8,12},{9,13},{10,... | collective-permute-start | bytes 49160 | tf_op jit(solution)/shard_map/ppermute | solution.py:27
  48.8 8.9 %collective-permute-start.12 = (f32[6,4,128]{2,1,0:T(4,128)S(1)}, f32[6,4,128]{2,1,0:T(4,128)S(1)}, u32[]{:S(2)}, u32[]{:S(2)}) collective-permute-start(f32[6,4,128]{2,1,0:T(4,128)S(1)} %slice_select_fusion), channel_id=1, source_target_pairs={{0,8},{1,9},{2,10},{3,11},{4,255},{5,254},{6,253},{7,252},{8,16},{... | collective-permute-start | bytes 36872 | tf_op jit(solution)/shard_map/ppermute | solution.py:27
  52.6 5.2 %collective-permute-start.13 = (f32[4,4,128]{2,1,0:T(4,128)S(1)}, f32[4,4,128]{2,1,0:T(4,128)S(1)}, u32[]{:S(2)}, u32[]{:S(2)}) collective-permute-start(f32[4,4,128]{2,1,0:T(4,128)S(1)} %slice_select_fusion.1), channel_id=1, source_target_pairs={{0,16},{1,17},{2,18},{3,19},{4,247},{5,246},{6,245},{7,244},{8,24}... | collective-permute-start | bytes 24584 | tf_op jit(solution)/shard_map/ppermute | solution.py:27
  53.8 4.0 %collective-permute-start.14 = (f32[2,4,128]{2,1,0:T(4,128)S(1)}, f32[2,4,128]{2,1,0:T(4,128)S(1)}, u32[]{:S(2)}, u32[]{:S(2)}) collective-permute-start(f32[2,4,128]{2,1,0:T(4,128)S(1)} %slice_select_fusion.3), channel_id=1, source_target_pairs={{0,24},{1,25},{2,26},{3,27},{4,239},{5,238},{6,237},{7,236},{8,35}... | collective-permute-start | bytes 12296 | tf_op jit(solution)/shard_map/ppermute | solution.py:27
  57.8 3.9 %collective-permute-start.15 = (f32[8,4,128]{2,1,0:T(4,128)S(1)}, f32[8,4,128]{2,1,0:T(4,128)S(1)}, u32[]{:S(2)}, u32[]{:S(2)}) collective-permute-start(f32[8,4,128]{2,1,0:T(4,128)S(1)} %log_add_fusion.2), channel_id=1, source_target_pairs={{0,4},{1,5},{2,6},{3,7},{4,0},{5,1},{6,2},{7,3},{8,12},{9,13},{10,... | collective-permute-start | bytes 49160 | tf_op jit(solution)/shard_map/ppermute | solution.py:27
  61.7 11.6 %copy-start = (bf16[1024,256]{1,0:T(8,128)(2,1)S(1)}, bf16[1024,256]{1,0:T(8,128)(2,1)}, u32[]{:S(2)}) copy-start(bf16[1024,256]{1,0:T(8,128)(2,1)} %points.1) | copy-start | bytes 1572868
  61.8 21.4 %copy-start.1 = (bf16[512,256]{1,0:T(8,128)(2,1)S(1)}, bf16[512,256]{1,0:T(8,128)(2,1)}, u32[]{:S(2)}) copy-start(bf16[512,256]{1,0:T(8,128)(2,1)} %src.1) | copy-start | bytes 786436
  64.1 3.5 %collective-permute-start.16 = (f32[1024]{0:T(1024)S(1)}, f32[1024]{0:T(1024)S(1)}, u32[]{:S(2)}, u32[]{:S(2)}) collective-permute-start(f32[1024]{0:T(1024)S(1)} %bitcast.41), channel_id=1, source_target_pairs={{0,5},{1,4},{2,7},{3,6},{4,1},{5,0},{6,3},{7,2},{8,13},{9,12},{10,... | collective-permute-start | bytes 12296 | tf_op jit(solution)/shard_map/ppermute | solution.py:27
  70.0 4.3 %collective-permute-start.19 = (f32[8,4,128]{2,1,0:T(4,128)S(1)}, f32[8,4,128]{2,1,0:T(4,128)S(1)}, u32[]{:S(2)}, u32[]{:S(2)}) collective-permute-start(f32[8,4,128]{2,1,0:T(4,128)S(1)} %columns.3), channel_id=1, source_target_pairs={{0,6},{1,7},{2,4},{3,5},{4,2},{5,3},{6,0},{7,1},{8,14},{9,15},{10,... | collective-permute-start | bytes 49160 | tf_op jit(solution)/shard_map/ppermute | solution.py:27
  72.9 3.5 %collective-permute-start.18 = (f32[8,4,128]{2,1,0:T(4,128)S(1)}, f32[8,4,128]{2,1,0:T(4,128)S(1)}, u32[]{:S(2)}, u32[]{:S(2)}) collective-permute-start(f32[8,4,128]{2,1,0:T(4,128)S(1)} %columns.3), channel_id=1, source_target_pairs={{0,2},{1,3},{2,0},{3,1},{4,6},{5,7},{6,4},{7,5},{8,10},{9,11},{10,... | collective-permute-start | bytes 49160 | tf_op jit(solution)/shard_map/ppermute | solution.py:27
  72.9 3.5 %collective-permute-start.17 = (f32[8,4,128]{2,1,0:T(4,128)S(1)}, f32[8,4,128]{2,1,0:T(4,128)S(1)}, u32[]{:S(2)}, u32[]{:S(2)}) collective-permute-start(f32[8,4,128]{2,1,0:T(4,128)S(1)} %columns.3), channel_id=1, source_target_pairs={{0,4},{1,5},{2,6},{3,7},{4,0},{5,1},{6,2},{7,3},{8,12},{9,13},{10,... | collective-permute-start | bytes 49160 | tf_op jit(solution)/shard_map/ppermute | solution.py:27
  76.4 6.8 %collective-permute-start.21 = (f32[4,128]{1,0:T(4,128)S(1)}, f32[4,128]{1,0:T(4,128)S(1)}, u32[]{:S(2)}, u32[]{:S(2)}) collective-permute-start(f32[4,128]{1,0:T(4,128)S(1)} %fusion.7), channel_id=1, source_target_pairs={{0,16},{1,17},{2,18},{3,19},{4,247},{5,246},{6,245},{7,244},{8,24}... | collective-permute-start | bytes 6152 | tf_op jit(solution)/shard_map/ppermute | solution.py:27
  79.3 4.6 %collective-permute-start.20 = (f32[2,4,128]{2,1,0:T(4,128)S(1)}, f32[2,4,128]{2,1,0:T(4,128)S(1)}, u32[]{:S(2)}, u32[]{:S(2)}) collective-permute-start(f32[2,4,128]{2,1,0:T(4,128)S(1)} %slice_select_fusion.2), channel_id=1, source_target_pairs={{0,8},{1,9},{2,10},{3,11},{4,255},{5,254},{6,253},{7,252},{8,16},{... | collective-permute-start | bytes 12296 | tf_op jit(solution)/shard_map/ppermute | solution.py:27
  83.9 5.8 %collective-permute-start.22 = (f32[2,4,128]{2,1,0:T(4,128)S(1)}, f32[2,4,128]{2,1,0:T(4,128)S(1)}, u32[]{:S(2)}, u32[]{:S(2)}) collective-permute-start(f32[2,4,128]{2,1,0:T(4,128)S(1)} %log_add_fusion.5), channel_id=1, source_target_pairs={{0,4},{1,5},{2,6},{3,7},{4,0},{5,1},{6,2},{7,3},{8,12},{9,13},{10,... | collective-permute-start | bytes 12296 | tf_op jit(solution)/shard_map/ppermute | solution.py:27
  89.8 2.8 %collective-permute-start.23 = (f32[512]{0:T(512)S(1)}, f32[512]{0:T(512)S(1)}, u32[]{:S(2)}, u32[]{:S(2)}) collective-permute-start(f32[512]{0:T(512)S(1)} %fusion.6), channel_id=1, source_target_pairs={{0,1},{1,0},{2,3},{3,2},{4,5},{5,4},{6,7},{7,6},{8,9},{9,8},{10,11... | collective-permute-start | bytes 6152 | tf_op jit(solution)/shard_map/ppermute | solution.py:27

commit v2 on v1

--- a/solution.py
+++ b/solution.py
@@ -105,6 +105,15 @@
         greatest = jnp.max(top, axis=0, keepdims=True)
         total = total_ref[q * 128 : (q + 1) * 128, :].T * jnp.exp(top - greatest)
         out[q : q + 1, :] = greatest + jnp.log(jnp.sum(total, axis=0, keepdims=True))
+
+
+def each_listed(flags, body):
+    def unit(u, _):
+        entry = flags[4 * BUFFERS + u]
+        body(lax.div(entry, 2), lax.rem(entry, 2))
+        return 0
+
+    lax.fori_loop(0, flags[3 * BUFFERS], unit, 0)
 
 
 def each_kept(flags, first, count, body):
@@ -212,14 +221,12 @@
         ]
         row_update(cross, number, bias, True, side, half, top_ref, total_ref)
 
-    each_kept(flags, 0, BUFFERS, body)
+    each_listed(flags, body)
     row_finish(top_ref, total_ref, out)
 
 
 def column_kernel(twice, flags, cross, weights, out, bias, top_ref, total_ref):
     out[...] = jnp.full(out.shape, NEG_FILL, jnp.float32)
-    top_ref[...] = jnp.full(top_ref.shape, NEG_FILL, jnp.float32)
-    total_ref[...] = jnp.zeros(total_ref.shape, jnp.float32)
     spread_rows(weights, bias)
     half = bias.shape[0] // 2
     pieces = cross.shape[2] // 128
@@ -239,31 +246,30 @@
                 tops.append(top)
             return tuple(tops), tuple(totals)
 
+        going = (side == 1) & (flags[number] != 0)
+        cuts = [slice(q * 128, (q + 1) * 128) for q in range(pieces)]
         state = (
-            tuple(top_ref[number, :, q * 128 : (q + 1) * 128] for q in range(pieces)),
-            tuple(total_ref[number, :, q * 128 : (q + 1) * 128] for q in range(pieces)),
+            tuple(jnp.where(going, top_ref[:, cut], NEG_FILL) for cut in cuts),
+            tuple(jnp.where(going, total_ref[:, cut], 0.0) for cut in cuts),
         )
         tops, totals = lax.fori_loop(0, half // step, chunk, state, unroll=COLUMN_UNROLL)
-        for q in range(pieces):
-            top_ref[number, :, q * 128 : (q + 1) * 128] = tops[q]
-            total_ref[number, :, q * 128 : (q + 1) * 128] = totals[q]
-
-    each_kept(flags, 0, BUFFERS, body)
-
-    def finish(number, _):
-        @pl.when((flags[number] | flags[BUFFERS + number]) != 0)
+        more = (side == 0) & (flags[BUFFERS + number] != 0)
+
+        @pl.when(more)
         def _():
-            for q in range(pieces):
-                top = top_ref[number, :, q * 128 : (q + 1) * 128]
+            for cut, top, total in zip(cuts, tops, totals):
+                top_ref[:, cut] = top
+                total_ref[:, cut] = total
+
+        @pl.when(jnp.logical_not(more))
+        def _():
+            slot = flags[2 * BUFFERS + number]
+            for q, (top, total) in enumerate(zip(tops, totals)):
                 greatest = jnp.max(top, axis=0, keepdims=True)
-                total = total_ref[number, :, q * 128 : (q + 1) * 128] * jnp.exp(top - greatest)
-                out[flags[2 * BUFFERS + number], q : q + 1, :] = greatest + jnp.log(
-                    jnp.sum(total, axis=0, keepdims=True)
-                )
-
-        return 0
-
-    lax.fori_loop(0, BUFFERS, finish, 0)
+                total = jnp.sum(total * jnp.exp(top - greatest), axis=0, keepdims=True)
+                out[slot, q : q + 1, :] = greatest + jnp.log(total)
+
+    each_listed(flags, body)
 
 
 WHOLE = pl.BlockSpec(memory_space=pltpu.VMEM)
@@ -358,7 +364,7 @@
         in_specs=[SCALARS] + [WHOLE] * 2,
         out_specs=WHOLE,
         scratch_shapes=[pltpu.VMEM((rows, 128), jnp.float32)]
-        + [pltpu.VMEM((BUFFERS, 8, columns), jnp.float32)] * 2,
+        + [pltpu.VMEM((8, columns), jnp.float32)] * 2,
         compiler_params=PARAMS,
         name="columns",
     )(flags, in_vmem(cross), weights)
@@ -385,9 +391,9 @@
 
     before = send(message, along(2, blocks), blocks)
     after = send(message, along(-2, blocks), blocks)
+    third = send(message, by_core(-3, 3, blocks), blocks)
     tied, mate = lax.optimization_barrier((message, mate))
-    third = send(tied, by_core(-3, 3, blocks), blocks)
-    beside = send(message, sibling, blocks)
+    beside = send(tied, sibling, blocks)
     sources = [own, mate]
     groups = ((0, 1), (2, 3, 4), (5, 6, 7))
 
@@ -401,7 +407,15 @@
         in_use = jnp.arange(row_names.shape[0], dtype=jnp.int32) < pair_count[source_block]
         return jnp.any((row_names[None, :] == names[:, None]) & in_use[None, :], axis=1).astype(jnp.int32)
 
-    flags = jnp.concatenate([kept(block), kept(block + 1 - 2 * core), slots])
+    kept_pairs = jnp.stack([kept(block), kept(block + 1 - 2 * core)])
+    entries = jnp.arange(2 * BUFFERS, dtype=jnp.int32)
+    listed = kept_pairs.T.reshape(-1)
+    rank = jnp.sum(jnp.where(entries[None, :] < entries[:, None], listed[None, :], 0), axis=1)
+    order = jnp.sum(
+        jnp.where((rank[:, None] == entries[None, :]) & (listed[:, None] != 0), entries[:, None], 0), axis=0
+    )
+    total = jnp.broadcast_to(jnp.sum(listed), (BUFFERS,))
+    flags = jnp.concatenate([kept_pairs.reshape(-1), slots, total, order])
 
     state = call_first(groups[0], True, False, flags, sources, [message, beside], ())
     state, arrived = lax.optimization_barrier((state, (before, after, third)))

time: 94.3 us -> 95.5 us (1.013); the launches traced: 93.2 us -> 95.5 us
  Pallas kernels: 13.2 us -> 20.8 us
  waiting for transfers between devices: 21.7 us -> 16.6 us
  starting transfers between devices: 51 us -> 48.5 us
  between operations: 0.87 us -> 2.18 us
    ppermute x24, waiting for transfers between devices: 21.7 us -> 16.6 us  [send(): return lax.ppermute(value, ('blk', 'rep'), pairs)]
    pallas_call x3, Pallas kernels: 4.91 us -> 8.46 us  [call_first(): pl.pallas_call(functools.partial(first_kernel, numbers, first, last), out...]
    ppermute x24, starting transfers between devices: 51 us -> 48.5 us  [send(): return lax.ppermute(value, ('blk', 'rep'), pairs)]
    pallas_call x2, Pallas kernels: 4.61 us -> 7.16 us  [call_columns(): pl.pallas_call(functools.partial(column_kernel, twice), out_shape=jax.Sha...]
    pallas_call x1, Pallas kernels: 2.36 us -> 3.89 us  [call_rows(): pl.pallas_call(row_kernel, out_shape=jax.ShapeDtypeStruct((rows // 128, 1...]
  transfers between devices with their start and end apart: 24 -> 24, of which waited for: 14 -> 13; matrix products, arithmetic and copies ran while one was open for 6% -> 7% of each run, Pallas kernels for 5% -> 8%
where the time goes in v2:
time: 95.5 us
  starting transfers between devices  48.5 us (51%)
  Pallas kernels  20.8 us (22%)
  waiting for transfers between devices  16.6 us (17%)
  other arithmetic  4.92 us (5%)
  local copies, waits for them, and re-layouts  2.57 us (3%)
  between operations  2.18 us (2%)
    ppermute x24, starting transfers between devices, send(): return lax.ppermute(value, ('blk', 'rep'), pairs)  48.5 us
    ppermute x24, waiting for transfers between devices, send(): return lax.ppermute(value, ('blk', 'rep'), pairs)  16.6 us
    pallas_call x3, Pallas kernels, call_first(): pl.pallas_call(functools.partial(first_kernel, numbers, first, last), out...  8.46 us
    pallas_call x2, Pallas kernels, call_columns(): pl.pallas_call(functools.partial(column_kernel, twice), out_shape=jax.Sha...  7.16 us
    pallas_call x1, Pallas kernels, call_rows(): pl.pallas_call(row_kernel, out_shape=jax.ShapeDtypeStruct((rows // 128, 1...  3.89 us
  transfers between devices with their start and end apart: 24, of which 13 were waited for; matrix products, arithmetic and copies ran while one was open for 7% of the time, Pallas kernels for 8%

profile of v2, /device:TPU:1, one launch (start us, length us, event | category | flops | bytes accessed | tf_op | source)
XLA Modules:
  0.0 95.5 jit_solution(11180575278624662770)
XLA Ops:
  0.6 3.1 %collective-permute-start = (bf16[512,256]{1,0:T(8,128)(2,1)}, bf16[512,256]{1,0:T(8,128)(2,1)S(1)}, u32[]{:S(2)}, u32[]{:S(2)}) collective-permute-start(bf16[512,256]{1,0:T(8,128)(2,1)} %src.1), channel_id=1, source_target_pairs={{0,5},{1,4},{2,7},{3,6},{4,1},{5,0},{6,3},{7,2},{8,13},{9,12},{10,... | collective-permute-start | bytes 786440 | tf_op jit(solution)/shard_map/ppermute | solution.py:27
  3.7 1.3 %message.1 = (bf16[528,256]{1,0:T(8,128)(2,1)S(1)}, bf16[512,256]{1,0:T(8,128)(2,1)S(1)}) custom-call(s32[1]{0:T(128)} %bitcast.5.half, bf16[1024,256]{1,0:T(8,128)(2,1)} %points.1, f32[8,128]{1,0:T(8,128)} %bitcast.67, f32[8,128]{1,0:T(8,128)} %bitcast.68, bf16[512,256]{1,0:T(8,128)(2,1)} %src.1), custom_call_target="tpu_custom_call" | custom-call | tf_op jit(solution)/shard_map/message/pallas_call | solution.py:290
  5.1 1.4 %collective-permute-start.2 = (bf16[528,256]{1,0:T(8,128)(2,1)S(1)}, bf16[528,256]{1,0:T(8,128)(2,1)S(1)}, u32[]{:S(2)}, u32[]{:S(2)}) collective-permute-start(bf16[528,256]{1,0:T(8,128)(2,1)S(1)} %get-tuple-element.27.refs_2_), channel_id=1, source_target_pairs={{0,8},{1,9},{2,10},{3,11},{4,12},{5,13},{6,14},{7,15},{8,16},{9,17... | collective-permute-start | bytes 811016 | tf_op jit(solution)/shard_map/ppermute | solution.py:27
  6.4 8.1 %collective-permute-start.3 = (bf16[528,256]{1,0:T(8,128)(2,1)S(1)}, bf16[528,256]{1,0:T(8,128)(2,1)S(1)}, u32[]{:S(2)}, u32[]{:S(2)}) collective-permute-start(bf16[528,256]{1,0:T(8,128)(2,1)S(1)} %get-tuple-element.27.refs_2_), channel_id=1, source_target_pairs={{0,251},{1,250},{2,249},{3,248},{4,255},{5,254},{6,253},{7,252},{8... | collective-permute-start | bytes 811016 | tf_op jit(solution)/shard_map/ppermute | solution.py:27
  14.5 0.0 collective-permute-start.4
  14.5 1.3 %fusion.11 = (s32[1]{0:T(128)}, s32[1]{0:T(128)}) fusion(s32[64]{0:T(128)} %param.15, s32[]{:T(128)S(6)} %select_n.129, s32[]{:T(128)S(6)} %select_n.124), kind=kLoop, calls=%fused_computation.63 | loop fusion | bytes 24 | tf_op jit(solution)/shard_map/dynamic_slice | solution.py:407
  15.9 0.6 iota_compare_fusion.2
  16.5 0.7 iota_compare_fusion.3
  17.2 1.0 %dynamic-slice_reduce_fusion.1 = (s32[7]{0:T(128)S(1)}, s32[7]{0:T(128)S(1)}) fusion(s32[64,7]{0,1:T(8,128)} %param.14, s32[]{:T(128)S(6)} %select_n.124, s32[]{:T(128)S(6)} %select_n.129), kind=kLoop, calls=%fused_computation.37 | loop fusion | bytes 120 | tf_op jit(solution)/shard_map/dynamic_slice | solution.py:406
  18.2 0.7 broadcast_select_fusion
  18.8 0.2 and_reduce_fusion.1
  19.0 0.1 copy.21
  19.1 0.1 broadcast_in_dim.25
  19.2 0.1 select_reduce_fusion.1
  19.3 0.0 collective-permute-done.refs_1_
  19.3 2.1 %collective-permute-start.1 = (bf16[528,256]{1,0:T(8,128)(2,1)S(1)}, bf16[528,256]{1,0:T(8,128)(2,1)S(1)}, u32[]{:S(2)}, u32[]{:S(2)}) collective-permute-start(bf16[528,256]{1,0:T(8,128)(2,1)S(1)} %get-tuple-element.27.refs_2_), channel_id=1, source_target_pairs={{0,4},{1,5},{2,6},{3,7},{4,0},{5,1},{6,2},{7,3},{8,12},{9,13},{10,... | collective-permute-start | bytes 811016 | tf_op jit(solution)/shard_map/ppermute | solution.py:27
  21.4 0.6 convert_reduce_fusion
  22.0 0.1 reshape.118
  23.4 0.1 select_reduce_fusion
  23.5 0.1 pad_add_fusion.flags
  23.6 3.1 %first_rows.3 = (f32[8,1024,512]{2,1,0:T(8,128)S(1)}, f32[8,4,128]{2,1,0:T(4,128)S(1)}, f32[1024,128]{1,0:T(8,128)S(1)}, f32[1024,128]{1,0:T(8,128)S(1)}) custom-call(s32[48]{0:T(128)S(1)} %pad_add_fusion.flags, bf16[512,256]{1,0:T(8,128)(2,1)S(1)} %get-tuple-element.24.refs_0_, bf16[512,256]{1,0:T(8,128)(2,1)S(1)} %collective-permute-done.refs_1_, ...), custom_call_target="tpu_custom_call" | custom-call | flops 536870912 | bytes 1048576 | tf_op jit(solution)/shard_map/first_rows/pallas_call | solution.py:325
  26.7 1.0 %collective-permute-done.2.refs_2_ = bf16[528,256]{1,0:T(8,128)(2,1)S(1)} collective-permute-done((bf16[528,256]{1,0:T(8,128)(2,1)S(1)}, bf16[528,256]{1,0:T(8,128)(2,1)S(1)}, u32[]{:S(2)}, u32[]{:S(2)}) %collective-permute-start.2) | collective-permute-done | bytes 270368 | tf_op jit(solution)/shard_map/ppermute | solution.py:27
  27.7 1.5 %collective-permute-done.3.refs_3_ = bf16[528,256]{1,0:T(8,128)(2,1)S(1)} collective-permute-done((bf16[528,256]{1,0:T(8,128)(2,1)S(1)}, bf16[528,256]{1,0:T(8,128)(2,1)S(1)}, u32[]{:S(2)}, u32[]{:S(2)}) %collective-permute-start.3) | collective-permute-done | bytes 270368 | tf_op jit(solution)/shard_map/ppermute | solution.py:27
  29.2 3.6 %collective-permute-start.5 = (bf16[528,256]{1,0:T(8,128)(2,1)S(1)}, bf16[528,256]{1,0:T(8,128)(2,1)S(1)}, u32[]{:S(2)}, u32[]{:S(2)}) collective-permute-start(bf16[528,256]{1,0:T(8,128)(2,1)S(1)} %collective-permute-done.2.refs_2_), channel_id=1, source_target_pairs={{0,4},{1,5},{2,6},{3,7},{4,0},{5,1},{6,2},{7,3},{8,12},{9,13},{10,... | collective-permute-start | bytes 811016 | tf_op jit(solution)/shard_map/ppermute | solution.py:27
  32.8 0.0 collective-permute-start.6
  32.8 0.5 collective-permute-start.7
  33.3 3.1 %first_rows.4 = (f32[8,1024,512]{2,1,0:T(8,128)S(1)}, f32[8,4,128]{2,1,0:T(4,128)S(1)}, f32[1024,128]{1,0:T(8,128)S(1)}, f32[1024,128]{1,0:T(8,128)S(1)}) custom-call(s32[48]{0:T(128)S(1)} %pad_add_fusion.flags, bf16[512,256]{1,0:T(8,128)(2,1)S(1)} %get-tuple-element.24.refs_0_, ...), custom_call_target="tpu_custom_call", output_to_operand_aliasing={{0}: (6, {}), {1}: (7, {}), {2}: (8, {}), {3}: (9, {})} | custom-call | flops 805306368 | bytes 1572864 | tf_op jit(solution)/shard_map/first_rows/pallas_call | solution.py:325
  36.5 2.3 %first_rows.5 = (f32[8,1024,512]{2,1,0:T(8,128)S(1)}, f32[8,4,128]{2,1,0:T(4,128)S(1)}, f32[1024,128]{1,0:T(8,128)S(1)}, f32[1024,128]{1,0:T(8,128)S(1)}, f32[8,128]{1,0:T(8,128)S(1)}) custom-call(s32[48]{0:T(128)S(1)} %pad_add_fusion.flags, ...), custom_call_target="tpu_custom_call", output_to_operand_aliasing={{0}: (6, {}), {1}: (7, {}), {2}: (8, {}), {3}: (9, {})} | custom-call | flops 805306368 | bytes 1572864 | tf_op jit(solution)/shard_map/first_rows/pallas_call | solution.py:325
  38.7 0.1 collective-permute-start.8
  38.9 3.1 %collective-permute-done.8 = f32[1536]{0:T(1024)S(1)} collective-permute-done((f32[1536]{0:T(1024)S(1)}, f32[1536]{0:T(1024)S(1)}, u32[]{:S(2)}, u32[]{:S(2)}) %collective-permute-start.8) | collective-permute-done | bytes 6176 | tf_op jit(solution)/shard_map/ppermute | solution.py:27
  41.9 3.4 %columns.2 = f32[8,4,128]{2,1,0:T(4,128)S(1)} custom-call(s32[48]{0:T(128)S(1)} %pad_add_fusion.flags, f32[8,1024,512]{2,1,0:T(8,128)S(1)} %get-tuple-element.43.cross, f32[8,128]{1,0:T(8,128)S(1)} %add_subtract_fusion.1.weights), custom_call_target="tpu_custom_call" | custom-call | tf_op jit(solution)/shard_map/columns/pallas_call | solution.py:361
  45.3 0.8 collective-permute-start.11
  46.1 1.6 %collective-permute-start.10 = (f32[8,4,128]{2,1,0:T(4,128)S(1)}, f32[8,4,128]{2,1,0:T(4,128)S(1)}, u32[]{:S(2)}, u32[]{:S(2)}) collective-permute-start(f32[8,4,128]{2,1,0:T(4,128)S(1)} %columns.2), channel_id=1, source_target_pairs={{0,2},{1,3},{2,0},{3,1},{4,6},{5,7},{6,4},{7,5},{8,10},{9,11},{10,... | collective-permute-start | bytes 49160 | tf_op jit(solution)/shard_map/ppermute | solution.py:27
  47.7 0.8 collective-permute-start.9
  48.5 1.1 %collective-permute-done.11 = f32[8,4,128]{2,1,0:T(4,128)S(1)} collective-permute-done((f32[8,4,128]{2,1,0:T(4,128)S(1)}, f32[8,4,128]{2,1,0:T(4,128)S(1)}, u32[]{:S(2)}, u32[]{:S(2)}) %collective-permute-start.11) | collective-permute-done | bytes 16416 | tf_op jit(solution)/shard_map/ppermute | solution.py:27
  49.6 0.1 collective-permute-done.10
  49.7 0.9 collective-permute-start.12
  50.6 4.4 %collective-permute-start.13 = (f32[4,4,128]{2,1,0:T(4,128)S(1)}, f32[4,4,128]{2,1,0:T(4,128)S(1)}, u32[]{:S(2)}, u32[]{:S(2)}) collective-permute-start(f32[4,4,128]{2,1,0:T(4,128)S(1)} %slice_select_fusion.1), channel_id=1, source_target_pairs={{0,16},{1,17},{2,18},{3,19},{4,247},{5,246},{6,245},{7,244},{8,24}... | collective-permute-start | bytes 24584 | tf_op jit(solution)/shard_map/ppermute | solution.py:27
  55.0 0.8 collective-permute-start.14
  55.8 3.2 %collective-permute-done.14 = f32[2,4,128]{2,1,0:T(4,128)S(1)} collective-permute-done((f32[2,4,128]{2,1,0:T(4,128)S(1)}, f32[2,4,128]{2,1,0:T(4,128)S(1)}, u32[]{:S(2)}, u32[]{:S(2)}) %collective-permute-start.14) | collective-permute-done | bytes 4128 | tf_op jit(solution)/shard_map/ppermute | solution.py:27
  59.0 2.4 %collective-permute-start.15 = (f32[8,4,128]{2,1,0:T(4,128)S(1)}, f32[8,4,128]{2,1,0:T(4,128)S(1)}, u32[]{:S(2)}, u32[]{:S(2)}) collective-permute-start(f32[8,4,128]{2,1,0:T(4,128)S(1)} %log_add_fusion.2), channel_id=1, source_target_pairs={{0,4},{1,5},{2,6},{3,7},{4,0},{5,1},{6,2},{7,3},{8,12},{9,13},{10,... | collective-permute-start | bytes 49160 | tf_op jit(solution)/shard_map/ppermute | solution.py:27
  61.5 0.8 collective-permute-done.15
  62.3 0.0 copy-start
  62.4 0.0 copy-start.1
  62.4 3.9 %rows.1 = f32[8,128]{1,0:T(8,128)S(1)} custom-call(s32[48]{0:T(128)S(1)} %pad_add_fusion.flags, f32[8,1024,512]{2,1,0:T(8,128)S(1)} %get-tuple-element.43.cross, f32[8,4,128]{2,1,0:T(4,128)S(1)} %get-tuple-element.44.masses, f32[8,4,128]{2,1,0:T(4,128)S(1)} %bitcast.44), custom_call_target="tpu_custom_call" | custom-call | tf_op jit(solution)/shard_map/rows/pallas_call | solution.py:348
  66.3 3.2 %collective-permute-start.16 = (f32[1024]{0:T(1024)S(1)}, f32[1024]{0:T(1024)S(1)}, u32[]{:S(2)}, u32[]{:S(2)}) collective-permute-start(f32[1024]{0:T(1024)S(1)} %bitcast.45), channel_id=1, source_target_pairs={{0,5},{1,4},{2,7},{3,6},{4,1},{5,0},{6,3},{7,2},{8,13},{9,12},{10,... | collective-permute-start | bytes 12296 | tf_op jit(solution)/shard_map/ppermute | solution.py:27
  69.4 1.3 %collective-permute-done.16 = f32[1024]{0:T(1024)S(1)} collective-permute-done((f32[1024]{0:T(1024)S(1)}, f32[1024]{0:T(1024)S(1)}, u32[]{:S(2)}, u32[]{:S(2)}) %collective-permute-start.16) | collective-permute-done | bytes 4128 | tf_op jit(solution)/shard_map/ppermute | solution.py:27
  70.8 3.8 %columns.3 = f32[8,4,128]{2,1,0:T(4,128)S(1)} custom-call(s32[48]{0:T(128)S(1)} %pad_add_fusion.flags, f32[8,1024,512]{2,1,0:T(8,128)S(1)} %get-tuple-element.43.cross, f32[8,128]{1,0:T(8,128)S(1)} %add_subtract_fusion.weights), custom_call_target="tpu_custom_call" | custom-call | tf_op jit(solution)/shard_map/columns/pallas_call | solution.py:361
  74.5 2.3 %collective-permute-start.19 = (f32[8,4,128]{2,1,0:T(4,128)S(1)}, f32[8,4,128]{2,1,0:T(4,128)S(1)}, u32[]{:S(2)}, u32[]{:S(2)}) collective-permute-start(f32[8,4,128]{2,1,0:T(4,128)S(1)} %columns.3), channel_id=1, source_target_pairs={{0,6},{1,7},{2,4},{3,5},{4,2},{5,3},{6,0},{7,1},{8,14},{9,15},{10,... | collective-permute-start | bytes 49160 | tf_op jit(solution)/shard_map/ppermute | solution.py:27
  76.8 0.3 collective-permute-start.18
  77.1 0.6 collective-permute-start.17
  77.7 0.2 multiply_reduce_fusion
  77.9 0.8 collective-permute-done.19
  78.7 1.6 %collective-permute-done.18 = f32[8,4,128]{2,1,0:T(4,128)S(1)} collective-permute-done((f32[8,4,128]{2,1,0:T(4,128)S(1)}, f32[8,4,128]{2,1,0:T(4,128)S(1)}, u32[]{:S(2)}, u32[]{:S(2)}) %collective-permute-start.18) | collective-permute-done | bytes 16416 | tf_op jit(solution)/shard_map/ppermute | solution.py:27
  80.4 1.4 %collective-permute-start.21 = (f32[4,128]{1,0:T(4,128)S(1)}, f32[4,128]{1,0:T(4,128)S(1)}, u32[]{:S(2)}, u32[]{:S(2)}) collective-permute-start(f32[4,128]{1,0:T(4,128)S(1)} %fusion.8), channel_id=1, source_target_pairs={{0,16},{1,17},{2,18},{3,19},{4,247},{5,246},{6,245},{7,244},{8,24}... | collective-permute-start | bytes 6152 | tf_op jit(solution)/shard_map/ppermute | solution.py:27
  81.8 1.7 %collective-permute-start.20 = (f32[2,4,128]{2,1,0:T(4,128)S(1)}, f32[2,4,128]{2,1,0:T(4,128)S(1)}, u32[]{:S(2)}, u32[]{:S(2)}) collective-permute-start(f32[2,4,128]{2,1,0:T(4,128)S(1)} %slice_select_fusion.2), channel_id=1, source_target_pairs={{0,8},{1,9},{2,10},{3,11},{4,255},{5,254},{6,253},{7,252},{8,16},{... | collective-permute-start | bytes 12296 | tf_op jit(solution)/shard_map/ppermute | solution.py:27
  83.5 0.1 multiply_reduce_fusion.1
  83.6 0.8 collective-permute-done.21
  84.4 6.8 %collective-permute-start.22 = (f32[2,4,128]{2,1,0:T(4,128)S(1)}, f32[2,4,128]{2,1,0:T(4,128)S(1)}, u32[]{:S(2)}, u32[]{:S(2)}) collective-permute-start(f32[2,4,128]{2,1,0:T(4,128)S(1)} %log_add_fusion.5), channel_id=1, source_target_pairs={{0,4},{1,5},{2,6},{3,7},{4,0},{5,1},{6,2},{7,3},{8,12},{9,13},{10,... | collective-permute-start | bytes 12296 | tf_op jit(solution)/shard_map/ppermute | solution.py:27
  91.2 0.8 collective-permute-done.22
  92.1 1.8 %collective-permute-start.23 = (f32[512]{0:T(512)S(1)}, f32[512]{0:T(512)S(1)}, u32[]{:S(2)}, u32[]{:S(2)}) collective-permute-start(f32[512]{0:T(512)S(1)} %fusion.7), channel_id=1, source_target_pairs={{0,1},{1,0},{2,3},{3,2},{4,5},{5,4},{6,7},{7,6},{8,9},{9,8},{10,11... | collective-permute-start | bytes 6152 | tf_op jit(solution)/shard_map/ppermute | solution.py:27
  93.9 0.6 multiply_subtract_fusion
  94.5 0.4 collective-permute-done.23
  94.9 0.6 fusion.2
  (35 shorter events, 0.3 us)
Async XLA Ops:
  0.6 18.7 %collective-permute-start = (bf16[512,256]{1,0:T(8,128)(2,1)}, bf16[512,256]{1,0:T(8,128)(2,1)S(1)}, u32[]{:S(2)}, u32[]{:S(2)}) collective-permute-start(bf16[512,256]{1,0:T(8,128)(2,1)} %src.1), channel_id=1, source_target_pairs={{0,5},{1,4},{2,7},{3,6},{4,1},{5,0},{6,3},{7,2},{8,13},{9,12},{10,... | collective-permute-start | bytes 786440 | tf_op jit(solution)/shard_map/ppermute | solution.py:27
  5.1 22.7 %collective-permute-start.2 = (bf16[528,256]{1,0:T(8,128)(2,1)S(1)}, bf16[528,256]{1,0:T(8,128)(2,1)S(1)}, u32[]{:S(2)}, u32[]{:S(2)}) collective-permute-start(bf16[528,256]{1,0:T(8,128)(2,1)S(1)} %get-tuple-element.27.refs_2_), channel_id=1, source_target_pairs={{0,8},{1,9},{2,10},{3,11},{4,12},{5,13},{6,14},{7,15},{8,16},{9,17... | collective-permute-start | bytes 811016 | tf_op jit(solution)/shard_map/ppermute | solution.py:27
  6.4 22.8 %collective-permute-start.3 = (bf16[528,256]{1,0:T(8,128)(2,1)S(1)}, bf16[528,256]{1,0:T(8,128)(2,1)S(1)}, u32[]{:S(2)}, u32[]{:S(2)}) collective-permute-start(bf16[528,256]{1,0:T(8,128)(2,1)S(1)} %get-tuple-element.27.refs_2_), channel_id=1, source_target_pairs={{0,251},{1,250},{2,249},{3,248},{4,255},{5,254},{6,253},{7,252},{8... | collective-permute-start | bytes 811016 | tf_op jit(solution)/shard_map/ppermute | solution.py:27
  14.5 14.7 %collective-permute-start.4 = (bf16[528,256]{1,0:T(8,128)(2,1)S(1)}, bf16[528,256]{1,0:T(8,128)(2,1)S(1)}, u32[]{:S(2)}, u32[]{:S(2)}) collective-permute-start(bf16[528,256]{1,0:T(8,128)(2,1)S(1)} %get-tuple-element.27.refs_2_), channel_id=1, source_target_pairs={{0,247},{1,246},{2,245},{3,244},{4,16},{5,17},{6,18},{7,19},{8,255... | collective-permute-start | bytes 811016 | tf_op jit(solution)/shard_map/ppermute | solution.py:27
  19.3 4.3 %collective-permute-start.1 = (bf16[528,256]{1,0:T(8,128)(2,1)S(1)}, bf16[528,256]{1,0:T(8,128)(2,1)S(1)}, u32[]{:S(2)}, u32[]{:S(2)}) collective-permute-start(bf16[528,256]{1,0:T(8,128)(2,1)S(1)} %get-tuple-element.27.refs_2_), channel_id=1, source_target_pairs={{0,4},{1,5},{2,6},{3,7},{4,0},{5,1},{6,2},{7,3},{8,12},{9,13},{10,... | collective-permute-start | bytes 811016 | tf_op jit(solution)/shard_map/ppermute | solution.py:27
  29.2 9.5 %copy-start.2 = (f32[512]{0:T(512)S(1)}, f32[512]{0:T(512)}, u32[]{:S(2)}) copy-start(f32[512]{0:T(512)} %param.10) | copy-start | bytes 6148
  29.2 7.2 %collective-permute-start.5 = (bf16[528,256]{1,0:T(8,128)(2,1)S(1)}, bf16[528,256]{1,0:T(8,128)(2,1)S(1)}, u32[]{:S(2)}, u32[]{:S(2)}) collective-permute-start(bf16[528,256]{1,0:T(8,128)(2,1)S(1)} %collective-permute-done.2.refs_2_), channel_id=1, source_target_pairs={{0,4},{1,5},{2,6},{3,7},{4,0},{5,1},{6,2},{7,3},{8,12},{9,13},{10,... | collective-permute-start | bytes 811016 | tf_op jit(solution)/shard_map/ppermute | solution.py:27
  32.8 3.6 %collective-permute-start.6 = (bf16[528,256]{1,0:T(8,128)(2,1)S(1)}, bf16[528,256]{1,0:T(8,128)(2,1)S(1)}, u32[]{:S(2)}, u32[]{:S(2)}) collective-permute-start(bf16[528,256]{1,0:T(8,128)(2,1)S(1)} %collective-permute-done.3.refs_3_), channel_id=1, source_target_pairs={{0,4},{1,5},{2,6},{3,7},{4,0},{5,1},{6,2},{7,3},{8,12},{9,13},{10,... | collective-permute-start | bytes 811016 | tf_op jit(solution)/shard_map/ppermute | solution.py:27
  32.8 3.6 %collective-permute-start.7 = (bf16[528,256]{1,0:T(8,128)(2,1)S(1)}, bf16[528,256]{1,0:T(8,128)(2,1)S(1)}, u32[]{:S(2)}, u32[]{:S(2)}) collective-permute-start(bf16[528,256]{1,0:T(8,128)(2,1)S(1)} %collective-permute-done.4.refs_4_), channel_id=1, source_target_pairs={{0,4},{1,5},{2,6},{3,7},{4,0},{5,1},{6,2},{7,3},{8,12},{9,13},{10,... | collective-permute-start | bytes 811016 | tf_op jit(solution)/shard_map/ppermute | solution.py:27
  38.7 3.2 %collective-permute-start.8 = (f32[1536]{0:T(1024)S(1)}, f32[1536]{0:T(1024)S(1)}, u32[]{:S(2)}, u32[]{:S(2)}) collective-permute-start(f32[1536]{0:T(1024)S(1)} %pad_maximum_fusion), channel_id=1, source_target_pairs={{0,5},{1,4},{2,7},{3,6},{4,1},{5,0},{6,3},{7,2},{8,13},{9,12},{10,... | collective-permute-start | bytes 18440 | tf_op jit(solution)/shard_map/ppermute | solution.py:27
  45.3 4.2 %collective-permute-start.11 = (f32[8,4,128]{2,1,0:T(4,128)S(1)}, f32[8,4,128]{2,1,0:T(4,128)S(1)}, u32[]{:S(2)}, u32[]{:S(2)}) collective-permute-start(f32[8,4,128]{2,1,0:T(4,128)S(1)} %columns.2), channel_id=1, source_target_pairs={{0,6},{1,7},{2,4},{3,5},{4,2},{5,3},{6,0},{7,1},{8,14},{9,15},{10,... | collective-permute-start | bytes 49160 | tf_op jit(solution)/shard_map/ppermute | solution.py:27
  46.1 3.6 %collective-permute-start.10 = (f32[8,4,128]{2,1,0:T(4,128)S(1)}, f32[8,4,128]{2,1,0:T(4,128)S(1)}, u32[]{:S(2)}, u32[]{:S(2)}) collective-permute-start(f32[8,4,128]{2,1,0:T(4,128)S(1)} %columns.2), channel_id=1, source_target_pairs={{0,2},{1,3},{2,0},{3,1},{4,6},{5,7},{6,4},{7,5},{8,10},{9,11},{10,... | collective-permute-start | bytes 49160 | tf_op jit(solution)/shard_map/ppermute | solution.py:27
  47.7 2.0 %collective-permute-start.9 = (f32[8,4,128]{2,1,0:T(4,128)S(1)}, f32[8,4,128]{2,1,0:T(4,128)S(1)}, u32[]{:S(2)}, u32[]{:S(2)}) collective-permute-start(f32[8,4,128]{2,1,0:T(4,128)S(1)} %columns.2), channel_id=1, source_target_pairs={{0,4},{1,5},{2,6},{3,7},{4,0},{5,1},{6,2},{7,3},{8,12},{9,13},{10,... | collective-permute-start | bytes 49160 | tf_op jit(solution)/shard_map/ppermute | solution.py:27
  49.7 9.3 %collective-permute-start.12 = (f32[6,4,128]{2,1,0:T(4,128)S(1)}, f32[6,4,128]{2,1,0:T(4,128)S(1)}, u32[]{:S(2)}, u32[]{:S(2)}) collective-permute-start(f32[6,4,128]{2,1,0:T(4,128)S(1)} %slice_select_fusion), channel_id=1, source_target_pairs={{0,8},{1,9},{2,10},{3,11},{4,255},{5,254},{6,253},{7,252},{8,16},{... | collective-permute-start | bytes 36872 | tf_op jit(solution)/shard_map/ppermute | solution.py:27
  50.6 8.4 %collective-permute-start.13 = (f32[4,4,128]{2,1,0:T(4,128)S(1)}, f32[4,4,128]{2,1,0:T(4,128)S(1)}, u32[]{:S(2)}, u32[]{:S(2)}) collective-permute-start(f32[4,4,128]{2,1,0:T(4,128)S(1)} %slice_select_fusion.1), channel_id=1, source_target_pairs={{0,16},{1,17},{2,18},{3,19},{4,247},{5,246},{6,245},{7,244},{8,24}... | collective-permute-start | bytes 24584 | tf_op jit(solution)/shard_map/ppermute | solution.py:27
  55.0 4.0 %collective-permute-start.14 = (f32[2,4,128]{2,1,0:T(4,128)S(1)}, f32[2,4,128]{2,1,0:T(4,128)S(1)}, u32[]{:S(2)}, u32[]{:S(2)}) collective-permute-start(f32[2,4,128]{2,1,0:T(4,128)S(1)} %slice_select_fusion.3), channel_id=1, source_target_pairs={{0,24},{1,25},{2,26},{3,27},{4,239},{5,238},{6,237},{7,236},{8,35}... | collective-permute-start | bytes 12296 | tf_op jit(solution)/shard_map/ppermute | solution.py:27
  59.0 3.3 %collective-permute-start.15 = (f32[8,4,128]{2,1,0:T(4,128)S(1)}, f32[8,4,128]{2,1,0:T(4,128)S(1)}, u32[]{:S(2)}, u32[]{:S(2)}) collective-permute-start(f32[8,4,128]{2,1,0:T(4,128)S(1)} %log_add_fusion.2), channel_id=1, source_target_pairs={{0,4},{1,5},{2,6},{3,7},{4,0},{5,1},{6,2},{7,3},{8,12},{9,13},{10,... | collective-permute-start | bytes 49160 | tf_op jit(solution)/shard_map/ppermute | solution.py:27
  62.3 15.3 %copy-start = (bf16[1024,256]{1,0:T(8,128)(2,1)S(1)}, bf16[1024,256]{1,0:T(8,128)(2,1)}, u32[]{:S(2)}) copy-start(bf16[1024,256]{1,0:T(8,128)(2,1)} %points.1) | copy-start | bytes 1572868
  62.4 21.1 %copy-start.1 = (bf16[512,256]{1,0:T(8,128)(2,1)S(1)}, bf16[512,256]{1,0:T(8,128)(2,1)}, u32[]{:S(2)}) copy-start(bf16[512,256]{1,0:T(8,128)(2,1)} %src.1) | copy-start | bytes 786436
  66.3 4.5 %collective-permute-start.16 = (f32[1024]{0:T(1024)S(1)}, f32[1024]{0:T(1024)S(1)}, u32[]{:S(2)}, u32[]{:S(2)}) collective-permute-start(f32[1024]{0:T(1024)S(1)} %bitcast.45), channel_id=1, source_target_pairs={{0,5},{1,4},{2,7},{3,6},{4,1},{5,0},{6,3},{7,2},{8,13},{9,12},{10,... | collective-permute-start | bytes 12296 | tf_op jit(solution)/shard_map/ppermute | solution.py:27
  74.5 4.2 %collective-permute-start.19 = (f32[8,4,128]{2,1,0:T(4,128)S(1)}, f32[8,4,128]{2,1,0:T(4,128)S(1)}, u32[]{:S(2)}, u32[]{:S(2)}) collective-permute-start(f32[8,4,128]{2,1,0:T(4,128)S(1)} %columns.3), channel_id=1, source_target_pairs={{0,6},{1,7},{2,4},{3,5},{4,2},{5,3},{6,0},{7,1},{8,14},{9,15},{10,... | collective-permute-start | bytes 49160 | tf_op jit(solution)/shard_map/ppermute | solution.py:27
  76.8 3.5 %collective-permute-start.18 = (f32[8,4,128]{2,1,0:T(4,128)S(1)}, f32[8,4,128]{2,1,0:T(4,128)S(1)}, u32[]{:S(2)}, u32[]{:S(2)}) collective-permute-start(f32[8,4,128]{2,1,0:T(4,128)S(1)} %columns.3), channel_id=1, source_target_pairs={{0,2},{1,3},{2,0},{3,1},{4,6},{5,7},{6,4},{7,5},{8,10},{9,11},{10,... | collective-permute-start | bytes 49160 | tf_op jit(solution)/shard_map/ppermute | solution.py:27
  77.1 3.2 %collective-permute-start.17 = (f32[8,4,128]{2,1,0:T(4,128)S(1)}, f32[8,4,128]{2,1,0:T(4,128)S(1)}, u32[]{:S(2)}, u32[]{:S(2)}) collective-permute-start(f32[8,4,128]{2,1,0:T(4,128)S(1)} %columns.3), channel_id=1, source_target_pairs={{0,4},{1,5},{2,6},{3,7},{4,0},{5,1},{6,2},{7,3},{8,12},{9,13},{10,... | collective-permute-start | bytes 49160 | tf_op jit(solution)/shard_map/ppermute | solution.py:27
  80.4 4.0 %collective-permute-start.21 = (f32[4,128]{1,0:T(4,128)S(1)}, f32[4,128]{1,0:T(4,128)S(1)}, u32[]{:S(2)}, u32[]{:S(2)}) collective-permute-start(f32[4,128]{1,0:T(4,128)S(1)} %fusion.8), channel_id=1, source_target_pairs={{0,16},{1,17},{2,18},{3,19},{4,247},{5,246},{6,245},{7,244},{8,24}... | collective-permute-start | bytes 6152 | tf_op jit(solution)/shard_map/ppermute | solution.py:27
  81.8 2.6 %collective-permute-start.20 = (f32[2,4,128]{2,1,0:T(4,128)S(1)}, f32[2,4,128]{2,1,0:T(4,128)S(1)}, u32[]{:S(2)}, u32[]{:S(2)}) collective-permute-start(f32[2,4,128]{2,1,0:T(4,128)S(1)} %slice_select_fusion.2), channel_id=1, source_target_pairs={{0,8},{1,9},{2,10},{3,11},{4,255},{5,254},{6,253},{7,252},{8,16},{... | collective-permute-start | bytes 12296 | tf_op jit(solution)/shard_map/ppermute | solution.py:27
  84.4 7.6 %collective-permute-start.22 = (f32[2,4,128]{2,1,0:T(4,128)S(1)}, f32[2,4,128]{2,1,0:T(4,128)S(1)}, u32[]{:S(2)}, u32[]{:S(2)}) collective-permute-start(f32[2,4,128]{2,1,0:T(4,128)S(1)} %log_add_fusion.5), channel_id=1, source_target_pairs={{0,4},{1,5},{2,6},{3,7},{4,0},{5,1},{6,2},{7,3},{8,12},{9,13},{10,... | collective-permute-start | bytes 12296 | tf_op jit(solution)/shard_map/ppermute | solution.py:27
  92.1 2.8 %collective-permute-start.23 = (f32[512]{0:T(512)S(1)}, f32[512]{0:T(512)S(1)}, u32[]{:S(2)}, u32[]{:S(2)}) collective-permute-start(f32[512]{0:T(512)S(1)} %fusion.7), channel_id=1, source_target_pairs={{0,1},{1,0},{2,3},{3,2},{4,5},{5,4},{6,7},{7,6},{8,9},{9,8},{10,11... | collective-permute-start | bytes 6152 | tf_op jit(solution)/shard_map/ppermute | solution.py:27

commit v3 on v2

--- a/solution.py
+++ b/solution.py
@@ -384,10 +384,10 @@
     width = tgt_points.shape[0]
     columns = width // 2
 
-    mate = send(src_points, diagonal, blocks)
     message, own = call_message(
         1.0 / EPS_START, half_index, tgt_points, tgt_log_mass, initial_potential, src_points
     )
+    mate = send(src_points, diagonal, blocks)
 
     before = send(message, along(2, blocks), blocks)
     after = send(message, along(-2, blocks), blocks)
@@ -461,10 +461,14 @@
             far = send(far, by_core(4, -4, blocks), blocks)
             empty = jnp.full_like(far, NEG_FILL)
             far = jnp.where(forward, jnp.stack([far, empty]), jnp.stack([empty, far]))
-            side = log_merge(near, far)
-            column_sums = log_merge(chip[3:5], side, send(side, sibling, blocks))
-            mine = jnp.where(core == 0, column_sums[0], column_sums[1]).reshape(columns)
-            other = send(mine, lambda b, r: (b, r ^ 1), blocks)
+            side = log_merge(jnp.where(forward, chip[3:5], jnp.full_like(near, NEG_FILL)), near, far)
+            over_core = send(side, sibling, blocks)
+            over_half = send(side, lambda b, r: (b, r ^ 1), blocks)
+            over_both = send(side, diagonal, blocks)
+            mine = log_merge(side, over_core)
+            other = log_merge(over_half, over_both)
+            mine = jnp.where(core == 0, mine[0], mine[1]).reshape(columns)
+            other = jnp.where(core == 0, other[0], other[1]).reshape(columns)
             whole = jnp.where(
                 half_index == 0, jnp.concatenate([mine, other]), jnp.concatenate([other, mine])
             )

time: 95.5 us -> 94.8 us (level); the launches traced: 95.5 us -> 93.3 us
  Pallas kernels: 20.8 us -> 10.7 us
  waiting for transfers between devices: 16.6 us -> 20.7 us
  starting transfers between devices: 48.5 us -> 52.3 us
    pallas_call x3, Pallas kernels: 8.46 us -> 4.32 us  [call_first(): pl.pallas_call(functools.partial(first_kernel, numbers, first, last), out...]
    ppermute x24 -> x25, waiting for transfers between devices: 16.6 us -> 20.7 us  [send(): return lax.ppermute(value, ('blk', 'rep'), pairs)]
    pallas_call x2, Pallas kernels: 7.16 us -> 3.22 us  [call_columns(): pl.pallas_call(functools.partial(column_kernel, twice), out_shape=jax.Sha...]
    ppermute x24 -> x25, starting transfers between devices: 48.5 us -> 52.3 us  [send(): return lax.ppermute(value, ('blk', 'rep'), pairs)]
    pallas_call x1, Pallas kernels: 3.89 us -> 1.84 us  [call_rows(): pl.pallas_call(row_kernel, out_shape=jax.ShapeDtypeStruct((rows // 128, 1...]
  transfers between devices with their start and end apart: 24 -> 25, of which waited for: 13 -> 14; matrix products, arithmetic and copies ran while one was open for 7% -> 7% of each run, Pallas kernels for 8% -> 4%
where the time goes in v3:
time: 94.8 us; the launch traced here: 93.3 us
  starting transfers between devices  52.3 us (55%)
  waiting for transfers between devices  20.7 us (22%)
  Pallas kernels  10.7 us (11%)
  other arithmetic  4.93 us (5%)
  local copies, waits for them, and re-layouts  2.57 us (3%)
  between operations  2.17 us (2%)
    ppermute x25, starting transfers between devices, send(): return lax.ppermute(value, ('blk', 'rep'), pairs)  52.3 us
    ppermute x25, waiting for transfers between devices, send(): return lax.ppermute(value, ('blk', 'rep'), pairs)  20.7 us
    pallas_call x3, Pallas kernels, call_first(): pl.pallas_call(functools.partial(first_kernel, numbers, first, last), out...  4.32 us
    pallas_call x2, Pallas kernels, call_columns(): pl.pallas_call(functools.partial(column_kernel, twice), out_shape=jax.Sha...  3.22 us
  transfers between devices with their start and end apart: 25, of which 14 were waited for; matrix products, arithmetic and copies ran while one was open for 7% of the time, Pallas kernels for 4%

profile of v3, /device:TPU:1, one launch (start us, length us, event | category | flops | bytes accessed | tf_op | source)
XLA Modules:
  0.0 93.3 jit_solution(14388958370582359578)
XLA Ops:
  0.6 3.1 %collective-permute-start = (bf16[512,256]{1,0:T(8,128)(2,1)}, bf16[512,256]{1,0:T(8,128)(2,1)S(1)}, u32[]{:S(2)}, u32[]{:S(2)}) collective-permute-start(bf16[512,256]{1,0:T(8,128)(2,1)} %src.1), channel_id=1, source_target_pairs={{0,5},{1,4},{2,7},{3,6},{4,1},{5,0},{6,3},{7,2},{8,13},{9,12},{10,... | collective-permute-start | bytes 786440 | tf_op jit(solution)/shard_map/ppermute | solution.py:27
  3.7 1.3 %message.1 = (bf16[528,256]{1,0:T(8,128)(2,1)S(1)}, bf16[512,256]{1,0:T(8,128)(2,1)S(1)}) custom-call(s32[1]{0:T(128)} %bitcast.5.half, bf16[1024,256]{1,0:T(8,128)(2,1)} %points.1, f32[8,128]{1,0:T(8,128)} %bitcast.76, f32[8,128]{1,0:T(8,128)} %bitcast.77, bf16[512,256]{1,0:T(8,128)(2,1)} %src.1), custom_call_target="tpu_custom_call" | custom-call | tf_op jit(solution)/shard_map/message/pallas_call | solution.py:290
  5.1 1.4 %collective-permute-start.2 = (bf16[528,256]{1,0:T(8,128)(2,1)S(1)}, bf16[528,256]{1,0:T(8,128)(2,1)S(1)}, u32[]{:S(2)}, u32[]{:S(2)}) collective-permute-start(bf16[528,256]{1,0:T(8,128)(2,1)S(1)} %get-tuple-element.27.refs_2_), channel_id=1, source_target_pairs={{0,8},{1,9},{2,10},{3,11},{4,12},{5,13},{6,14},{7,15},{8,16},{9,17... | collective-permute-start | bytes 811016 | tf_op jit(solution)/shard_map/ppermute | solution.py:27
  6.4 8.1 %collective-permute-start.3 = (bf16[528,256]{1,0:T(8,128)(2,1)S(1)}, bf16[528,256]{1,0:T(8,128)(2,1)S(1)}, u32[]{:S(2)}, u32[]{:S(2)}) collective-permute-start(bf16[528,256]{1,0:T(8,128)(2,1)S(1)} %get-tuple-element.27.refs_2_), channel_id=1, source_target_pairs={{0,251},{1,250},{2,249},{3,248},{4,255},{5,254},{6,253},{7,252},{8... | collective-permute-start | bytes 811016 | tf_op jit(solution)/shard_map/ppermute | solution.py:27
  14.5 0.0 collective-permute-start.4
  14.5 1.3 %fusion.13 = (s32[1]{0:T(128)}, s32[1]{0:T(128)}) fusion(s32[64]{0:T(128)} %param.15, s32[]{:T(128)S(6)} %select_n.141, s32[]{:T(128)S(6)} %select_n.136), kind=kLoop, calls=%fused_computation.69 | loop fusion | bytes 24 | tf_op jit(solution)/shard_map/dynamic_slice | solution.py:407
  15.9 0.6 iota_compare_fusion.2
  16.5 0.7 iota_compare_fusion.3
  17.2 1.0 %dynamic-slice_reduce_fusion.1 = (s32[7]{0:T(128)S(1)}, s32[7]{0:T(128)S(1)}) fusion(s32[64,7]{0,1:T(8,128)} %param.14, s32[]{:T(128)S(6)} %select_n.136, s32[]{:T(128)S(6)} %select_n.141), kind=kLoop, calls=%fused_computation.41 | loop fusion | bytes 120 | tf_op jit(solution)/shard_map/dynamic_slice | solution.py:406
  18.2 0.7 broadcast_select_fusion
  18.8 0.2 and_reduce_fusion.1
  19.0 0.1 copy.21
  19.1 0.1 broadcast_in_dim.38
  19.2 0.1 select_reduce_fusion.1
  19.3 2.1 %collective-permute-start.1 = (bf16[528,256]{1,0:T(8,128)(2,1)S(1)}, bf16[528,256]{1,0:T(8,128)(2,1)S(1)}, u32[]{:S(2)}, u32[]{:S(2)}) collective-permute-start(bf16[528,256]{1,0:T(8,128)(2,1)S(1)} %get-tuple-element.27.refs_2_), channel_id=1, source_target_pairs={{0,4},{1,5},{2,6},{3,7},{4,0},{5,1},{6,2},{7,3},{8,12},{9,13},{10,... | collective-permute-start | bytes 811016 | tf_op jit(solution)/shard_map/ppermute | solution.py:27
  21.4 0.6 convert_reduce_fusion
  22.0 0.1 reshape.123
  23.4 0.1 select_reduce_fusion
  23.5 0.1 pad_add_fusion.flags
  23.6 1.9 %first_rows.3 = (f32[8,1024,512]{2,1,0:T(8,128)S(1)}, f32[8,4,128]{2,1,0:T(4,128)S(1)}, f32[1024,128]{1,0:T(8,128)S(1)}, f32[1024,128]{1,0:T(8,128)S(1)}) custom-call(s32[48]{0:T(128)S(1)} %pad_add_fusion.flags, bf16[512,256]{1,0:T(8,128)(2,1)S(1)} %get-tuple-element.24.refs_0_, bf16[512,256]{1,0:T(8,128)(2,1)S(1)} %collective-permute-done.refs_1_, ...), custom_call_target="tpu_custom_call" | custom-call | flops 536870912 | bytes 1048576 | tf_op jit(solution)/shard_map/first_rows/pallas_call | solution.py:325
  25.5 2.2 %collective-permute-done.2.refs_2_ = bf16[528,256]{1,0:T(8,128)(2,1)S(1)} collective-permute-done((bf16[528,256]{1,0:T(8,128)(2,1)S(1)}, bf16[528,256]{1,0:T(8,128)(2,1)S(1)}, u32[]{:S(2)}, u32[]{:S(2)}) %collective-permute-start.2) | collective-permute-done | bytes 270368 | tf_op jit(solution)/shard_map/ppermute | solution.py:27
  27.7 1.5 %collective-permute-done.3.refs_3_ = bf16[528,256]{1,0:T(8,128)(2,1)S(1)} collective-permute-done((bf16[528,256]{1,0:T(8,128)(2,1)S(1)}, bf16[528,256]{1,0:T(8,128)(2,1)S(1)}, u32[]{:S(2)}, u32[]{:S(2)}) %collective-permute-start.3) | collective-permute-done | bytes 270368 | tf_op jit(solution)/shard_map/ppermute | solution.py:27
  29.2 3.6 %collective-permute-start.5 = (bf16[528,256]{1,0:T(8,128)(2,1)S(1)}, bf16[528,256]{1,0:T(8,128)(2,1)S(1)}, u32[]{:S(2)}, u32[]{:S(2)}) collective-permute-start(bf16[528,256]{1,0:T(8,128)(2,1)S(1)} %collective-permute-done.2.refs_2_), channel_id=1, source_target_pairs={{0,4},{1,5},{2,6},{3,7},{4,0},{5,1},{6,2},{7,3},{8,12},{9,13},{10,... | collective-permute-start | bytes 811016 | tf_op jit(solution)/shard_map/ppermute | solution.py:27
  32.8 0.5 collective-permute-start.7
  33.3 0.7 first_rows.4
  34.1 0.3 collective-permute-done.6.refs_3_
  34.4 0.4 collective-permute-done.7.refs_4_
  34.8 1.7 %first_rows.5 = (f32[8,1024,512]{2,1,0:T(8,128)S(1)}, f32[8,4,128]{2,1,0:T(4,128)S(1)}, f32[1024,128]{1,0:T(8,128)S(1)}, f32[1024,128]{1,0:T(8,128)S(1)}, f32[8,128]{1,0:T(8,128)S(1)}) custom-call(s32[48]{0:T(128)S(1)} %pad_add_fusion.flags, ...), custom_call_target="tpu_custom_call", output_to_operand_aliasing={{0}: (6, {}), {1}: (7, {}), {2}: (8, {}), {3}: (9, {})} | custom-call | flops 805306368 | bytes 1572864 | tf_op jit(solution)/shard_map/first_rows/pallas_call | solution.py:325
  36.5 0.1 collective-permute-start.8
  36.6 3.1 %collective-permute-done.8 = f32[1536]{0:T(1024)S(1)} collective-permute-done((f32[1536]{0:T(1024)S(1)}, f32[1536]{0:T(1024)S(1)}, u32[]{:S(2)}, u32[]{:S(2)}) %collective-permute-start.8) | collective-permute-done | bytes 6176 | tf_op jit(solution)/shard_map/ppermute | solution.py:27
  39.7 1.6 %columns.2 = f32[8,4,128]{2,1,0:T(4,128)S(1)} custom-call(s32[48]{0:T(128)S(1)} %pad_add_fusion.flags, f32[8,1024,512]{2,1,0:T(8,128)S(1)} %get-tuple-element.43.cross, f32[8,128]{1,0:T(8,128)S(1)} %add_subtract_fusion.1.weights), custom_call_target="tpu_custom_call" | custom-call | tf_op jit(solution)/shard_map/columns/pallas_call | solution.py:361
  41.2 0.6 collective-permute-start.11
  41.8 1.6 %collective-permute-start.10 = (f32[8,4,128]{2,1,0:T(4,128)S(1)}, f32[8,4,128]{2,1,0:T(4,128)S(1)}, u32[]{:S(2)}, u32[]{:S(2)}) collective-permute-start(f32[8,4,128]{2,1,0:T(4,128)S(1)} %columns.2), channel_id=1, source_target_pairs={{0,2},{1,3},{2,0},{3,1},{4,6},{5,7},{6,4},{7,5},{8,10},{9,11},{10,... | collective-permute-start | bytes 49160 | tf_op jit(solution)/shard_map/ppermute | solution.py:27
  43.3 1.0 %collective-permute-start.9 = (f32[8,4,128]{2,1,0:T(4,128)S(1)}, f32[8,4,128]{2,1,0:T(4,128)S(1)}, u32[]{:S(2)}, u32[]{:S(2)}) collective-permute-start(f32[8,4,128]{2,1,0:T(4,128)S(1)} %columns.2), channel_id=1, source_target_pairs={{0,4},{1,5},{2,6},{3,7},{4,0},{5,1},{6,2},{7,3},{8,12},{9,13},{10,... | collective-permute-start | bytes 49160 | tf_op jit(solution)/shard_map/ppermute | solution.py:27
  44.3 1.2 %collective-permute-done.11 = f32[8,4,128]{2,1,0:T(4,128)S(1)} collective-permute-done((f32[8,4,128]{2,1,0:T(4,128)S(1)}, f32[8,4,128]{2,1,0:T(4,128)S(1)}, u32[]{:S(2)}, u32[]{:S(2)}) %collective-permute-start.11) | collective-permute-done | bytes 16416 | tf_op jit(solution)/shard_map/ppermute | solution.py:27
  45.6 5.3 %collective-permute-start.12 = (f32[6,4,128]{2,1,0:T(4,128)S(1)}, f32[6,4,128]{2,1,0:T(4,128)S(1)}, u32[]{:S(2)}, u32[]{:S(2)}) collective-permute-start(f32[6,4,128]{2,1,0:T(4,128)S(1)} %slice_select_fusion), channel_id=1, source_target_pairs={{0,8},{1,9},{2,10},{3,11},{4,255},{5,254},{6,253},{7,252},{8,16},{... | collective-permute-start | bytes 36872 | tf_op jit(solution)/shard_map/ppermute | solution.py:27
  51.0 3.3 %collective-permute-start.13 = (f32[4,4,128]{2,1,0:T(4,128)S(1)}, f32[4,4,128]{2,1,0:T(4,128)S(1)}, u32[]{:S(2)}, u32[]{:S(2)}) collective-permute-start(f32[4,4,128]{2,1,0:T(4,128)S(1)} %slice_select_fusion.1), channel_id=1, source_target_pairs={{0,16},{1,17},{2,18},{3,19},{4,247},{5,246},{6,245},{7,244},{8,24}... | collective-permute-start | bytes 24584 | tf_op jit(solution)/shard_map/ppermute | solution.py:27
  54.3 0.7 collective-permute-start.14
  55.0 3.2 %collective-permute-done.14 = f32[2,4,128]{2,1,0:T(4,128)S(1)} collective-permute-done((f32[2,4,128]{2,1,0:T(4,128)S(1)}, f32[2,4,128]{2,1,0:T(4,128)S(1)}, u32[]{:S(2)}, u32[]{:S(2)}) %collective-permute-start.14) | collective-permute-done | bytes 4128 | tf_op jit(solution)/shard_map/ppermute | solution.py:27
  58.3 1.6 %collective-permute-start.15 = (f32[8,4,128]{2,1,0:T(4,128)S(1)}, f32[8,4,128]{2,1,0:T(4,128)S(1)}, u32[]{:S(2)}, u32[]{:S(2)}) collective-permute-start(f32[8,4,128]{2,1,0:T(4,128)S(1)} %log_add_fusion.2), channel_id=1, source_target_pairs={{0,4},{1,5},{2,6},{3,7},{4,0},{5,1},{6,2},{7,3},{8,12},{9,13},{10,... | collective-permute-start | bytes 49160 | tf_op jit(solution)/shard_map/ppermute | solution.py:27
  59.9 0.8 collective-permute-done.15
  60.7 0.0 copy-start.1
  60.8 1.8 %rows.1 = f32[8,128]{1,0:T(8,128)S(1)} custom-call(s32[48]{0:T(128)S(1)} %pad_add_fusion.flags, f32[8,1024,512]{2,1,0:T(8,128)S(1)} %get-tuple-element.43.cross, f32[8,4,128]{2,1,0:T(4,128)S(1)} %get-tuple-element.44.masses, f32[8,4,128]{2,1,0:T(4,128)S(1)} %bitcast.52), custom_call_target="tpu_custom_call" | custom-call | tf_op jit(solution)/shard_map/rows/pallas_call | solution.py:348
  62.6 3.0 %collective-permute-start.16 = (f32[1024]{0:T(1024)S(1)}, f32[1024]{0:T(1024)S(1)}, u32[]{:S(2)}, u32[]{:S(2)}) collective-permute-start(f32[1024]{0:T(1024)S(1)} %bitcast.53), channel_id=1, source_target_pairs={{0,5},{1,4},{2,7},{3,6},{4,1},{5,0},{6,3},{7,2},{8,13},{9,12},{10,... | collective-permute-start | bytes 12296 | tf_op jit(solution)/shard_map/ppermute | solution.py:27
  65.6 0.2 multiply_reduce_fusion
  65.8 1.1 %collective-permute-done.16 = f32[1024]{0:T(1024)S(1)} collective-permute-done((f32[1024]{0:T(1024)S(1)}, f32[1024]{0:T(1024)S(1)}, u32[]{:S(2)}, u32[]{:S(2)}) %collective-permute-start.16) | collective-permute-done | bytes 4128 | tf_op jit(solution)/shard_map/ppermute | solution.py:27
  66.9 1.7 %columns.3 = f32[8,4,128]{2,1,0:T(4,128)S(1)} custom-call(s32[48]{0:T(128)S(1)} %pad_add_fusion.flags, f32[8,1024,512]{2,1,0:T(8,128)S(1)} %get-tuple-element.43.cross, f32[8,128]{1,0:T(8,128)S(1)} %add_subtract_fusion.weights), custom_call_target="tpu_custom_call" | custom-call | tf_op jit(solution)/shard_map/columns/pallas_call | solution.py:361
  68.6 2.3 %collective-permute-start.19 = (f32[8,4,128]{2,1,0:T(4,128)S(1)}, f32[8,4,128]{2,1,0:T(4,128)S(1)}, u32[]{:S(2)}, u32[]{:S(2)}) collective-permute-start(f32[8,4,128]{2,1,0:T(4,128)S(1)} %columns.3), channel_id=1, source_target_pairs={{0,6},{1,7},{2,4},{3,5},{4,2},{5,3},{6,0},{7,1},{8,14},{9,15},{10,... | collective-permute-start | bytes 49160 | tf_op jit(solution)/shard_map/ppermute | solution.py:27
  70.9 0.2 collective-permute-start.18
  71.2 0.6 collective-permute-start.17
  71.8 0.1 multiply_reduce_fusion.1
  71.9 0.9 collective-permute-done.19
  72.8 1.6 %collective-permute-done.18 = f32[8,4,128]{2,1,0:T(4,128)S(1)} collective-permute-done((f32[8,4,128]{2,1,0:T(4,128)S(1)}, f32[8,4,128]{2,1,0:T(4,128)S(1)}, u32[]{:S(2)}, u32[]{:S(2)}) %collective-permute-start.18) | collective-permute-done | bytes 16416 | tf_op jit(solution)/shard_map/ppermute | solution.py:27
  74.5 6.0 %collective-permute-start.21 = (f32[4,128]{1,0:T(4,128)S(1)}, f32[4,128]{1,0:T(4,128)S(1)}, u32[]{:S(2)}, u32[]{:S(2)}) collective-permute-start(f32[4,128]{1,0:T(4,128)S(1)} %fusion.10), channel_id=1, source_target_pairs={{0,16},{1,17},{2,18},{3,19},{4,247},{5,246},{6,245},{7,244},{8,24}... | collective-permute-start | bytes 6152 | tf_op jit(solution)/shard_map/ppermute | solution.py:27
  80.4 0.7 collective-permute-start.20
  81.1 0.0 collective-permute-done.21
  81.2 2.0 %collective-permute-done.20 = f32[2,4,128]{2,1,0:T(4,128)S(1)} collective-permute-done((f32[2,4,128]{2,1,0:T(4,128)S(1)}, f32[2,4,128]{2,1,0:T(4,128)S(1)}, u32[]{:S(2)}, u32[]{:S(2)}) %collective-permute-start.20) | collective-permute-done | bytes 4128 | tf_op jit(solution)/shard_map/ppermute | solution.py:27
  83.2 4.9 %collective-permute-start.22 = (f32[2,4,128]{2,1,0:T(4,128)S(1)}, f32[2,4,128]{2,1,0:T(4,128)S(1)}, u32[]{:S(2)}, u32[]{:S(2)}) collective-permute-start(f32[2,4,128]{2,1,0:T(4,128)S(1)} %log_add_fusion.6), channel_id=1, source_target_pairs={{0,4},{1,5},{2,6},{3,7},{4,0},{5,1},{6,2},{7,3},{8,12},{9,13},{10,... | collective-permute-start | bytes 12296 | tf_op jit(solution)/shard_map/ppermute | solution.py:27
  88.1 0.6 multiply_subtract_fusion
  88.7 1.5 %collective-permute-start.24 = (f32[2,4,128]{2,1,0:T(4,128)S(1)}, f32[2,4,128]{2,1,0:T(4,128)S(1)}, u32[]{:S(2)}, u32[]{:S(2)}) collective-permute-start(f32[2,4,128]{2,1,0:T(4,128)S(1)} %log_add_fusion.6), channel_id=1, source_target_pairs={{0,5},{1,4},{2,7},{3,6},{4,1},{5,0},{6,3},{7,2},{8,13},{9,12},{10,... | collective-permute-start | bytes 12296 | tf_op jit(solution)/shard_map/ppermute | solution.py:27
  90.2 0.1 collective-permute-start.23
  90.4 1.4 %collective-permute-done.24 = f32[2,4,128]{2,1,0:T(4,128)S(1)} collective-permute-done((f32[2,4,128]{2,1,0:T(4,128)S(1)}, f32[2,4,128]{2,1,0:T(4,128)S(1)}, u32[]{:S(2)}, u32[]{:S(2)}) %collective-permute-start.24) | collective-permute-done | bytes 4128 | tf_op jit(solution)/shard_map/ppermute | solution.py:27
  91.8 0.9 collective-permute-done.23
  92.7 0.6 fusion.2
  (39 shorter events, 0.3 us)
Async XLA Ops:
  0.6 18.7 %collective-permute-start = (bf16[512,256]{1,0:T(8,128)(2,1)}, bf16[512,256]{1,0:T(8,128)(2,1)S(1)}, u32[]{:S(2)}, u32[]{:S(2)}) collective-permute-start(bf16[512,256]{1,0:T(8,128)(2,1)} %src.1), channel_id=1, source_target_pairs={{0,5},{1,4},{2,7},{3,6},{4,1},{5,0},{6,3},{7,2},{8,13},{9,12},{10,... | collective-permute-start | bytes 786440 | tf_op jit(solution)/shard_map/ppermute | solution.py:27
  5.1 22.7 %collective-permute-start.2 = (bf16[528,256]{1,0:T(8,128)(2,1)S(1)}, bf16[528,256]{1,0:T(8,128)(2,1)S(1)}, u32[]{:S(2)}, u32[]{:S(2)}) collective-permute-start(bf16[528,256]{1,0:T(8,128)(2,1)S(1)} %get-tuple-element.27.refs_2_), channel_id=1, source_target_pairs={{0,8},{1,9},{2,10},{3,11},{4,12},{5,13},{6,14},{7,15},{8,16},{9,17... | collective-permute-start | bytes 811016 | tf_op jit(solution)/shard_map/ppermute | solution.py:27
  6.4 22.8 %collective-permute-start.3 = (bf16[528,256]{1,0:T(8,128)(2,1)S(1)}, bf16[528,256]{1,0:T(8,128)(2,1)S(1)}, u32[]{:S(2)}, u32[]{:S(2)}) collective-permute-start(bf16[528,256]{1,0:T(8,128)(2,1)S(1)} %get-tuple-element.27.refs_2_), channel_id=1, source_target_pairs={{0,251},{1,250},{2,249},{3,248},{4,255},{5,254},{6,253},{7,252},{8... | collective-permute-start | bytes 811016 | tf_op jit(solution)/shard_map/ppermute | solution.py:27
  14.5 14.7 %collective-permute-start.4 = (bf16[528,256]{1,0:T(8,128)(2,1)S(1)}, bf16[528,256]{1,0:T(8,128)(2,1)S(1)}, u32[]{:S(2)}, u32[]{:S(2)}) collective-permute-start(bf16[528,256]{1,0:T(8,128)(2,1)S(1)} %get-tuple-element.27.refs_2_), channel_id=1, source_target_pairs={{0,247},{1,246},{2,245},{3,244},{4,16},{5,17},{6,18},{7,19},{8,255... | collective-permute-start | bytes 811016 | tf_op jit(solution)/shard_map/ppermute | solution.py:27
  19.3 4.3 %collective-permute-start.1 = (bf16[528,256]{1,0:T(8,128)(2,1)S(1)}, bf16[528,256]{1,0:T(8,128)(2,1)S(1)}, u32[]{:S(2)}, u32[]{:S(2)}) collective-permute-start(bf16[528,256]{1,0:T(8,128)(2,1)S(1)} %get-tuple-element.27.refs_2_), channel_id=1, source_target_pairs={{0,4},{1,5},{2,6},{3,7},{4,0},{5,1},{6,2},{7,3},{8,12},{9,13},{10,... | collective-permute-start | bytes 811016 | tf_op jit(solution)/shard_map/ppermute | solution.py:27
  29.2 7.2 %copy-start.2 = (f32[512]{0:T(512)S(1)}, f32[512]{0:T(512)}, u32[]{:S(2)}) copy-start(f32[512]{0:T(512)} %param.10) | copy-start | bytes 6148
  29.2 4.8 %collective-permute-start.5 = (bf16[528,256]{1,0:T(8,128)(2,1)S(1)}, bf16[528,256]{1,0:T(8,128)(2,1)S(1)}, u32[]{:S(2)}, u32[]{:S(2)}) collective-permute-start(bf16[528,256]{1,0:T(8,128)(2,1)S(1)} %collective-permute-done.2.refs_2_), channel_id=1, source_target_pairs={{0,4},{1,5},{2,6},{3,7},{4,0},{5,1},{6,2},{7,3},{8,12},{9,13},{10,... | collective-permute-start | bytes 811016 | tf_op jit(solution)/shard_map/ppermute | solution.py:27
  32.8 1.6 %collective-permute-start.6 = (bf16[528,256]{1,0:T(8,128)(2,1)S(1)}, bf16[528,256]{1,0:T(8,128)(2,1)S(1)}, u32[]{:S(2)}, u32[]{:S(2)}) collective-permute-start(bf16[528,256]{1,0:T(8,128)(2,1)S(1)} %collective-permute-done.3.refs_3_), channel_id=1, source_target_pairs={{0,4},{1,5},{2,6},{3,7},{4,0},{5,1},{6,2},{7,3},{8,12},{9,13},{10,... | collective-permute-start | bytes 811016 | tf_op jit(solution)/shard_map/ppermute | solution.py:27
  32.8 1.9 %collective-permute-start.7 = (bf16[528,256]{1,0:T(8,128)(2,1)S(1)}, bf16[528,256]{1,0:T(8,128)(2,1)S(1)}, u32[]{:S(2)}, u32[]{:S(2)}) collective-permute-start(bf16[528,256]{1,0:T(8,128)(2,1)S(1)} %collective-permute-done.4.refs_4_), channel_id=1, source_target_pairs={{0,4},{1,5},{2,6},{3,7},{4,0},{5,1},{6,2},{7,3},{8,12},{9,13},{10,... | collective-permute-start | bytes 811016 | tf_op jit(solution)/shard_map/ppermute | solution.py:27
  36.5 3.2 %collective-permute-start.8 = (f32[1536]{0:T(1024)S(1)}, f32[1536]{0:T(1024)S(1)}, u32[]{:S(2)}, u32[]{:S(2)}) collective-permute-start(f32[1536]{0:T(1024)S(1)} %pad_maximum_fusion), channel_id=1, source_target_pairs={{0,5},{1,4},{2,7},{3,6},{4,1},{5,0},{6,3},{7,2},{8,13},{9,12},{10,... | collective-permute-start | bytes 18440 | tf_op jit(solution)/shard_map/ppermute | solution.py:27
  39.6 26.0 %copy-start = (bf16[1024,256]{1,0:T(8,128)(2,1)S(1)}, bf16[1024,256]{1,0:T(8,128)(2,1)}, u32[]{:S(2)}) copy-start(bf16[1024,256]{1,0:T(8,128)(2,1)} %points.1) | copy-start | bytes 1572868
  41.2 4.3 %collective-permute-start.11 = (f32[8,4,128]{2,1,0:T(4,128)S(1)}, f32[8,4,128]{2,1,0:T(4,128)S(1)}, u32[]{:S(2)}, u32[]{:S(2)}) collective-permute-start(f32[8,4,128]{2,1,0:T(4,128)S(1)} %columns.2), channel_id=1, source_target_pairs={{0,6},{1,7},{2,4},{3,5},{4,2},{5,3},{6,0},{7,1},{8,14},{9,15},{10,... | collective-permute-start | bytes 49160 | tf_op jit(solution)/shard_map/ppermute | solution.py:27
  41.8 3.8 %collective-permute-start.10 = (f32[8,4,128]{2,1,0:T(4,128)S(1)}, f32[8,4,128]{2,1,0:T(4,128)S(1)}, u32[]{:S(2)}, u32[]{:S(2)}) collective-permute-start(f32[8,4,128]{2,1,0:T(4,128)S(1)} %columns.2), channel_id=1, source_target_pairs={{0,2},{1,3},{2,0},{3,1},{4,6},{5,7},{6,4},{7,5},{8,10},{9,11},{10,... | collective-permute-start | bytes 49160 | tf_op jit(solution)/shard_map/ppermute | solution.py:27
  43.3 2.2 %collective-permute-start.9 = (f32[8,4,128]{2,1,0:T(4,128)S(1)}, f32[8,4,128]{2,1,0:T(4,128)S(1)}, u32[]{:S(2)}, u32[]{:S(2)}) collective-permute-start(f32[8,4,128]{2,1,0:T(4,128)S(1)} %columns.2), channel_id=1, source_target_pairs={{0,4},{1,5},{2,6},{3,7},{4,0},{5,1},{6,2},{7,3},{8,12},{9,13},{10,... | collective-permute-start | bytes 49160 | tf_op jit(solution)/shard_map/ppermute | solution.py:27
  45.6 12.6 %collective-permute-start.12 = (f32[6,4,128]{2,1,0:T(4,128)S(1)}, f32[6,4,128]{2,1,0:T(4,128)S(1)}, u32[]{:S(2)}, u32[]{:S(2)}) collective-permute-start(f32[6,4,128]{2,1,0:T(4,128)S(1)} %slice_select_fusion), channel_id=1, source_target_pairs={{0,8},{1,9},{2,10},{3,11},{4,255},{5,254},{6,253},{7,252},{8,16},{... | collective-permute-start | bytes 36872 | tf_op jit(solution)/shard_map/ppermute | solution.py:27
  51.0 7.3 %collective-permute-start.13 = (f32[4,4,128]{2,1,0:T(4,128)S(1)}, f32[4,4,128]{2,1,0:T(4,128)S(1)}, u32[]{:S(2)}, u32[]{:S(2)}) collective-permute-start(f32[4,4,128]{2,1,0:T(4,128)S(1)} %slice_select_fusion.1), channel_id=1, source_target_pairs={{0,16},{1,17},{2,18},{3,19},{4,247},{5,246},{6,245},{7,244},{8,24}... | collective-permute-start | bytes 24584 | tf_op jit(solution)/shard_map/ppermute | solution.py:27
  54.3 4.0 %collective-permute-start.14 = (f32[2,4,128]{2,1,0:T(4,128)S(1)}, f32[2,4,128]{2,1,0:T(4,128)S(1)}, u32[]{:S(2)}, u32[]{:S(2)}) collective-permute-start(f32[2,4,128]{2,1,0:T(4,128)S(1)} %slice_select_fusion.4), channel_id=1, source_target_pairs={{0,24},{1,25},{2,26},{3,27},{4,239},{5,238},{6,237},{7,236},{8,35}... | collective-permute-start | bytes 12296 | tf_op jit(solution)/shard_map/ppermute | solution.py:27
  58.3 2.4 %collective-permute-start.15 = (f32[8,4,128]{2,1,0:T(4,128)S(1)}, f32[8,4,128]{2,1,0:T(4,128)S(1)}, u32[]{:S(2)}, u32[]{:S(2)}) collective-permute-start(f32[8,4,128]{2,1,0:T(4,128)S(1)} %log_add_fusion.2), channel_id=1, source_target_pairs={{0,4},{1,5},{2,6},{3,7},{4,0},{5,1},{6,2},{7,3},{8,12},{9,13},{10,... | collective-permute-start | bytes 49160 | tf_op jit(solution)/shard_map/ppermute | solution.py:27
  60.7 11.0 %copy-start.1 = (bf16[512,256]{1,0:T(8,128)(2,1)S(1)}, bf16[512,256]{1,0:T(8,128)(2,1)}, u32[]{:S(2)}) copy-start(bf16[512,256]{1,0:T(8,128)(2,1)} %src.1) | copy-start | bytes 786436
  62.6 4.3 %collective-permute-start.16 = (f32[1024]{0:T(1024)S(1)}, f32[1024]{0:T(1024)S(1)}, u32[]{:S(2)}, u32[]{:S(2)}) collective-permute-start(f32[1024]{0:T(1024)S(1)} %bitcast.53), channel_id=1, source_target_pairs={{0,5},{1,4},{2,7},{3,6},{4,1},{5,0},{6,3},{7,2},{8,13},{9,12},{10,... | collective-permute-start | bytes 12296 | tf_op jit(solution)/shard_map/ppermute | solution.py:27
  68.6 4.2 %collective-permute-start.19 = (f32[8,4,128]{2,1,0:T(4,128)S(1)}, f32[8,4,128]{2,1,0:T(4,128)S(1)}, u32[]{:S(2)}, u32[]{:S(2)}) collective-permute-start(f32[8,4,128]{2,1,0:T(4,128)S(1)} %columns.3), channel_id=1, source_target_pairs={{0,6},{1,7},{2,4},{3,5},{4,2},{5,3},{6,0},{7,1},{8,14},{9,15},{10,... | collective-permute-start | bytes 49160 | tf_op jit(solution)/shard_map/ppermute | solution.py:27
  70.9 3.5 %collective-permute-start.18 = (f32[8,4,128]{2,1,0:T(4,128)S(1)}, f32[8,4,128]{2,1,0:T(4,128)S(1)}, u32[]{:S(2)}, u32[]{:S(2)}) collective-permute-start(f32[8,4,128]{2,1,0:T(4,128)S(1)} %columns.3), channel_id=1, source_target_pairs={{0,2},{1,3},{2,0},{3,1},{4,6},{5,7},{6,4},{7,5},{8,10},{9,11},{10,... | collective-permute-start | bytes 49160 | tf_op jit(solution)/shard_map/ppermute | solution.py:27
  71.2 3.2 %collective-permute-start.17 = (f32[8,4,128]{2,1,0:T(4,128)S(1)}, f32[8,4,128]{2,1,0:T(4,128)S(1)}, u32[]{:S(2)}, u32[]{:S(2)}) collective-permute-start(f32[8,4,128]{2,1,0:T(4,128)S(1)} %columns.3), channel_id=1, source_target_pairs={{0,4},{1,5},{2,6},{3,7},{4,0},{5,1},{6,2},{7,3},{8,12},{9,13},{10,... | collective-permute-start | bytes 49160 | tf_op jit(solution)/shard_map/ppermute | solution.py:27
  74.5 6.7 %collective-permute-start.21 = (f32[4,128]{1,0:T(4,128)S(1)}, f32[4,128]{1,0:T(4,128)S(1)}, u32[]{:S(2)}, u32[]{:S(2)}) collective-permute-start(f32[4,128]{1,0:T(4,128)S(1)} %fusion.10), channel_id=1, source_target_pairs={{0,16},{1,17},{2,18},{3,19},{4,247},{5,246},{6,245},{7,244},{8,24}... | collective-permute-start | bytes 6152 | tf_op jit(solution)/shard_map/ppermute | solution.py:27
  80.4 2.8 %collective-permute-start.20 = (f32[2,4,128]{2,1,0:T(4,128)S(1)}, f32[2,4,128]{2,1,0:T(4,128)S(1)}, u32[]{:S(2)}, u32[]{:S(2)}) collective-permute-start(f32[2,4,128]{2,1,0:T(4,128)S(1)} %slice_select_fusion.2), channel_id=1, source_target_pairs={{0,8},{1,9},{2,10},{3,11},{4,255},{5,254},{6,253},{7,252},{8,16},{... | collective-permute-start | bytes 12296 | tf_op jit(solution)/shard_map/ppermute | solution.py:27
  83.2 7.1 %collective-permute-start.22 = (f32[2,4,128]{2,1,0:T(4,128)S(1)}, f32[2,4,128]{2,1,0:T(4,128)S(1)}, u32[]{:S(2)}, u32[]{:S(2)}) collective-permute-start(f32[2,4,128]{2,1,0:T(4,128)S(1)} %log_add_fusion.6), channel_id=1, source_target_pairs={{0,4},{1,5},{2,6},{3,7},{4,0},{5,1},{6,2},{7,3},{8,12},{9,13},{10,... | collective-permute-start | bytes 12296 | tf_op jit(solution)/shard_map/ppermute | solution.py:27
  88.7 3.0 %collective-permute-start.24 = (f32[2,4,128]{2,1,0:T(4,128)S(1)}, f32[2,4,128]{2,1,0:T(4,128)S(1)}, u32[]{:S(2)}, u32[]{:S(2)}) collective-permute-start(f32[2,4,128]{2,1,0:T(4,128)S(1)} %log_add_fusion.6), channel_id=1, source_target_pairs={{0,5},{1,4},{2,7},{3,6},{4,1},{5,0},{6,3},{7,2},{8,13},{9,12},{10,... | collective-permute-start | bytes 12296 | tf_op jit(solution)/shard_map/ppermute | solution.py:27
  90.2 2.5 %collective-permute-start.23 = (f32[2,4,128]{2,1,0:T(4,128)S(1)}, f32[2,4,128]{2,1,0:T(4,128)S(1)}, u32[]{:S(2)}, u32[]{:S(2)}) collective-permute-start(f32[2,4,128]{2,1,0:T(4,128)S(1)} %log_add_fusion.6), channel_id=1, source_target_pairs={{0,1},{1,0},{2,3},{3,2},{4,5},{5,4},{6,7},{7,6},{8,9},{9,8},{10,11... | collective-permute-start | bytes 12296 | tf_op jit(solution)/shard_map/ppermute | solution.py:27

commit v4 on v3

--- a/solution.py
+++ b/solution.py
@@ -22,21 +22,28 @@
     pairs = []
     for block in range(blocks):
         for rep in range(REPS):
-            to_block, to_rep = place(block, rep)
-            pairs.append((block * REPS + rep, to_block % blocks * REPS + to_rep))
+            target = place(block, rep)
+            if target is not None:
+                pairs.append((block * REPS + rep, target[0] % blocks * REPS + target[1]))
     return lax.ppermute(value, ("blk", "rep"), pairs)
 
 
-def along(steps, blocks):
+def crosses(one, other, blocks):
+    return one % blocks // SEGMENT != other % blocks // SEGMENT
+
+
+def along(steps, blocks, crossing=None):
     def place(block, rep):
-        target = (block + steps) % blocks
-        return target, rep if (target // SEGMENT - block // SEGMENT) % 2 == 0 else REPS - 1 - rep
+        target = block + steps
+        if crossing not in (None, crosses(block, target, blocks)):
+            return None
+        return target, REPS - 1 - rep if crosses(block, target, blocks) else rep
 
     return place
 
 
-def by_core(even_steps, odd_steps, blocks):
-    even, odd = along(even_steps, blocks), along(odd_steps, blocks)
+def by_core(even_steps, odd_steps, blocks, crossing=None):
+    even, odd = along(even_steps, blocks, crossing), along(odd_steps, blocks, crossing)
     return lambda block, rep: even(block, rep) if block % 2 == 0 else odd(block, rep)
 
 
@@ -45,7 +52,7 @@
 
 
 def diagonal(block, rep):
-    return block ^ 1, rep ^ 1
+    return block ^ 1, rep ^ 2
 
 
 def half_norms(points):
@@ -129,7 +136,9 @@
     lax.fori_loop(0, 2 * count, unit, 0)
 
 
-def message_kernel(scale, half, points, masses, initial, src, out, src_out, block_ref, mass_ref, initial_ref, sems):
+def message_kernel(
+    scale, half, points, masses, initial, src, out, quarter, src_out, block_ref, mass_ref, initial_ref, sems
+):
     columns, depth = block_ref.shape
     src_copy = pltpu.make_async_copy(src, src_out, sems.at[1])
     copy = pltpu.make_async_copy(
@@ -164,8 +173,37 @@
     bias = mass + (pick(initial_ref) - 0.5 * norms) * scale
     rows = [jnp.concatenate(pair, axis=1) for pair in zip(terms(bias), terms(mass))]
     rows.append(jnp.zeros((TAIL - 3 * count, 256), jnp.float32))
-    out[columns:, :] = jnp.concatenate(rows, axis=0).astype(jnp.bfloat16)
+    tail = jnp.concatenate(rows, axis=0).astype(jnp.bfloat16)
+    out[columns:, :] = tail
+    quarter[columns // 2 :, :] = tail
+    for q in range(2):
+
+        @pl.when(half[1] == q)
+        def _(q=q):
+            quarter[: columns // 2, :] = out[q * columns // 2 : (q + 1) * columns // 2, :]
+
     src_copy.wait()
+
+
+def arrive_kernel(where, *refs):
+    count = len(refs) // 4
+    for d in range(count):
+        whole, first, second, out = refs[d::count]
+        half = first.shape[0] - TAIL
+
+        @pl.when(where[d] == 0)
+        def _(whole=whole, out=out):
+            out[...] = whole[...]
+
+        @pl.when(where[d] != 0)
+        def _(first=first, second=second, out=out):
+            out[2 * half :, :] = first[half:, :]
+            for q in range(2):
+
+                @pl.when(where[count] == q)
+                def _(q=q):
+                    out[q * half : (q + 1) * half, :] = first[:half, :]
+                    out[(1 - q) * half : (2 - q) * half, :] = second[:half, :]
 
 
 def first_kernel(numbers, first, last, flags, *refs):
@@ -291,10 +329,11 @@
         functools.partial(message_kernel, scale),
         out_shape=[
             pltpu.VMEM((columns + TAIL, depth), jnp.bfloat16),
+            pltpu.VMEM((columns // 2 + TAIL, depth), jnp.bfloat16),
             pltpu.VMEM(src.shape, jnp.bfloat16),
         ],
         in_specs=[SCALARS] + [pl.BlockSpec(memory_space=pltpu.HBM)] * 4,
-        out_specs=[WHOLE] * 2,
+        out_specs=[WHOLE] * 3,
         scratch_shapes=[
             pltpu.VMEM((columns, depth), jnp.bfloat16),
             pltpu.VMEM((2 * columns // 128, 128), jnp.float32),
@@ -303,7 +342,18 @@
         ],
         compiler_params=PARAMS,
         name="message",
-    )(half_index.reshape(1), *map(in_hbm, (points, masses.reshape(-1, 128), initial.reshape(-1, 128), src)))
+    )(half_index, *map(in_hbm, (points, masses.reshape(-1, 128), initial.reshape(-1, 128), src)))
+
+
+def call_arrive(where, wholes, firsts, seconds):
+    return pl.pallas_call(
+        arrive_kernel,
+        out_shape=[pltpu.VMEM(whole.shape, whole.dtype) for whole in wholes],
+        in_specs=[SCALARS] + [WHOLE] * (3 * len(wholes)),
+        out_specs=[WHOLE] * len(wholes),
+        compiler_params=PARAMS,
+        name="arrive",
+    )(where, *wholes, *firsts, *seconds)
 
 
 def call_first(numbers, first, last, flags, sources, targets, state):
@@ -379,19 +429,38 @@
     rep = lax.axis_index("rep")
     blocks = lax.axis_size("blk")
     core = block % 2
-    half_index = (rep % 2) ^ ((block // SEGMENT) % 2)
+    half_index = (rep // 2) ^ ((block // SEGMENT) % 2)
     rows = src_points.shape[0]
     width = tgt_points.shape[0]
     columns = width // 2
 
-    message, own = call_message(
-        1.0 / EPS_START, half_index, tgt_points, tgt_log_mass, initial_potential, src_points
+    message, quarter, own = call_message(
+        1.0 / EPS_START, jnp.stack([half_index, rep % 2]), tgt_points, tgt_log_mass, initial_potential, src_points
     )
     mate = send(src_points, diagonal, blocks)
 
-    before = send(message, along(2, blocks), blocks)
-    after = send(message, along(-2, blocks), blocks)
-    third = send(message, by_core(-3, 3, blocks), blocks)
+    routes = ((2, 2), (-2, -2), (-3, 3))
+
+    def either(*places):
+        return lambda b, r: next((place(b, r) for place in places if place(b, r)), None)
+
+    crossing = [by_core(*steps, blocks, True) for steps in routes]
+    crossed = [send(quarter, either(*crossing[:2]), blocks), send(quarter, crossing[2], blocks)]
+    wholes = [send(message, by_core(*steps, blocks, False), blocks) for steps in routes]
+
+    def handed_on(*origins):
+        def place(b, r):
+            return (b, r ^ 1) if any(crosses(b, b + origin[b % 2], blocks) for origin in origins) else None
+
+        return place
+
+    handed = [
+        send(crossed[0], handed_on((-2, -2), (2, 2)), blocks),
+        send(crossed[1], handed_on((-3, 3)), blocks),
+    ]
+    firsts, seconds = [[pieces[0], pieces[0], pieces[1]] for pieces in (crossed, handed)]
+    origins = (block - 2, block + 2, block - 3 + 6 * core)
+    where = jnp.stack([crosses(block, origin, blocks).astype(jnp.int32) for origin in origins] + [1 - rep % 2])
     tied, mate = lax.optimization_barrier((message, mate))
     beside = send(tied, sibling, blocks)
     sources = [own, mate]
@@ -418,7 +487,8 @@
     flags = jnp.concatenate([kept_pairs.reshape(-1), slots, total, order])
 
     state = call_first(groups[0], True, False, flags, sources, [message, beside], ())
-    state, arrived = lax.optimization_barrier((state, (before, after, third)))
+    state, where = lax.optimization_barrier((state, where))
+    arrived = call_arrive(where, wholes, firsts, seconds)
     passed_on = [send(value, sibling, blocks) for value in arrived]
     state = call_first(groups[1], False, False, flags, sources, arrived, state)
     *state, last = call_first(groups[2], False, True, flags, sources, passed_on, state)
@@ -439,8 +509,8 @@
         chip = log_merge(
             part,
             send(part, sibling, blocks),
-            send(part, lambda b, r: (b, r ^ 2), blocks),
-            send(part, lambda b, r: (b ^ 1, r ^ 2), blocks),
+            send(part, lambda b, r: (b, r ^ 1), blocks),
+            send(part, lambda b, r: (b ^ 1, r ^ 1), blocks),
         )
         forward = core == 0
         if sweep + 1 < ITERS:
@@ -463,7 +533,7 @@
             far = jnp.where(forward, jnp.stack([far, empty]), jnp.stack([empty, far]))
             side = log_merge(jnp.where(forward, chip[3:5], jnp.full_like(near, NEG_FILL)), near, far)
             over_core = send(side, sibling, blocks)
-            over_half = send(side, lambda b, r: (b, r ^ 1), blocks)
+            over_half = send(side, lambda b, r: (b, r ^ 2), blocks)
             over_both = send(side, diagonal, blocks)
             mine = log_merge(side, over_core)
             other = log_merge(over_half, over_both)

time: 94.8 us -> 107 us (1.13); the launches traced: 93.3 us -> 107 us
  starting transfers between devices: 52.3 us -> 64.8 us
  Pallas kernels: 10.7 us -> 14.7 us
  waiting for transfers between devices: 20.7 us -> 17.2 us
    ppermute x25 -> x29, starting transfers between devices: 52.3 us -> 64.8 us  [send(): return lax.ppermute(value, ('blk', 'rep'), pairs)]
    ppermute x25 -> x29, waiting for transfers between devices: 20.7 us -> 17.2 us  [send(): return lax.ppermute(value, ('blk', 'rep'), pairs)]
    pallas_call x3, Pallas kernels: 4.32 us -> 5.49 us  [call_first(): pl.pallas_call(functools.partial(first_kernel, numbers, first, last), out...]
    pallas_call x2, Pallas kernels: 3.22 us -> 4.34 us  [call_columns(): pl.pallas_call(functools.partial(column_kernel, twice), out_shape=jax.Sha...]
  transfers between devices with their start and end apart: 25 -> 29, of which waited for: 14 -> 12; matrix products, arithmetic and copies ran while one was open for 7% -> 6% of each run, Pallas kernels for 4% -> 5%
where the time goes in v4:
time: 107 us
  starting transfers between devices  64.8 us (61%)
  waiting for transfers between devices  17.2 us (16%)
  Pallas kernels  14.7 us (14%)
  other arithmetic  5.08 us (5%)
  local copies, waits for them, and re-layouts  2.58 us (2%)
  between operations  2.3 us (2%)
    ppermute x29, starting transfers between devices, send(): return lax.ppermute(value, ('blk', 'rep'), pairs)  64.8 us
    ppermute x29, waiting for transfers between devices, send(): return lax.ppermute(value, ('blk', 'rep'), pairs)  17.2 us
    pallas_call x3, Pallas kernels, call_first(): pl.pallas_call(functools.partial(first_kernel, numbers, first, last), out...  5.49 us
    pallas_call x2, Pallas kernels, call_columns(): pl.pallas_call(functools.partial(column_kernel, twice), out_shape=jax.Sha...  4.34 us
    pallas_call x1, Pallas kernels, call_rows(): pl.pallas_call(row_kernel, out_shape=jax.ShapeDtypeStruct((rows // 128, 1...  2.42 us
  transfers between devices with their start and end apart: 29, of which 12 were waited for; matrix products, arithmetic and copies ran while one was open for 6% of the time, Pallas kernels for 5%

profile of v4, /device:TPU:1, one launch (start us, length us, event | category | flops | bytes accessed | tf_op | source)
XLA Modules:
  0.0 106.7 jit_solution(3607335937010913122)
XLA Ops:
  0.6 4.5 %collective-permute-start = (bf16[512,256]{1,0:T(8,128)(2,1)}, bf16[512,256]{1,0:T(8,128)(2,1)S(1)}, u32[]{:S(2)}, u32[]{:S(2)}) collective-permute-start(bf16[512,256]{1,0:T(8,128)(2,1)} %src.1), channel_id=1, source_target_pairs={{0,6},{1,7},{2,4},{3,5},{4,2},{5,3},{6,0},{7,1},{8,14},{9,15},{10,... | collective-permute-start | bytes 786440 | tf_op jit(solution)/shard_map/ppermute | solution.py:28
  5.2 1.9 %message.1 = (bf16[528,256]{1,0:T(8,128)(2,1)S(1)}, bf16[272,256]{1,0:T(8,128)(2,1)S(1)}, bf16[512,256]{1,0:T(8,128)(2,1)S(1)}) custom-call(s32[2]{0:T(128)S(1)} %pad_add_fusion.1.half, bf16[1024,256]{1,0:T(8,128)(2,1)} %points.1, f32[8,128]{1,0:T(8,128)} %bitcast.81, f32[8,128]{1,0:T(8,128)} %bitcast.82, bf16[512,256]{1,0:T(8,128)(2,1)} %src.1), custom_call_target="tpu_custom_call" | custom-call | tf_op jit(solution)/shard_map/message/pallas_call | solution.py:328
  7.0 10.3 %collective-permute-start.5 = (bf16[272,256]{1,0:T(8,128)(2,1)S(1)}, bf16[272,256]{1,0:T(8,128)(2,1)S(1)}, u32[]{:S(2)}, u32[]{:S(2)}) collective-permute-start(bf16[272,256]{1,0:T(8,128)(2,1)S(1)} %get-tuple-element.35), channel_id=1, source_target_pairs={{0,251},{1,250},{2,249},{3,248},{4,255},{5,254},{6,253},{7,252},{2... | collective-permute-start | bytes 417800 | tf_op jit(solution)/shard_map/ppermute | solution.py:28
  17.4 0.7 collective-permute-start.6
  18.0 1.3 %collective-permute-start.2 = (bf16[528,256]{1,0:T(8,128)(2,1)S(1)}, bf16[528,256]{1,0:T(8,128)(2,1)S(1)}, u32[]{:S(2)}, u32[]{:S(2)}) collective-permute-start(bf16[528,256]{1,0:T(8,128)(2,1)S(1)} %get-tuple-element.29.refs_2_), channel_id=1, source_target_pairs={{0,8},{1,9},{2,10},{3,11},{4,12},{5,13},{6,14},{7,15},{8,16},{9,17... | collective-permute-start | bytes 811016 | tf_op jit(solution)/shard_map/ppermute | solution.py:28
  19.3 1.3 %collective-permute-start.3 = (bf16[528,256]{1,0:T(8,128)(2,1)S(1)}, bf16[528,256]{1,0:T(8,128)(2,1)S(1)}, u32[]{:S(2)}, u32[]{:S(2)}) collective-permute-start(bf16[528,256]{1,0:T(8,128)(2,1)S(1)} %get-tuple-element.29.refs_2_), channel_id=1, source_target_pairs={{8,0},{9,1},{10,2},{11,3},{12,4},{13,5},{14,6},{15,7},{16,8},{17,9... | collective-permute-start | bytes 811016 | tf_op jit(solution)/shard_map/ppermute | solution.py:28
  20.7 1.3 %fusion.13 = (s32[1]{0:T(128)}, s32[1]{0:T(128)}) fusion(s32[64]{0:T(128)} %param.15, s32[]{:T(128)S(6)} %select_n.180, s32[]{:T(128)S(6)} %select_n.175), kind=kLoop, calls=%fused_computation.71 | loop fusion | bytes 24 | tf_op jit(solution)/shard_map/dynamic_slice | solution.py:476
  22.0 0.6 iota_compare_fusion.2
  22.6 0.7 iota_compare_fusion.3
  23.3 1.0 dynamic-slice_reduce_fusion.1
  24.3 0.7 broadcast_select_fusion
  25.0 0.2 and_reduce_fusion.1
  25.2 0.1 copy.21
  25.3 0.1 broadcast_in_dim.38
  25.3 0.1 select_reduce_fusion.1
  25.5 3.2 %collective-permute-start.1 = (bf16[528,256]{1,0:T(8,128)(2,1)S(1)}, bf16[528,256]{1,0:T(8,128)(2,1)S(1)}, u32[]{:S(2)}, u32[]{:S(2)}) collective-permute-start(bf16[528,256]{1,0:T(8,128)(2,1)S(1)} %get-tuple-element.29.refs_2_), channel_id=1, source_target_pairs={{0,4},{1,5},{2,6},{3,7},{4,0},{5,1},{6,2},{7,3},{8,12},{9,13},{10,... | collective-permute-start | bytes 811016 | tf_op jit(solution)/shard_map/ppermute | solution.py:28
  28.7 0.1 select_reduce_fusion
  28.8 0.6 convert_reduce_fusion
  29.4 0.1 reshape.120
  30.8 4.2 %collective-permute-start.4 = (bf16[528,256]{1,0:T(8,128)(2,1)S(1)}, bf16[528,256]{1,0:T(8,128)(2,1)S(1)}, u32[]{:S(2)}, u32[]{:S(2)}) collective-permute-start(bf16[528,256]{1,0:T(8,128)(2,1)S(1)} %get-tuple-element.29.refs_2_), channel_id=1, source_target_pairs={{4,16},{5,17},{6,18},{7,19},{12,24},{13,25},{14,26},{15,27},{16,4}... | collective-permute-start | bytes 811016 | tf_op jit(solution)/shard_map/ppermute | solution.py:28
  35.1 3.8 %collective-permute-start.7 = (bf16[272,256]{1,0:T(8,128)(2,1)S(1)}, bf16[272,256]{1,0:T(8,128)(2,1)S(1)}, u32[]{:S(2)}, u32[]{:S(2)}) collective-permute-start(bf16[272,256]{1,0:T(8,128)(2,1)S(1)} %collective-permute-done.5.refs_3_.refs_4_), channel_id=1, source_target_pairs={{0,1},{1,0},{2,3},{3,2},{4,5},{5,4},{6,7},{7,6},{24,25},{25,24},{2... | collective-permute-start | bytes 417800 | tf_op jit(solution)/shard_map/ppermute | solution.py:28
  38.9 0.7 collective-permute-start.8
  39.6 0.1 pad_add_fusion.2.where
  39.7 2.5 %first_rows.3 = (f32[8,1024,512]{2,1,0:T(8,128)S(1)}, f32[8,4,128]{2,1,0:T(4,128)S(1)}, f32[1024,128]{1,0:T(8,128)S(1)}, f32[1024,128]{1,0:T(8,128)S(1)}) custom-call(s32[48]{0:T(128)S(1)} %pad_add_fusion.flags, bf16[512,256]{1,0:T(8,128)(2,1)S(1)} %get-tuple-element.26.refs_0_, bf16[512,256]{1,0:T(8,128)(2,1)S(1)} %collective-permute-done.refs_1_, ...), custom_call_target="tpu_custom_call" | custom-call | flops 536870912 | bytes 1048576 | tf_op jit(solution)/shard_map/first_rows/pallas_call | solution.py:375
  42.3 0.4 collective-permute-done.7.refs_6_.refs_7_
  42.6 0.6 arrive.1
  43.3 1.0 collective-permute-start.10
  44.3 0.1 collective-permute-start.11
  44.4 0.4 collective-permute-start.9
  44.8 1.3 %first_rows.4 = (f32[8,1024,512]{2,1,0:T(8,128)S(1)}, f32[8,4,128]{2,1,0:T(4,128)S(1)}, f32[1024,128]{1,0:T(8,128)S(1)}, f32[1024,128]{1,0:T(8,128)S(1)}) custom-call(s32[48]{0:T(128)S(1)} %pad_add_fusion.flags, bf16[512,256]{1,0:T(8,128)(2,1)S(1)} %get-tuple-element.26.refs_0_, ...), custom_call_target="tpu_custom_call", output_to_operand_aliasing={{0}: (6, {}), {1}: (7, {}), {2}: (8, {}), {3}: (9, {})} | custom-call | flops 805306368 | bytes 1572864 | tf_op jit(solution)/shard_map/first_rows/pallas_call | solution.py:375
  46.2 0.1 collective-permute-done.9.refs_2_
  46.2 1.7 %first_rows.5 = (f32[8,1024,512]{2,1,0:T(8,128)S(1)}, f32[8,4,128]{2,1,0:T(4,128)S(1)}, f32[1024,128]{1,0:T(8,128)S(1)}, f32[1024,128]{1,0:T(8,128)S(1)}, f32[8,128]{1,0:T(8,128)S(1)}) custom-call(s32[48]{0:T(128)S(1)} %pad_add_fusion.flags, ...), custom_call_target="tpu_custom_call", output_to_operand_aliasing={{0}: (6, {}), {1}: (7, {}), {2}: (8, {}), {3}: (9, {})} | custom-call | flops 805306368 | bytes 1572864 | tf_op jit(solution)/shard_map/first_rows/pallas_call | solution.py:375
  47.9 0.4 collective-permute-start.12
  48.3 3.7 %collective-permute-done.12 = f32[1536]{0:T(1024)S(1)} collective-permute-done((f32[1536]{0:T(1024)S(1)}, f32[1536]{0:T(1024)S(1)}, u32[]{:S(2)}, u32[]{:S(2)}) %collective-permute-start.12) | collective-permute-done | bytes 6176 | tf_op jit(solution)/shard_map/ppermute | solution.py:28
  52.0 2.1 %columns.2 = f32[8,4,128]{2,1,0:T(4,128)S(1)} custom-call(s32[48]{0:T(128)S(1)} %pad_add_fusion.flags, f32[8,1024,512]{2,1,0:T(8,128)S(1)} %get-tuple-element.47.cross, f32[8,128]{1,0:T(8,128)S(1)} %add_subtract_fusion.1.weights), custom_call_target="tpu_custom_call" | custom-call | tf_op jit(solution)/shard_map/columns/pallas_call | solution.py:411
  54.1 0.1 collective-permute-start.15
  54.2 1.7 %collective-permute-start.14 = (f32[8,4,128]{2,1,0:T(4,128)S(1)}, f32[8,4,128]{2,1,0:T(4,128)S(1)}, u32[]{:S(2)}, u32[]{:S(2)}) collective-permute-start(f32[8,4,128]{2,1,0:T(4,128)S(1)} %columns.2), channel_id=1, source_target_pairs={{0,1},{1,0},{2,3},{3,2},{4,5},{5,4},{6,7},{7,6},{8,9},{9,8},{10,11... | collective-permute-start | bytes 49160 | tf_op jit(solution)/shard_map/ppermute | solution.py:28
  55.9 0.4 collective-permute-start.13
  56.4 1.0 collective-permute-done.15
  57.5 6.9 %collective-permute-start.16 = (f32[6,4,128]{2,1,0:T(4,128)S(1)}, f32[6,4,128]{2,1,0:T(4,128)S(1)}, u32[]{:S(2)}, u32[]{:S(2)}) collective-permute-start(f32[6,4,128]{2,1,0:T(4,128)S(1)} %slice_select_fusion), channel_id=1, source_target_pairs={{0,8},{1,9},{2,10},{3,11},{4,255},{5,254},{6,253},{7,252},{8,16},{... | collective-permute-start | bytes 36872 | tf_op jit(solution)/shard_map/ppermute | solution.py:28
  64.4 0.5 collective-permute-start.17
  64.9 3.7 %collective-permute-done.18 = f32[2,4,128]{2,1,0:T(4,128)S(1)} collective-permute-done((f32[2,4,128]{2,1,0:T(4,128)S(1)}, f32[2,4,128]{2,1,0:T(4,128)S(1)}, u32[]{:S(2)}, u32[]{:S(2)}) %collective-permute-start.18) | collective-permute-done | bytes 4128 | tf_op jit(solution)/shard_map/ppermute | solution.py:28
  68.7 3.5 %collective-permute-start.19 = (f32[8,4,128]{2,1,0:T(4,128)S(1)}, f32[8,4,128]{2,1,0:T(4,128)S(1)}, u32[]{:S(2)}, u32[]{:S(2)}) collective-permute-start(f32[8,4,128]{2,1,0:T(4,128)S(1)} %log_add_fusion.2), channel_id=1, source_target_pairs={{0,4},{1,5},{2,6},{3,7},{4,0},{5,1},{6,2},{7,3},{8,12},{9,13},{10,... | collective-permute-start | bytes 49160 | tf_op jit(solution)/shard_map/ppermute | solution.py:28
  72.2 0.8 collective-permute-done.19
  73.1 2.4 %rows.1 = f32[8,128]{1,0:T(8,128)S(1)} custom-call(s32[48]{0:T(128)S(1)} %pad_add_fusion.flags, f32[8,1024,512]{2,1,0:T(8,128)S(1)} %get-tuple-element.47.cross, f32[8,4,128]{2,1,0:T(4,128)S(1)} %get-tuple-element.48.masses, f32[8,4,128]{2,1,0:T(4,128)S(1)} %bitcast.57), custom_call_target="tpu_custom_call" | custom-call | tf_op jit(solution)/shard_map/rows/pallas_call | solution.py:398
  75.5 2.2 %collective-permute-start.20 = (f32[1024]{0:T(1024)S(1)}, f32[1024]{0:T(1024)S(1)}, u32[]{:S(2)}, u32[]{:S(2)}) collective-permute-start(f32[1024]{0:T(1024)S(1)} %bitcast.58), channel_id=1, source_target_pairs={{0,6},{1,7},{2,4},{3,5},{4,2},{5,3},{6,0},{7,1},{8,14},{9,15},{10,... | collective-permute-start | bytes 12296 | tf_op jit(solution)/shard_map/ppermute | solution.py:28
  77.7 0.2 multiply_reduce_fusion
  77.9 1.6 %collective-permute-done.20 = f32[1024]{0:T(1024)S(1)} collective-permute-done((f32[1024]{0:T(1024)S(1)}, f32[1024]{0:T(1024)S(1)}, u32[]{:S(2)}, u32[]{:S(2)}) %collective-permute-start.20) | collective-permute-done | bytes 4128 | tf_op jit(solution)/shard_map/ppermute | solution.py:28
  79.6 2.3 %columns.3 = f32[8,4,128]{2,1,0:T(4,128)S(1)} custom-call(s32[48]{0:T(128)S(1)} %pad_add_fusion.flags, f32[8,1024,512]{2,1,0:T(8,128)S(1)} %get-tuple-element.47.cross, f32[8,128]{1,0:T(8,128)S(1)} %add_subtract_fusion.weights), custom_call_target="tpu_custom_call" | custom-call | tf_op jit(solution)/shard_map/columns/pallas_call | solution.py:411
  81.8 2.0 %collective-permute-start.23 = (f32[8,4,128]{2,1,0:T(4,128)S(1)}, f32[8,4,128]{2,1,0:T(4,128)S(1)}, u32[]{:S(2)}, u32[]{:S(2)}) collective-permute-start(f32[8,4,128]{2,1,0:T(4,128)S(1)} %columns.3), channel_id=1, source_target_pairs={{0,5},{1,4},{2,7},{3,6},{4,1},{5,0},{6,3},{7,2},{8,13},{9,12},{10,... | collective-permute-start | bytes 49160 | tf_op jit(solution)/shard_map/ppermute | solution.py:28
  83.9 0.5 collective-permute-start.21
  84.4 0.1 multiply_reduce_fusion.1
  84.5 0.8 collective-permute-done.23
  85.3 1.2 %collective-permute-done.22 = f32[8,4,128]{2,1,0:T(4,128)S(1)} collective-permute-done((f32[8,4,128]{2,1,0:T(4,128)S(1)}, f32[8,4,128]{2,1,0:T(4,128)S(1)}, u32[]{:S(2)}, u32[]{:S(2)}) %collective-permute-start.22) | collective-permute-done | bytes 16416 | tf_op jit(solution)/shard_map/ppermute | solution.py:28
  86.5 2.5 %collective-permute-start.25 = (f32[4,128]{1,0:T(4,128)S(1)}, f32[4,128]{1,0:T(4,128)S(1)}, u32[]{:S(2)}, u32[]{:S(2)}) collective-permute-start(f32[4,128]{1,0:T(4,128)S(1)} %fusion.10), channel_id=1, source_target_pairs={{0,16},{1,17},{2,18},{3,19},{4,247},{5,246},{6,245},{7,244},{8,24}... | collective-permute-start | bytes 6152 | tf_op jit(solution)/shard_map/ppermute | solution.py:28
  89.1 2.8 %collective-permute-start.24 = (f32[2,4,128]{2,1,0:T(4,128)S(1)}, f32[2,4,128]{2,1,0:T(4,128)S(1)}, u32[]{:S(2)}, u32[]{:S(2)}) collective-permute-start(f32[2,4,128]{2,1,0:T(4,128)S(1)} %slice_select_fusion.2), channel_id=1, source_target_pairs={{0,8},{1,9},{2,10},{3,11},{4,255},{5,254},{6,253},{7,252},{8,16},{... | collective-permute-start | bytes 12296 | tf_op jit(solution)/shard_map/ppermute | solution.py:28
  91.9 0.7 collective-permute-done.24
  92.6 7.3 %collective-permute-start.26 = (f32[2,4,128]{2,1,0:T(4,128)S(1)}, f32[2,4,128]{2,1,0:T(4,128)S(1)}, u32[]{:S(2)}, u32[]{:S(2)}) collective-permute-start(f32[2,4,128]{2,1,0:T(4,128)S(1)} %log_add_fusion.6), channel_id=1, source_target_pairs={{0,4},{1,5},{2,6},{3,7},{4,0},{5,1},{6,2},{7,3},{8,12},{9,13},{10,... | collective-permute-start | bytes 12296 | tf_op jit(solution)/shard_map/ppermute | solution.py:28
  99.9 0.6 multiply_subtract_fusion
  100.5 2.2 %collective-permute-start.28 = (f32[2,4,128]{2,1,0:T(4,128)S(1)}, f32[2,4,128]{2,1,0:T(4,128)S(1)}, u32[]{:S(2)}, u32[]{:S(2)}) collective-permute-start(f32[2,4,128]{2,1,0:T(4,128)S(1)} %log_add_fusion.6), channel_id=1, source_target_pairs={{0,6},{1,7},{2,4},{3,5},{4,2},{5,3},{6,0},{7,1},{8,14},{9,15},{10,... | collective-permute-start | bytes 12296 | tf_op jit(solution)/shard_map/ppermute | solution.py:28
  102.7 0.1 collective-permute-start.27
  102.8 1.5 %collective-permute-done.28 = f32[2,4,128]{2,1,0:T(4,128)S(1)} collective-permute-done((f32[2,4,128]{2,1,0:T(4,128)S(1)}, f32[2,4,128]{2,1,0:T(4,128)S(1)}, u32[]{:S(2)}, u32[]{:S(2)}) %collective-permute-start.28) | collective-permute-done | bytes 4128 | tf_op jit(solution)/shard_map/ppermute | solution.py:28
  104.4 1.6 %collective-permute-done.27 = f32[2,4,128]{2,1,0:T(4,128)S(1)} collective-permute-done((f32[2,4,128]{2,1,0:T(4,128)S(1)}, f32[2,4,128]{2,1,0:T(4,128)S(1)}, u32[]{:S(2)}, u32[]{:S(2)}) %collective-permute-start.27) | collective-permute-done | bytes 4128 | tf_op jit(solution)/shard_map/ppermute | solution.py:28
  106.1 0.6 fusion.2
  (50 shorter events, 0.5 us)
Async XLA Ops:
  0.6 24.8 %collective-permute-start = (bf16[512,256]{1,0:T(8,128)(2,1)}, bf16[512,256]{1,0:T(8,128)(2,1)S(1)}, u32[]{:S(2)}, u32[]{:S(2)}) collective-permute-start(bf16[512,256]{1,0:T(8,128)(2,1)} %src.1), channel_id=1, source_target_pairs={{0,6},{1,7},{2,4},{3,5},{4,2},{5,3},{6,0},{7,1},{8,14},{9,15},{10,... | collective-permute-start | bytes 786440 | tf_op jit(solution)/shard_map/ppermute | solution.py:28
  7.0 23.8 %collective-permute-start.5 = (bf16[272,256]{1,0:T(8,128)(2,1)S(1)}, bf16[272,256]{1,0:T(8,128)(2,1)S(1)}, u32[]{:S(2)}, u32[]{:S(2)}) collective-permute-start(bf16[272,256]{1,0:T(8,128)(2,1)S(1)} %get-tuple-element.35), channel_id=1, source_target_pairs={{0,251},{1,250},{2,249},{3,248},{4,255},{5,254},{6,253},{7,252},{2... | collective-permute-start | bytes 417800 | tf_op jit(solution)/shard_map/ppermute | solution.py:28
  17.4 17.8 %collective-permute-start.6 = (bf16[272,256]{1,0:T(8,128)(2,1)S(1)}, bf16[272,256]{1,0:T(8,128)(2,1)S(1)}, u32[]{:S(2)}, u32[]{:S(2)}) collective-permute-start(bf16[272,256]{1,0:T(8,128)(2,1)S(1)} %get-tuple-element.35), channel_id=1, source_target_pairs={{0,247},{1,246},{2,245},{3,244},{8,255},{9,254},{10,253},{11,252},... | collective-permute-start | bytes 417800 | tf_op jit(solution)/shard_map/ppermute | solution.py:28
  18.0 24.2 %collective-permute-start.2 = (bf16[528,256]{1,0:T(8,128)(2,1)S(1)}, bf16[528,256]{1,0:T(8,128)(2,1)S(1)}, u32[]{:S(2)}, u32[]{:S(2)}) collective-permute-start(bf16[528,256]{1,0:T(8,128)(2,1)S(1)} %get-tuple-element.29.refs_2_), channel_id=1, source_target_pairs={{0,8},{1,9},{2,10},{3,11},{4,12},{5,13},{6,14},{7,15},{8,16},{9,17... | collective-permute-start | bytes 811016 | tf_op jit(solution)/shard_map/ppermute | solution.py:28
  19.3 22.9 %collective-permute-start.3 = (bf16[528,256]{1,0:T(8,128)(2,1)S(1)}, bf16[528,256]{1,0:T(8,128)(2,1)S(1)}, u32[]{:S(2)}, u32[]{:S(2)}) collective-permute-start(bf16[528,256]{1,0:T(8,128)(2,1)S(1)} %get-tuple-element.29.refs_2_), channel_id=1, source_target_pairs={{8,0},{9,1},{10,2},{11,3},{12,4},{13,5},{14,6},{15,7},{16,8},{17,9... | collective-permute-start | bytes 811016 | tf_op jit(solution)/shard_map/ppermute | solution.py:28
  25.5 13.5 %collective-permute-start.1 = (bf16[528,256]{1,0:T(8,128)(2,1)S(1)}, bf16[528,256]{1,0:T(8,128)(2,1)S(1)}, u32[]{:S(2)}, u32[]{:S(2)}) collective-permute-start(bf16[528,256]{1,0:T(8,128)(2,1)S(1)} %get-tuple-element.29.refs_2_), channel_id=1, source_target_pairs={{0,4},{1,5},{2,6},{3,7},{4,0},{5,1},{6,2},{7,3},{8,12},{9,13},{10,... | collective-permute-start | bytes 811016 | tf_op jit(solution)/shard_map/ppermute | solution.py:28
  30.8 11.4 %collective-permute-start.4 = (bf16[528,256]{1,0:T(8,128)(2,1)S(1)}, bf16[528,256]{1,0:T(8,128)(2,1)S(1)}, u32[]{:S(2)}, u32[]{:S(2)}) collective-permute-start(bf16[528,256]{1,0:T(8,128)(2,1)S(1)} %get-tuple-element.29.refs_2_), channel_id=1, source_target_pairs={{4,16},{5,17},{6,18},{7,19},{12,24},{13,25},{14,26},{15,27},{16,4}... | collective-permute-start | bytes 811016 | tf_op jit(solution)/shard_map/ppermute | solution.py:28
  35.1 7.5 %collective-permute-start.7 = (bf16[272,256]{1,0:T(8,128)(2,1)S(1)}, bf16[272,256]{1,0:T(8,128)(2,1)S(1)}, u32[]{:S(2)}, u32[]{:S(2)}) collective-permute-start(bf16[272,256]{1,0:T(8,128)(2,1)S(1)} %collective-permute-done.5.refs_3_.refs_4_), channel_id=1, source_target_pairs={{0,1},{1,0},{2,3},{3,2},{4,5},{5,4},{6,7},{7,6},{24,25},{25,24},{2... | collective-permute-start | bytes 417800 | tf_op jit(solution)/shard_map/ppermute | solution.py:28
  38.9 3.7 %collective-permute-start.8 = (bf16[272,256]{1,0:T(8,128)(2,1)S(1)}, bf16[272,256]{1,0:T(8,128)(2,1)S(1)}, u32[]{:S(2)}, u32[]{:S(2)}) collective-permute-start(bf16[272,256]{1,0:T(8,128)(2,1)S(1)} %collective-permute-done.6.refs_5_), channel_id=1, source_target_pairs={{0,1},{1,0},{2,3},{3,2},{8,9},{9,8},{10,11},{11,10},{20,21},{21,20... | collective-permute-start | bytes 417800 | tf_op jit(solution)/shard_map/ppermute | solution.py:28
  43.3 2.9 %collective-permute-start.10 = (bf16[528,256]{1,0:T(8,128)(2,1)S(1)}, bf16[528,256]{1,0:T(8,128)(2,1)S(1)}, u32[]{:S(2)}, u32[]{:S(2)}) collective-permute-start(bf16[528,256]{1,0:T(8,128)(2,1)S(1)} %get-tuple-element.37.refs_3_), channel_id=1, source_target_pairs={{0,4},{1,5},{2,6},{3,7},{4,0},{5,1},{6,2},{7,3},{8,12},{9,13},{10,... | collective-permute-start | bytes 811016 | tf_op jit(solution)/shard_map/ppermute | solution.py:28
  44.3 1.9 %collective-permute-start.11 = (bf16[528,256]{1,0:T(8,128)(2,1)S(1)}, bf16[528,256]{1,0:T(8,128)(2,1)S(1)}, u32[]{:S(2)}, u32[]{:S(2)}) collective-permute-start(bf16[528,256]{1,0:T(8,128)(2,1)S(1)} %get-tuple-element.38.refs_4_), channel_id=1, source_target_pairs={{0,4},{1,5},{2,6},{3,7},{4,0},{5,1},{6,2},{7,3},{8,12},{9,13},{10,... | collective-permute-start | bytes 811016 | tf_op jit(solution)/shard_map/ppermute | solution.py:28
  44.4 3.5 %copy-start.2 = (f32[512]{0:T(512)S(1)}, f32[512]{0:T(512)}, u32[]{:S(2)}) copy-start(f32[512]{0:T(512)} %param.10) | copy-start | bytes 6148
  44.4 1.8 %collective-permute-start.9 = (bf16[528,256]{1,0:T(8,128)(2,1)S(1)}, bf16[528,256]{1,0:T(8,128)(2,1)S(1)}, u32[]{:S(2)}, u32[]{:S(2)}) collective-permute-start(bf16[528,256]{1,0:T(8,128)(2,1)S(1)} %get-tuple-element.36.refs_2_), channel_id=1, source_target_pairs={{0,4},{1,5},{2,6},{3,7},{4,0},{5,1},{6,2},{7,3},{8,12},{9,13},{10,... | collective-permute-start | bytes 811016 | tf_op jit(solution)/shard_map/ppermute | solution.py:28
  47.9 4.1 %collective-permute-start.12 = (f32[1536]{0:T(1024)S(1)}, f32[1536]{0:T(1024)S(1)}, u32[]{:S(2)}, u32[]{:S(2)}) collective-permute-start(f32[1536]{0:T(1024)S(1)} %pad_maximum_fusion), channel_id=1, source_target_pairs={{0,6},{1,7},{2,4},{3,5},{4,2},{5,3},{6,0},{7,1},{8,14},{9,15},{10,... | collective-permute-start | bytes 18440 | tf_op jit(solution)/shard_map/ppermute | solution.py:28
  52.0 25.7 %copy-start = (bf16[1024,256]{1,0:T(8,128)(2,1)S(1)}, bf16[1024,256]{1,0:T(8,128)(2,1)}, u32[]{:S(2)}) copy-start(bf16[1024,256]{1,0:T(8,128)(2,1)} %points.1) | copy-start | bytes 1572868
  54.1 3.3 %collective-permute-start.15 = (f32[8,4,128]{2,1,0:T(4,128)S(1)}, f32[8,4,128]{2,1,0:T(4,128)S(1)}, u32[]{:S(2)}, u32[]{:S(2)}) collective-permute-start(f32[8,4,128]{2,1,0:T(4,128)S(1)} %columns.2), channel_id=1, source_target_pairs={{0,5},{1,4},{2,7},{3,6},{4,1},{5,0},{6,3},{7,2},{8,13},{9,12},{10,... | collective-permute-start | bytes 49160 | tf_op jit(solution)/shard_map/ppermute | solution.py:28
  54.2 3.2 %collective-permute-start.14 = (f32[8,4,128]{2,1,0:T(4,128)S(1)}, f32[8,4,128]{2,1,0:T(4,128)S(1)}, u32[]{:S(2)}, u32[]{:S(2)}) collective-permute-start(f32[8,4,128]{2,1,0:T(4,128)S(1)} %columns.2), channel_id=1, source_target_pairs={{0,1},{1,0},{2,3},{3,2},{4,5},{5,4},{6,7},{7,6},{8,9},{9,8},{10,11... | collective-permute-start | bytes 49160 | tf_op jit(solution)/shard_map/ppermute | solution.py:28
  55.9 1.5 %collective-permute-start.13 = (f32[8,4,128]{2,1,0:T(4,128)S(1)}, f32[8,4,128]{2,1,0:T(4,128)S(1)}, u32[]{:S(2)}, u32[]{:S(2)}) collective-permute-start(f32[8,4,128]{2,1,0:T(4,128)S(1)} %columns.2), channel_id=1, source_target_pairs={{0,4},{1,5},{2,6},{3,7},{4,0},{5,1},{6,2},{7,3},{8,12},{9,13},{10,... | collective-permute-start | bytes 49160 | tf_op jit(solution)/shard_map/ppermute | solution.py:28
  57.5 11.2 %collective-permute-start.16 = (f32[6,4,128]{2,1,0:T(4,128)S(1)}, f32[6,4,128]{2,1,0:T(4,128)S(1)}, u32[]{:S(2)}, u32[]{:S(2)}) collective-permute-start(f32[6,4,128]{2,1,0:T(4,128)S(1)} %slice_select_fusion), channel_id=1, source_target_pairs={{0,8},{1,9},{2,10},{3,11},{4,255},{5,254},{6,253},{7,252},{8,16},{... | collective-permute-start | bytes 36872 | tf_op jit(solution)/shard_map/ppermute | solution.py:28
  64.4 4.2 %collective-permute-start.17 = (f32[4,4,128]{2,1,0:T(4,128)S(1)}, f32[4,4,128]{2,1,0:T(4,128)S(1)}, u32[]{:S(2)}, u32[]{:S(2)}) collective-permute-start(f32[4,4,128]{2,1,0:T(4,128)S(1)} %slice_select_fusion.1), channel_id=1, source_target_pairs={{0,16},{1,17},{2,18},{3,19},{4,247},{5,246},{6,245},{7,244},{8,24}... | collective-permute-start | bytes 24584 | tf_op jit(solution)/shard_map/ppermute | solution.py:28
  64.9 3.7 %collective-permute-start.18 = (f32[2,4,128]{2,1,0:T(4,128)S(1)}, f32[2,4,128]{2,1,0:T(4,128)S(1)}, u32[]{:S(2)}, u32[]{:S(2)}) collective-permute-start(f32[2,4,128]{2,1,0:T(4,128)S(1)} %slice_select_fusion.4), channel_id=1, source_target_pairs={{0,24},{1,25},{2,26},{3,27},{4,239},{5,238},{6,237},{7,236},{8,35}... | collective-permute-start | bytes 12296 | tf_op jit(solution)/shard_map/ppermute | solution.py:28
  68.7 4.4 %collective-permute-start.19 = (f32[8,4,128]{2,1,0:T(4,128)S(1)}, f32[8,4,128]{2,1,0:T(4,128)S(1)}, u32[]{:S(2)}, u32[]{:S(2)}) collective-permute-start(f32[8,4,128]{2,1,0:T(4,128)S(1)} %log_add_fusion.2), channel_id=1, source_target_pairs={{0,4},{1,5},{2,6},{3,7},{4,0},{5,1},{6,2},{7,3},{8,12},{9,13},{10,... | collective-permute-start | bytes 49160 | tf_op jit(solution)/shard_map/ppermute | solution.py:28
  73.1 11.3 %copy-start.1 = (bf16[512,256]{1,0:T(8,128)(2,1)S(1)}, bf16[512,256]{1,0:T(8,128)(2,1)}, u32[]{:S(2)}) copy-start(bf16[512,256]{1,0:T(8,128)(2,1)} %src.1) | copy-start | bytes 786436
  75.5 4.0 %collective-permute-start.20 = (f32[1024]{0:T(1024)S(1)}, f32[1024]{0:T(1024)S(1)}, u32[]{:S(2)}, u32[]{:S(2)}) collective-permute-start(f32[1024]{0:T(1024)S(1)} %bitcast.58), channel_id=1, source_target_pairs={{0,6},{1,7},{2,4},{3,5},{4,2},{5,3},{6,0},{7,1},{8,14},{9,15},{10,... | collective-permute-start | bytes 12296 | tf_op jit(solution)/shard_map/ppermute | solution.py:28
  81.8 3.4 %collective-permute-start.23 = (f32[8,4,128]{2,1,0:T(4,128)S(1)}, f32[8,4,128]{2,1,0:T(4,128)S(1)}, u32[]{:S(2)}, u32[]{:S(2)}) collective-permute-start(f32[8,4,128]{2,1,0:T(4,128)S(1)} %columns.3), channel_id=1, source_target_pairs={{0,5},{1,4},{2,7},{3,6},{4,1},{5,0},{6,3},{7,2},{8,13},{9,12},{10,... | collective-permute-start | bytes 49160 | tf_op jit(solution)/shard_map/ppermute | solution.py:28
  83.9 2.6 %collective-permute-start.22 = (f32[8,4,128]{2,1,0:T(4,128)S(1)}, f32[8,4,128]{2,1,0:T(4,128)S(1)}, u32[]{:S(2)}, u32[]{:S(2)}) collective-permute-start(f32[8,4,128]{2,1,0:T(4,128)S(1)} %columns.3), channel_id=1, source_target_pairs={{0,1},{1,0},{2,3},{3,2},{4,5},{5,4},{6,7},{7,6},{8,9},{9,8},{10,11... | collective-permute-start | bytes 49160 | tf_op jit(solution)/shard_map/ppermute | solution.py:28
  83.9 2.6 %collective-permute-start.21 = (f32[8,4,128]{2,1,0:T(4,128)S(1)}, f32[8,4,128]{2,1,0:T(4,128)S(1)}, u32[]{:S(2)}, u32[]{:S(2)}) collective-permute-start(f32[8,4,128]{2,1,0:T(4,128)S(1)} %columns.3), channel_id=1, source_target_pairs={{0,4},{1,5},{2,6},{3,7},{4,0},{5,1},{6,2},{7,3},{8,12},{9,13},{10,... | collective-permute-start | bytes 49160 | tf_op jit(solution)/shard_map/ppermute | solution.py:28
  86.5 5.3 %collective-permute-start.25 = (f32[4,128]{1,0:T(4,128)S(1)}, f32[4,128]{1,0:T(4,128)S(1)}, u32[]{:S(2)}, u32[]{:S(2)}) collective-permute-start(f32[4,128]{1,0:T(4,128)S(1)} %fusion.10), channel_id=1, source_target_pairs={{0,16},{1,17},{2,18},{3,19},{4,247},{5,246},{6,245},{7,244},{8,24}... | collective-permute-start | bytes 6152 | tf_op jit(solution)/shard_map/ppermute | solution.py:28
  89.1 3.5 %collective-permute-start.24 = (f32[2,4,128]{2,1,0:T(4,128)S(1)}, f32[2,4,128]{2,1,0:T(4,128)S(1)}, u32[]{:S(2)}, u32[]{:S(2)}) collective-permute-start(f32[2,4,128]{2,1,0:T(4,128)S(1)} %slice_select_fusion.2), channel_id=1, source_target_pairs={{0,8},{1,9},{2,10},{3,11},{4,255},{5,254},{6,253},{7,252},{8,16},{... | collective-permute-start | bytes 12296 | tf_op jit(solution)/shard_map/ppermute | solution.py:28
  92.6 10.2 %collective-permute-start.26 = (f32[2,4,128]{2,1,0:T(4,128)S(1)}, f32[2,4,128]{2,1,0:T(4,128)S(1)}, u32[]{:S(2)}, u32[]{:S(2)}) collective-permute-start(f32[2,4,128]{2,1,0:T(4,128)S(1)} %log_add_fusion.6), channel_id=1, source_target_pairs={{0,4},{1,5},{2,6},{3,7},{4,0},{5,1},{6,2},{7,3},{8,12},{9,13},{10,... | collective-permute-start | bytes 12296 | tf_op jit(solution)/shard_map/ppermute | solution.py:28
  100.5 3.9 %collective-permute-start.28 = (f32[2,4,128]{2,1,0:T(4,128)S(1)}, f32[2,4,128]{2,1,0:T(4,128)S(1)}, u32[]{:S(2)}, u32[]{:S(2)}) collective-permute-start(f32[2,4,128]{2,1,0:T(4,128)S(1)} %log_add_fusion.6), channel_id=1, source_target_pairs={{0,6},{1,7},{2,4},{3,5},{4,2},{5,3},{6,0},{7,1},{8,14},{9,15},{10,... | collective-permute-start | bytes 12296 | tf_op jit(solution)/shard_map/ppermute | solution.py:28
  102.7 3.4 %collective-permute-start.27 = (f32[2,4,128]{2,1,0:T(4,128)S(1)}, f32[2,4,128]{2,1,0:T(4,128)S(1)}, u32[]{:S(2)}, u32[]{:S(2)}) collective-permute-start(f32[2,4,128]{2,1,0:T(4,128)S(1)} %log_add_fusion.6), channel_id=1, source_target_pairs={{0,2},{1,3},{2,0},{3,1},{4,6},{5,7},{6,4},{7,5},{8,10},{9,11},{10,... | collective-permute-start | bytes 12296 | tf_op jit(solution)/shard_map/ppermute | solution.py:28
